TPU v7x, 32 devices: a whole 2x2x4 slice. The times are simulated.
32 devices in a mesh: mesh: 16 (over z, x, core), mem: 2 (over y).
Axes of the slice: x: 2, y: 2, z: 4, core: 2. Of those that a mesh axis runs over, the one named last changes fastest.
Arguments:
- perturbations: bfloat16 [3072, 8192], P('mem', 'mesh')
- node_coord: int32 [8192], P('mesh'), may hold values from 0 to 32767, as said below
- threshold_level: int32 [8192], P('mesh'), may hold values from 0 to 4
Outputs:
- band_cov: float32 [8192, 2048], P(('mesh', 'mem'))
Inputs may be any that keep to these rules, and one draw needn't show every extreme that they name: node_coord[n] lies in 4 n to 4 n + 3; node 0 has 0 and the last node 32767.
All inputs are finite; a program needn't handle non-finite values.
Results may differ from a plain program's by a relative error of at most 0.0003.
Values may be sent and summed in bfloat16 or wider, within the bound.
No kernel may reach another device: no remote copies, remote signals or barrier semaphores. Data moves between devices by JAX's collectives and lax.ppermute only.
A program may use at most 64 MiB of HBM per device.

v0:
```python
import jax
import jax.numpy as jnp
from jax import lax
from jax.sharding import PartitionSpec as P

SHIFTS = 3


def shifted(array, axis, by):
    peers = lax.axis_size(axis)
    return lax.ppermute(array, axis, [(i, (i + by) % peers) for i in range(peers)])


def gc_taper(radius):
    near = -0.25 * radius**5 + 0.5 * radius**4 + 0.625 * radius**3 - 5.0 / 3.0 * radius**2 + 1.0
    safe = jnp.maximum(radius, 1.0)
    far = (
        safe**5 / 12.0
        - 0.5 * safe**4
        + 0.625 * safe**3
        + 5.0 / 3.0 * safe**2
        - 5.0 * safe
        + 4.0
        - 2.0 / (3.0 * safe)
    )
    return jnp.where(radius <= 1.0, near, jnp.where(radius <= 2.0, far, 0.0))


def per_device(perturbations, node_coord, threshold_level):
    members_here, width = perturbations.shape
    groups = lax.axis_size("mem")
    period = 4 * width * lax.axis_size("mesh")
    blocks = [(perturbations, node_coord)]
    current = (perturbations, node_coord)
    for step in range(SHIFTS):
        current = shifted((current[0], current[1]), "mesh", -1)
        blocks.append(current)
    owned = width // groups
    first_row = lax.axis_index("mem") * owned
    pieces = []
    for pair in blocks:
        pieces.append(
            lax.psum_scatter(
                lax.dot_general(
                    perturbations,
                    pair[0],
                    (((0,), (0,)), ((), ())),
                    preferred_element_type=jnp.float32,
                ),
                "mem",
                scatter_dimension=0,
                tiled=True,
            )
        )
    raw = jnp.concatenate(pieces, axis=1)
    cov = raw / jnp.float32(members_here * groups - 1)
    row_coord = lax.dynamic_slice_in_dim(node_coord, first_row, owned, 0)
    row_level = lax.dynamic_slice_in_dim(threshold_level, first_row, owned, 0)
    col_coord = jnp.concatenate([pair[1] for pair in blocks], axis=0)
    gap = jnp.mod(col_coord[None, :] - row_coord[:, None], period)
    dist = jnp.minimum(gap, period - gap).astype(jnp.float32)
    taper = gc_taper(dist / jnp.float32(12 * width))
    level = (0.05 * row_level.astype(jnp.float32))[:, None]
    tapered = taper * cov
    return tapered - jnp.clip(tapered, -level, level)


def solution(mesh):
    in_specs = (P("mem", "mesh"), P("mesh"), P("mesh"))
    out_specs = P(("mesh", "mem"), None)
    return jax.shard_map(
        per_device, mesh=mesh, in_specs=in_specs, out_specs=out_specs, check_vma=False
    )
```

profile of v0, /device:TPU:26, one launch (start us, length us, event | category | flops | bytes accessed | tf_op | source)
XLA Modules:
  0.0 119.6 jit_solution(12836397996914948031)
XLA Ops:
  6.5 4.1 %fusion.26 = f32[512,512]{1,0:T(8,128)} fusion(bf16[1536,512]{1,0:T(8,128)(2,1)} %param.3), kind=kOutput, calls=%fused_computation.44 | convolution fusion | flops 805306368 | bytes 2621440 | tf_op jit(solution)/shard_map/dot_general | solution.py:44
  10.6 0.0 reduce-scatter.7.cloned.1.call-start
  10.7 0.1 collective-permute-start.3
  10.8 17.9 %collective-permute-done.3 = bf16[1536,512]{1,0:T(8,128)(2,1)S(1)} collective-permute-done((bf16[1536,512]{1,0:T(8,128)(2,1)S(1)}, bf16[1536,512]{1,0:T(8,128)(2,1)S(1)}, u32[]{:S(2)}, u32[]{:S(2)}) %collective-permute-start.3) | collective-permute-done | bytes 1572896 | tf_op jit(solution)/shard_map/ppermute | solution.py:11
  28.7 1.1 copy-done.1
  29.8 2.0 %fusion.27 = f32[512,512]{1,0:T(8,128)} fusion(bf16[1536,512]{1,0:T(8,128)(2,1)S(1)} %copy-done, bf16[1536,512]{1,0:T(8,128)(2,1)S(1)} %collective-permute-done.3), kind=kOutput, calls=%fused_computation.45 | convolution fusion | flops 805306368 | bytes 4194304 | tf_op jit(solution)/shard_map/dot_general | solution.py:44
  31.9 0.0 reduce-scatter.9.cloned.1.call-start
  31.9 2.4 %collective-permute-start.4 = (bf16[1536,512]{1,0:T(8,128)(2,1)}, bf16[1536,512]{1,0:T(8,128)(2,1)S(1)}, u32[]{:S(2)}, u32[]{:S(2)}) collective-permute-start(bf16[1536,512]{1,0:T(8,128)(2,1)} %copy-done.1), channel_id=1, source_target_pairs={{0,30},{2,0},{4,2},{6,4},{8,6},{10,8},{12,10},{14,12},{16,14},{18,... | collective-permute-start | bytes 4718600 | tf_op jit(solution)/shard_map/ppermute | solution.py:11
  34.3 18.3 %collective-permute-done.4 = bf16[1536,512]{1,0:T(8,128)(2,1)S(1)} collective-permute-done((bf16[1536,512]{1,0:T(8,128)(2,1)}, bf16[1536,512]{1,0:T(8,128)(2,1)S(1)}, u32[]{:S(2)}, u32[]{:S(2)}) %collective-permute-start.4) | collective-permute-done | bytes 1572896 | tf_op jit(solution)/shard_map/ppermute | solution.py:11
  52.5 2.0 %fusion.28 = f32[512,512]{1,0:T(8,128)} fusion(bf16[1536,512]{1,0:T(8,128)(2,1)S(1)} %copy-done, bf16[1536,512]{1,0:T(8,128)(2,1)S(1)} %collective-permute-done.4), kind=kOutput, calls=%fused_computation.46 | convolution fusion | flops 805306368 | bytes 4194304 | tf_op jit(solution)/shard_map/dot_general | solution.py:44
  54.6 0.0 reduce-scatter.11.cloned.1.call-start
  54.6 2.2 %collective-permute-start.5 = (bf16[1536,512]{1,0:T(8,128)(2,1)S(1)}, bf16[1536,512]{1,0:T(8,128)(2,1)S(1)}, u32[]{:S(2)}, u32[]{:S(2)}) collective-permute-start(bf16[1536,512]{1,0:T(8,128)(2,1)S(1)} %collective-permute-done.4), channel_id=1, source_target_pairs={{0,30},{2,0},{4,2},{6,4},{8,6},{10,8},{12,10},{14,12},{16,14},{18,... | collective-permute-start | bytes 4718600 | tf_op jit(solution)/shard_map/ppermute | solution.py:11
  56.9 17.9 %collective-permute-done.5 = bf16[1536,512]{1,0:T(8,128)(2,1)S(1)} collective-permute-done((bf16[1536,512]{1,0:T(8,128)(2,1)S(1)}, bf16[1536,512]{1,0:T(8,128)(2,1)S(1)}, u32[]{:S(2)}, u32[]{:S(2)}) %collective-permute-start.5) | collective-permute-done | bytes 1572896 | tf_op jit(solution)/shard_map/ppermute | solution.py:11
  74.8 2.0 %fusion.29 = f32[512,512]{1,0:T(8,128)} fusion(bf16[1536,512]{1,0:T(8,128)(2,1)S(1)} %copy-done, bf16[1536,512]{1,0:T(8,128)(2,1)S(1)} %collective-permute-done.5), kind=kOutput, calls=%fused_computation.47 | convolution fusion | flops 805306368 | bytes 4194304 | tf_op jit(solution)/shard_map/dot_general | solution.py:44
  76.8 2.4 %collective-permute-start = (s32[512]{0:T(512)S(1)}, s32[512]{0:T(512)S(1)}, u32[]{:S(2)}, u32[]{:S(2)}) collective-permute-start(s32[512]{0:T(512)S(1)} %copy-done.2), channel_id=1, source_target_pairs={{0,30},{2,0},{4,2},{6,4},{8,6},{10,8},{12,10},{14,12},{16,14},{18,... | collective-permute-start | bytes 6152 | tf_op jit(solution)/shard_map/ppermute | solution.py:11
  79.2 7.4 %collective-permute-done = s32[512]{0:T(512)S(1)} collective-permute-done((s32[512]{0:T(512)S(1)}, s32[512]{0:T(512)S(1)}, u32[]{:S(2)}, u32[]{:S(2)}) %collective-permute-start) | collective-permute-done | bytes 2080 | tf_op jit(solution)/shard_map/ppermute | solution.py:11
  86.5 5.7 %collective-permute-done.1 = s32[512]{0:T(512)S(1)} collective-permute-done((s32[512]{0:T(512)S(1)}, s32[512]{0:T(512)S(1)}, u32[]{:S(2)}, u32[]{:S(2)}) %collective-permute-start.1) | collective-permute-done | bytes 2080 | tf_op jit(solution)/shard_map/ppermute | solution.py:11
  92.2 0.1 fusion.25
  92.3 0.1 dynamic_slice.6
  92.4 5.6 %collective-permute-done.2 = s32[512]{0:T(512)S(1)} collective-permute-done((s32[512]{0:T(512)S(1)}, s32[512]{0:T(512)S(1)}, u32[]{:S(2)}, u32[]{:S(2)}) %collective-permute-start.2) | collective-permute-done | bytes 2080 | tf_op jit(solution)/shard_map/ppermute | solution.py:11
  98.0 0.0 reduce-scatter.7.cloned.1.call-done
  98.0 0.0 reduce-scatter.9.cloned.1.call-done
  98.0 8.9 %reduce-scatter.11.cloned.1.call-done = f32[256,512]{1,0:T(8,128)} async-done(((f32[512,512]{1,0:T(8,128)}), f32[256,512]{1,0:T(8,128)}) %reduce-scatter.11.cloned.1.call-update) | async-done | bytes 524304 | tf_op jit(solution)/shard_map/reduce_scatter | solution.py:43
  106.9 6.2 %minimum_subtract_fusion = f32[256,2048]{1,0:T(8,128)} fusion(f32[256,512]{1,0:T(8,128)} %reduce-scatter.11.cloned.1.call-done, f32[256,512]{1,0:T(8,128)} %reduce-scatter.9.cloned.1.call-done, f32[256,512]{1,0:T(8,128)} %reduce-scatter.7.cloned.1.call-done, f32[256,512]{1,0:T(8,128)} %reduce-scatter.5.cloned.1.call-done, f32[256]{0:T(256)S(1)} %get-tuple-element.5, ...), kind=kLoop, calls=%fused_computation.40 | loop fusion | flops 30408704 | bytes 4205568 | tf_op jit(solution)/shard_map/sub | solution.py:65
  (16 shorter events, 0.1 us)
Async XLA Ops:
  6.5 4.1 %copy-start = (bf16[1536,512]{1,0:T(8,128)(2,1)S(1)}, bf16[1536,512]{1,0:T(8,128)(2,1)}, u32[]{:S(2)}) copy-start(bf16[1536,512]{1,0:T(8,128)(2,1)} %param.3) | copy-start | bytes 4718596
  6.5 91.4 %reduce-scatter.5.cloned.1.call-start = ((), (), s32[]{:S(2)}) async-start(), calls=%async_computation.4 | async-start | bytes 1572864 | tf_op jit(solution)/shard_map/reduce_scatter | solution.py:43
  10.6 87.4 %reduce-scatter.7.cloned.1.call-start = ((), (), s32[]{:S(2)}) async-start(), calls=%async_computation.5 | async-start | bytes 1572864 | tf_op jit(solution)/shard_map/reduce_scatter | solution.py:43
  10.7 18.0 %collective-permute-start.3 = (bf16[1536,512]{1,0:T(8,128)(2,1)S(1)}, bf16[1536,512]{1,0:T(8,128)(2,1)S(1)}, u32[]{:S(2)}, u32[]{:S(2)}) collective-permute-start(bf16[1536,512]{1,0:T(8,128)(2,1)S(1)} %copy-done), channel_id=1, source_target_pairs={{0,30},{2,0},{4,2},{6,4},{8,6},{10,8},{12,10},{14,12},{16,14},{18,... | collective-permute-start | bytes 4718600 | tf_op jit(solution)/shard_map/ppermute | solution.py:11
  28.7 1.1 copy-start.1
  31.9 66.2 %reduce-scatter.9.cloned.1.call-start = ((), (), s32[]{:S(2)}) async-start(), calls=%async_computation.6 | async-start | bytes 1572864 | tf_op jit(solution)/shard_map/reduce_scatter | solution.py:43
  31.9 20.6 %collective-permute-start.4 = (bf16[1536,512]{1,0:T(8,128)(2,1)}, bf16[1536,512]{1,0:T(8,128)(2,1)S(1)}, u32[]{:S(2)}, u32[]{:S(2)}) collective-permute-start(bf16[1536,512]{1,0:T(8,128)(2,1)} %copy-done.1), channel_id=1, source_target_pairs={{0,30},{2,0},{4,2},{6,4},{8,6},{10,8},{12,10},{14,12},{16,14},{18,... | collective-permute-start | bytes 4718600 | tf_op jit(solution)/shard_map/ppermute | solution.py:11
  54.5 22.3 %copy-start.2 = (s32[512]{0:T(512)S(1)}, s32[512]{0:T(512)}, u32[]{:S(2)}) copy-start(s32[512]{0:T(512)} %param.4) | copy-start | bytes 6148
  54.5 37.7 %copy-start.3 = (s32[512]{0:T(512)S(1)}, s32[512]{0:T(512)}, u32[]{:S(2)}) copy-start(s32[512]{0:T(512)} %param.5) | copy-start | bytes 6148
  54.6 52.3 %reduce-scatter.11.cloned.1.call-start = ((), (), s32[]{:S(2)}) async-start(), calls=%async_computation.7 | async-start | bytes 1572864 | tf_op jit(solution)/shard_map/reduce_scatter | solution.py:43
  54.6 20.2 %collective-permute-start.5 = (bf16[1536,512]{1,0:T(8,128)(2,1)S(1)}, bf16[1536,512]{1,0:T(8,128)(2,1)S(1)}, u32[]{:S(2)}, u32[]{:S(2)}) collective-permute-start(bf16[1536,512]{1,0:T(8,128)(2,1)S(1)} %collective-permute-done.4), channel_id=1, source_target_pairs={{0,30},{2,0},{4,2},{6,4},{8,6},{10,8},{12,10},{14,12},{16,14},{18,... | collective-permute-start | bytes 4718600 | tf_op jit(solution)/shard_map/ppermute | solution.py:11
  76.8 9.7 %collective-permute-start = (s32[512]{0:T(512)S(1)}, s32[512]{0:T(512)S(1)}, u32[]{:S(2)}, u32[]{:S(2)}) collective-permute-start(s32[512]{0:T(512)S(1)} %copy-done.2), channel_id=1, source_target_pairs={{0,30},{2,0},{4,2},{6,4},{8,6},{10,8},{12,10},{14,12},{16,14},{18,... | collective-permute-start | bytes 6152 | tf_op jit(solution)/shard_map/ppermute | solution.py:11
  86.5 5.7 %collective-permute-start.1 = (s32[512]{0:T(512)S(1)}, s32[512]{0:T(512)S(1)}, u32[]{:S(2)}, u32[]{:S(2)}) collective-permute-start(s32[512]{0:T(512)S(1)} %collective-permute-done), channel_id=1, source_target_pairs={{0,30},{2,0},{4,2},{6,4},{8,6},{10,8},{12,10},{14,12},{16,14},{18,... | collective-permute-start | bytes 6152 | tf_op jit(solution)/shard_map/ppermute | solution.py:11
  92.2 5.7 %collective-permute-start.2 = (s32[512]{0:T(512)S(1)}, s32[512]{0:T(512)S(1)}, u32[]{:S(2)}, u32[]{:S(2)}) collective-permute-start(s32[512]{0:T(512)S(1)} %collective-permute-done.1), channel_id=1, source_target_pairs={{0,30},{2,0},{4,2},{6,4},{8,6},{10,8},{12,10},{14,12},{16,14},{18,... | collective-permute-start | bytes 6152 | tf_op jit(solution)/shard_map/ppermute | solution.py:11
Sparse Core Ops, SparseCore 0:
  10.8 21.2 reduce-scatter.4
  34.4 22.9 reduce-scatter.6
  59.6 22.5 reduce-scatter.8
  84.4 22.4 reduce-scatter.10
where the time goes:
time: 122 us; the launch traced here: 120 us
  waiting for transfers between devices  81.7 us (67%)
  between operations  13.2 us (11%)
  matrix products  10 us (8%)
  starting transfers between devices  7.16 us (6%)
  other arithmetic  6.3 us (5%)
  local copies, waits for them, and re-layouts  1.23 us (1%)
    ppermute x6, waiting for transfers between devices, shifted(): lax.ppermute(array, axis, [(i, (i + by) % peers) for i in range(peers)])  72.7 us
    dot_general x4, matrix products, per_device(): lax.dot_general(perturbations, pair[0], (((0,), (0,)), ((), ())), preferr...  10 us
    reduce_scatter x4, waiting for transfers between devices, per_device(): lax.psum_scatter(lax.dot_general(perturbations, pair[0], (((0,), (0,)), (...  8.9 us
    ppermute x6, starting transfers between devices, shifted(): lax.ppermute(array, axis, [(i, (i + by) % peers) for i in range(peers)])  7.04 us
    sub x1, other arithmetic, per_device(): return tapered - jnp.clip(tapered, -level, level)  6.22 us
  transfers between devices with their start and end apart: 10, of which 7 were waited for; matrix products, arithmetic and copies ran while one was open for 5% of the time, Pallas kernels for 0%

commit v1 on v0

v1 whole, which is shorter than its diff:
```python
import functools

import jax
import jax.numpy as jnp
from jax import lax
from jax.experimental import pallas as pl
from jax.experimental.pallas import tpu as pltpu
from jax.sharding import PartitionSpec as P

PAD = 16
CHUNK = 128
PARAMS = pltpu.CompilerParams(vmem_limit_bytes=32 * 1024 * 1024)


def gc_taper(r):
    near = 1.0 + r * r * (-5.0 / 3.0 + r * (0.625 + r * (0.5 - 0.25 * r)))
    s = jnp.maximum(r, 1.0)
    far = 4.0 - 5.0 * s + s * s * (5.0 / 3.0 + s * (0.625 + s * (s * (1.0 / 12.0) - 0.5))) - (2.0 / 3.0) / s
    return jnp.where(r <= 1.0, near, jnp.where(r <= 2.0, far, 0.0))


def own_kernel(place, x, lt, *outs, owned, split):
    members, width = x.shape
    groups = width // owned
    for part in range(groups):
        if split:
            start = pl.multiple_of(lax.rem(place[0] + 1 + part, groups) * owned, owned)
        else:
            start = part * owned
        rows = x[:, pl.ds(start, owned)].T
        lt[part * owned : (part + 1) * owned, :] = rows
        tile = jnp.dot(rows, x[...], preferred_element_type=jnp.float32)
        if split:
            outs[part][...] = tile
        else:
            outs[0][part * owned : (part + 1) * owned, :] = tile


def own_tile(place, x, owned, split):
    members, width = x.shape
    rows = [owned] * (width // owned) if split else [width]
    return pl.pallas_call(
        functools.partial(own_kernel, owned=owned, split=split),
        out_shape=[jax.ShapeDtypeStruct((width, members), x.dtype)]
        + [jax.ShapeDtypeStruct((r, width), jnp.float32) for r in rows],
        in_specs=[pl.BlockSpec(memory_space=pltpu.SMEM), pl.BlockSpec(memory_space=pltpu.VMEM)],
        out_specs=[pl.BlockSpec(memory_space=pltpu.VMEM)] * (1 + len(rows)),
        compiler_params=PARAMS,
        cost_estimate=pl.CostEstimate(flops=2 * members * width * width, bytes_accessed=5 << 20, transcendentals=0),
        name="own_tile",
    )(place, x)


def panel_kernel(place, lt, *refs, picks, count, rows):
    panels, cols, outs = refs[:count], refs[count], refs[count + 1 :]
    members = lt.shape[1]

    def run(which):
        at = 0
        for slot, index in enumerate(which):
            panel = panels[index]
            wide = panel.shape[1]
            first = 0
            for out, r in zip(outs, rows):
                out[:, at : at + wide] = jnp.dot(
                    lt[first : first + r, :], panel[:members, :], preferred_element_type=jnp.float32
                )
                first += r
            node = place[2 + slot] + lax.broadcasted_iota(jnp.int32, (8, wide), 1)
            jitter = panel[members : members + PAD, :].astype(jnp.float32)[:8]
            cols[:, at : at + wide] = (4 * node).astype(jnp.float32) + jitter
            at += wide

    if len(picks) == 1:
        run(picks[0])
    else:
        for value, which in enumerate(picks):
            pl.when(place[1] == value)(functools.partial(run, which))


def panel_tile(place, lt, panels, picks, rows):
    wide = sum(panels[i].shape[1] for i in picks[0])
    width, members = lt.shape
    return pl.pallas_call(
        functools.partial(panel_kernel, picks=picks, count=len(panels), rows=rows),
        out_shape=[jax.ShapeDtypeStruct((8, wide), jnp.float32)]
        + [jax.ShapeDtypeStruct((r, wide), jnp.float32) for r in rows],
        in_specs=[pl.BlockSpec(memory_space=pltpu.SMEM)]
        + [pl.BlockSpec(memory_space=pltpu.VMEM)] * (1 + len(panels)),
        out_specs=[pl.BlockSpec(memory_space=pltpu.VMEM)] * (1 + len(rows)),
        compiler_params=PARAMS,
        cost_estimate=pl.CostEstimate(flops=2 * members * width * wide, bytes_accessed=3 << 20, transcendentals=0),
        name="panel_tile",
    )(place, lt, *panels)


def finish_kernel(block, row_coord, row_level, cols, *refs, period, half, members):
    parts, out = refs[:-1], refs[-1]
    raw = parts[0][...]
    for extra in parts[1:-1]:
        raw = raw + extra[...]
    cov = raw * jnp.float32(1.0 / (members - 1))
    wide = out.shape[1]
    level = row_level[...]
    coord = row_coord[...]
    if wide != level.shape[1]:
        level = jnp.concatenate([level] * (wide // level.shape[1]), axis=1)
        coord = jnp.concatenate([coord] * (wide // coord.shape[1]), axis=1)
    gap = jnp.abs(cols[0:1, :] - coord)
    dist = jnp.minimum(gap, period - gap)
    c = gc_taper(dist * jnp.float32(1.0 / half)) * cov
    out[...] = c - jnp.clip(c, -level, level)


def finish(block, row_coord, row_level, cols, parts, out, shape, count, period, half, members):
    owned, wide = parts[0].shape
    piece = wide // count
    first = out is None
    specs = (
        [pl.BlockSpec((owned, CHUNK), lambda i, b: (0, 0))] * 2
        + [pl.BlockSpec((8, piece), lambda i, b: (0, i))]
        + [pl.BlockSpec((owned, piece), lambda i, b: (0, i))] * len(parts)
    )
    operands = [block, row_coord, row_level, cols, *parts]
    if first:
        kernel = lambda b, rc, rl, co, *refs: finish_kernel(
            b, rc, rl, co, *refs[:-1], None, refs[-1], period=period, half=half, members=members
        )
        aliases = {}
    else:
        specs.append(pl.BlockSpec(memory_space=pl.ANY))
        operands.append(out)
        kernel = functools.partial(finish_kernel, period=period, half=half, members=members)
        aliases = {len(operands) - 1: 0}
    return pl.pallas_call(
        kernel,
        out_shape=jax.ShapeDtypeStruct(shape, jnp.float32),
        grid_spec=pltpu.PrefetchScalarGridSpec(
            num_scalar_prefetch=1,
            grid=(count,),
            in_specs=specs,
            out_specs=pl.BlockSpec((owned, piece), lambda i, b: (0, b[i])),
        ),
        input_output_aliases=aliases,
        compiler_params=PARAMS,
        cost_estimate=pl.CostEstimate(flops=20 * owned * wide, bytes_accessed=16 * owned * wide, transcendentals=0),
        name="finish",
    )(*operands)


def per_device(perturbations, node_coord, threshold_level):
    members, width = perturbations.shape
    groups = lax.axis_size("mem")
    count = lax.axis_size("mesh")
    nodes = width * count
    period = 4.0 * nodes
    half = 12 * width
    owned = width // groups
    everyone = members * groups
    split = groups == 2
    rows = [owned] * groups if split else [width]
    shape = (owned, 4 * width)
    mem = lax.axis_index("mem")
    me = lax.axis_index("mesh")
    odd = me % 2
    cross = (me // 2) % 2

    def permute(array, pairs):
        return lax.ppermute(array, "mesh", pairs)

    everywhere = range(count)
    swap_x = [(p, p ^ 2) for p in everywhere]
    relay = [(p, (p - 4) % count) if p % 4 >= 2 else (p, p ^ 1) for p in everywhere]
    far_siblings = [(p, p ^ 1) for p in everywhere if p % 4 >= 2]
    back_two = [(p, (p - 2) % count) for p in everywhere]
    siblings = [(p, p ^ 1) for p in everywhere]
    extra_pairs = [(p, p - 1) if p % 2 else (p, (p - 3) % count) for p in everywhere]

    def reduced(parts):
        if split:
            return [parts[1], lax.ppermute(parts[0], "mem", [(0, 1), (1, 0)])]
        return [lax.psum_scatter(parts[0], "mem", scatter_dimension=0, tiled=True)]

    jitter = (node_coord - 4 * (me * width + jnp.arange(width, dtype=jnp.int32))).astype(perturbations.dtype)
    panel = jnp.concatenate([perturbations, jnp.broadcast_to(jitter[None, :], (PAD, width))], axis=0)
    chunks = [panel[:, i * CHUNK : (i + 1) * CHUNK] for i in range(width // CHUNK)]
    relayed = len(chunks) // 2

    first_row = mem * owned
    row_coord = lax.dynamic_slice_in_dim(node_coord, first_row, owned, 0).astype(jnp.float32)
    row_level = 0.05 * lax.dynamic_slice_in_dim(threshold_level, first_row, owned, 0).astype(jnp.float32)
    row_coord = jnp.broadcast_to(row_coord[:, None], (owned, CHUNK))
    row_level = jnp.broadcast_to(row_level[:, None], (owned, CHUNK))
    own_cols = jnp.broadcast_to(node_coord.astype(jnp.float32)[None, :], (8, width))

    def done(out, blocks, cols, parts, pieces):
        block = jnp.stack([jnp.asarray(b, jnp.int32) for b in blocks])
        return finish(block, row_coord, row_level, cols, parts, out, shape, pieces, period, half, everyone)

    def place(*starts):
        return jnp.stack([mem, cross] + [jnp.asarray(s, jnp.int32) for s in starts]).astype(jnp.int32)

    arrived = [permute(c, swap_x) for c in chunks[:relayed]]
    extra = permute(panel, extra_pairs)
    arrived += [permute(c, back_two) for c in chunks[relayed:]]

    lt, *own = own_tile(place(), perturbations, owned, split)
    own = reduced(own)

    passed = [permute(a, relay) for a in arrived[:relayed]]
    passed_on = [permute(a, far_siblings) for a in passed]
    others = [permute(a, siblings) for a in arrived[relayed:]]

    def first_node(step):
        return ((me + step) % count) * width

    extra_step = 1 + 2 * odd
    other_step = 3 - 2 * odd
    extra_cols, *extra_parts = panel_tile(place(first_node(extra_step)), lt, [extra], [[0]], rows)
    extra_parts = reduced(extra_parts)

    per_panel = width // CHUNK
    pieces = []
    for i in range(per_panel):
        at = place(first_node(2) + i * CHUNK, first_node(other_step) + i * CHUNK)
        if i < relayed:
            panels, picks = [arrived[i], passed[i], passed_on[i]], [[0, 1], [1, 2]]
        else:
            panels, picks = [arrived[i], others[i - relayed]], [[0, 1]]
        cols, *parts = panel_tile(at, lt, panels, picks, rows)
        pieces.append((cols, reduced(parts)))

    out = done(None, [0], own_cols, own, 1)
    out = done(out, [extra_step], extra_cols, extra_parts, 1)
    for i, (cols, parts) in enumerate(pieces):
        out = done(out, [2 * per_panel + i, other_step * per_panel + i], cols, parts, 2)
    return out


def solution(mesh):
    in_specs = (P("mem", "mesh"), P("mesh"), P("mesh"))
    out_specs = P(("mesh", "mem"), None)
    return jax.shard_map(
        per_device, mesh=mesh, in_specs=in_specs, out_specs=out_specs, check_vma=False
    )
```

time: 122 us -> 107 us (0.88)
  the two profiles are of different devices: /device:TPU:26 before, /device:TPU:18 now
where the time goes in v1:
time: 107 us
  waiting for transfers between devices  42.2 us (39%)
  Pallas kernels  29.3 us (27%)
  starting transfers between devices  16.5 us (15%)
  other arithmetic  10.2 us (10%)
  local copies, waits for them, and re-layouts  8.29 us (8%)
    ppermute x11, waiting for transfers between devices, permute(): return lax.ppermute(array, 'mesh', pairs)  37.1 us
    pallas_call x5, Pallas kernels, panel_tile(): pl.pallas_call(functools.partial(panel_kernel, picks=picks, count=len(pan...  13.9 us
    pallas_call x6, Pallas kernels, finish(): pl.pallas_call(kernel, out_shape=jax.ShapeDtypeStruct(shape, jnp.float32)...  13.2 us
    ppermute x11, starting transfers between devices, permute(): return lax.ppermute(array, 'mesh', pairs)  9.37 us
    unnamed x54, local copies, waits for them, and re-layouts  7.42 us
    ppermute x6, starting transfers between devices, reduced(): return [parts[1], lax.ppermute(parts[0], 'mem', [(0, 1), (1, 0)])]  7.11 us
    ppermute x6, waiting for transfers between devices, reduced(): return [parts[1], lax.ppermute(parts[0], 'mem', [(0, 1), (1, 0)])]  5.11 us
    concatenate x2, other arithmetic, per_device(): jnp.concatenate([perturbations, jnp.broadcast_to(jitter[None, :], (PAD, w...  3.96 us
  transfers between devices with their start and end apart: 17, of which 5 were waited for; matrix products, arithmetic and copies ran while one was open for 7% of the time, Pallas kernels for 25%

profile of v1, /device:TPU:18, one launch (start us, length us, event | category | flops | bytes accessed | tf_op | source)
XLA Modules:
  0.0 106.6 jit_solution(9592224273593268388)
XLA Ops:
  1.4 2.8 %pad_maximum_fusion = bf16[1552,512]{1,0:T(8,128)(2,1)} fusion(bf16[16,512]{1,0:T(8,128)(2,1)S(1)} %broadcast_in_dim.10, bf16[1536,512]{1,0:T(8,128)(2,1)} %x.1), kind=kLoop, calls=%fused_computation.4 | loop fusion | flops 3178496 | bytes 3178496 | tf_op jit(solution)/shard_map/concatenate | solution.py:185
  5.9 1.5 %collective-permute-start.6 = (bf16[1552,128]{1,0:T(8,128)(2,1)S(1)}, bf16[1552,128]{1,0:T(8,128)(2,1)S(1)}, u32[]{:S(2)}, u32[]{:S(2)}) collective-permute-start(bf16[1552,128]{1,0:T(8,128)(2,1)S(1)} %get-tuple-element.46), channel_id=1, source_target_pairs={{0,4},{2,6},{4,0},{6,2},{8,12},{10,14},{12,8},{14,10},{16,20},{18,... | collective-permute-start | bytes 1191944 | tf_op jit(solution)/shard_map/ppermute | solution.py:169
  9.9 13.7 %collective-permute-done.10.refs_0_ = bf16[1552,128]{1,0:T(8,128)(2,1)} collective-permute-done((bf16[1552,128]{1,0:T(8,128)(2,1)S(1)}, bf16[1552,128]{1,0:T(8,128)(2,1)}, u32[]{:S(2)}, u32[]{:S(2)}) %collective-permute-start.10) | collective-permute-done | bytes 397344 | tf_op jit(solution)/shard_map/ppermute | solution.py:169
  24.1 18.3 %collective-permute-done.6.refs_0_ = bf16[1552,128]{1,0:T(8,128)(2,1)S(1)} collective-permute-done((bf16[1552,128]{1,0:T(8,128)(2,1)S(1)}, bf16[1552,128]{1,0:T(8,128)(2,1)S(1)}, u32[]{:S(2)}, u32[]{:S(2)}) %collective-permute-start.6) | collective-permute-done | bytes 397344 | tf_op jit(solution)/shard_map/ppermute | solution.py:169
  42.9 2.2 %own_tile.1 = (bf16[512,1536]{1,0:T(8,128)(2,1)S(1)}, f32[256,512]{1,0:T(8,128)}, f32[256,512]{1,0:T(8,128)S(1)}) custom-call(s32[2]{0:T(128)S(1)} %pad_add_fusion.3.place, bf16[1536,512]{1,0:T(8,128)(2,1)S(1)} %copy-done), custom_call_target="tpu_custom_call" | custom-call | flops 805306368 | bytes 5242880 | tf_op jit(solution)/shard_map/own_tile/pallas_call | solution.py:42
  46.6 1.5 %collective-permute-start.16 = (f32[256,512]{1,0:T(8,128)}, f32[256,512]{1,0:T(8,128)S(1)}, u32[]{:S(2)}, u32[]{:S(2)}) collective-permute-start(f32[256,512]{1,0:T(8,128)} %get-tuple-element.40), channel_id=1, source_target_pairs={{0,1},{1,0},{2,3},{3,2},{4,5},{5,4},{6,7},{7,6},{8,9},{9,8},{10,11... | collective-permute-start | bytes 1572872 | tf_op jit(solution)/shard_map/ppermute | solution.py:181
  48.4 4.9 %collective-permute-done.7.refs_1_ = bf16[1552,128]{1,0:T(8,128)(2,1)S(1)} collective-permute-done((bf16[1552,128]{1,0:T(8,128)(2,1)S(1)}, bf16[1552,128]{1,0:T(8,128)(2,1)S(1)}, u32[]{:S(2)}, u32[]{:S(2)}) %collective-permute-start.7) | collective-permute-done | bytes 397344 | tf_op jit(solution)/shard_map/ppermute | solution.py:169
  54.1 1.9 %collective-permute-start.12 = (bf16[1552,128]{1,0:T(8,128)(2,1)}, bf16[1552,128]{1,0:T(8,128)(2,1)}, u32[]{:S(2)}, u32[]{:S(2)}) collective-permute-start(bf16[1552,128]{1,0:T(8,128)(2,1)} %collective-permute-done.11.refs_1_), channel_id=1, source_target_pairs={{4,6},{6,4},{12,14},{14,12},{20,22},{22,20},{28,30},{30,28},{5,7},... | collective-permute-start | bytes 1191944 | tf_op jit(solution)/shard_map/ppermute | solution.py:169
  56.7 2.4 %collective-permute-start.8 = (bf16[1552,128]{1,0:T(8,128)(2,1)}, bf16[1552,128]{1,0:T(8,128)(2,1)}, u32[]{:S(2)}, u32[]{:S(2)}) collective-permute-start(bf16[1552,128]{1,0:T(8,128)(2,1)} %copy-done.3), channel_id=1, source_target_pairs={{4,6},{6,4},{12,14},{14,12},{20,22},{22,20},{28,30},{30,28},{5,7},... | collective-permute-start | bytes 1191944 | tf_op jit(solution)/shard_map/ppermute | solution.py:169
  59.7 3.0 %panel_tile.9 = (f32[8,512]{1,0:T(8,128)S(1)}, f32[256,512]{1,0:T(8,128)}, f32[256,512]{1,0:T(8,128)S(1)}) custom-call(s32[3]{0:T(128)S(1)} %pad_add_fusion.10.place, bf16[512,1536]{1,0:T(8,128)(2,1)S(1)} %get-tuple-element.23.lt, bf16[1552,512]{1,0:T(8,128)(2,1)} %collective-permute-done.14.refs_0_), custom_call_target="tpu_custom_call" | custom-call | flops 805306368 | bytes 3145728 | tf_op jit(solution)/shard_map/panel_tile/pallas_call | solution.py:84
  63.3 1.5 %collective-permute-start.15 = (f32[256,512]{1,0:T(8,128)}, f32[256,512]{1,0:T(8,128)}, u32[]{:S(2)}, u32[]{:S(2)}) collective-permute-start(f32[256,512]{1,0:T(8,128)} %get-tuple-element.38), channel_id=1, source_target_pairs={{0,1},{1,0},{2,3},{3,2},{4,5},{5,4},{6,7},{7,6},{8,9},{9,8},{10,11... | collective-permute-start | bytes 1572872 | tf_op jit(solution)/shard_map/ppermute | solution.py:181
  66.0 2.6 %panel_tile.6 = (f32[8,256]{1,0:T(8,128)S(1)}, f32[256,256]{1,0:T(8,128)}, f32[256,256]{1,0:T(8,128)S(1)}) custom-call(s32[4]{0:T(128)S(1)} %copy-done.23, bf16[512,1536]{1,0:T(8,128)(2,1)S(1)} %get-tuple-element.23.lt, bf16[1552,128]{1,0:T(8,128)(2,1)} %collective-permute-done.3.refs_0_, bf16[1552,128]{1,0:T(8,128)(2,1)} %collective-permute-done.4.refs_1_), custom_call_target="tpu_custom_call" | custom-call | flops 402653184 | bytes 3145728 | tf_op jit(solution)/shard_map/panel_tile/pallas_call | solution.py:84
  69.9 2.6 %panel_tile.5 = (f32[8,256]{1,0:T(8,128)S(1)}, f32[256,256]{1,0:T(8,128)}, f32[256,256]{1,0:T(8,128)S(1)}) custom-call(s32[4]{0:T(128)S(1)} %copy-done.22, bf16[512,1536]{1,0:T(8,128)(2,1)S(1)} %get-tuple-element.23.lt, bf16[1552,128]{1,0:T(8,128)(2,1)} %collective-permute-done.refs_0_, bf16[1552,128]{1,0:T(8,128)(2,1)} %collective-permute-done.1.refs_1_), custom_call_target="tpu_custom_call" | custom-call | flops 402653184 | bytes 3145728 | tf_op jit(solution)/shard_map/panel_tile/pallas_call | solution.py:84
  73.8 1.5 %collective-permute-start.2 = (f32[256,256]{1,0:T(8,128)}, f32[256,256]{1,0:T(8,128)}, u32[]{:S(2)}, u32[]{:S(2)}) collective-permute-start(f32[256,256]{1,0:T(8,128)} %get-tuple-element.26), channel_id=1, source_target_pairs={{0,1},{1,0},{2,3},{3,2},{4,5},{5,4},{6,7},{7,6},{8,9},{9,8},{10,11... | collective-permute-start | bytes 786440 | tf_op jit(solution)/shard_map/ppermute | solution.py:181
  75.3 3.0 %panel_tile.8 = (f32[8,256]{1,0:T(8,128)S(1)}, f32[256,256]{1,0:T(8,128)}, f32[256,256]{1,0:T(8,128)S(1)}) custom-call(s32[4]{0:T(128)S(1)} %copy-done.21, bf16[512,1536]{1,0:T(8,128)(2,1)S(1)} %get-tuple-element.23.lt, bf16[1552,128]{1,0:T(8,128)(2,1)} %collective-permute-done.10.refs_0_, bf16[1552,128]{1,0:T(8,128)(2,1)} %collective-permute-done.11.refs_1_, ...), custom_call_target="tpu_custom_call" | custom-call | flops 402653184 | bytes 3145728 | tf_op jit(solution)/shard_map/panel_tile/pallas_call | solution.py:84
  80.1 2.7 %panel_tile.7 = (f32[8,256]{1,0:T(8,128)S(1)}, f32[256,256]{1,0:T(8,128)}, f32[256,256]{1,0:T(8,128)S(1)}) custom-call(s32[4]{0:T(128)S(1)} %get-tuple-element.49.place, bf16[512,1536]{1,0:T(8,128)(2,1)S(1)} %get-tuple-element.23.lt, bf16[1552,128]{1,0:T(8,128)(2,1)S(1)} %collective-permute-done.6.refs_0_, bf16[1552,128]{1,0:T(8,128)(2,1)S(1)} %copy-done.4, ...), custom_call_target="tpu_custom_call" | custom-call | flops 402653184 | bytes 3145728 | tf_op jit(solution)/shard_map/panel_tile/pallas_call | solution.py:84
  84.1 1.5 %collective-permute-start.9 = (f32[256,256]{1,0:T(8,128)}, f32[256,256]{1,0:T(8,128)S(1)}, u32[]{:S(2)}, u32[]{:S(2)}) collective-permute-start(f32[256,256]{1,0:T(8,128)} %get-tuple-element.32), channel_id=1, source_target_pairs={{0,1},{1,0},{2,3},{3,2},{4,5},{5,4},{6,7},{7,6},{8,9},{9,8},{10,11... | collective-permute-start | bytes 786440 | tf_op jit(solution)/shard_map/ppermute | solution.py:181
  89.6 2.6 %finish.7.refs_2_ = f32[256,2048]{1,0:T(8,128)} custom-call(s32[1]{0:T(128)} %bitcast.14.block, f32[256,128]{1,0:T(8,128)S(1)} %broadcast_in_dim.8.rc.row_coord, f32[256,128]{1,0:T(8,128)S(1)} %broadcast_in_dim.9.rl.row_level, f32[8,512]{1,0:T(8,128)S(1)} %copy-done.14, f32[256,512]{1,0:T(8,128)S(1)} %get-tuple-element.37.refs_0_, ...), custom_call_target="tpu_custom_call", output_to_operand_aliasing={{}: (6, {})} | custom-call | flops 2621440 | bytes 2097152 | tf_op jit(solution)/shard_map/finish/pallas_call | solution.py:135
  92.2 3.1 %collective-permute-done.13.refs_1_ = f32[256,256]{1,0:T(8,128)} collective-permute-done((f32[256,256]{1,0:T(8,128)}, f32[256,256]{1,0:T(8,128)}, u32[]{:S(2)}, u32[]{:S(2)}) %collective-permute-start.13) | collective-permute-done | bytes 262176 | tf_op jit(solution)/shard_map/ppermute | solution.py:181
  95.3 2.5 %finish.8.refs_2_ = f32[256,2048]{1,0:T(8,128)} custom-call(s32[2]{0:T(128)S(1)} %copy-done.24, f32[256,128]{1,0:T(8,128)S(1)} %broadcast_in_dim.8.rc.row_coord, f32[256,128]{1,0:T(8,128)S(1)} %broadcast_in_dim.9.rl.row_level, f32[8,256]{1,0:T(8,128)S(1)} %copy-done.18, f32[256,256]{1,0:T(8,128)S(1)} %copy-done.10, ...), custom_call_target="tpu_custom_call", output_to_operand_aliasing={{}: (6, {})} | custom-call | flops 1310720 | bytes 1048576 | tf_op jit(solution)/shard_map/finish/pallas_call | solution.py:135
  97.8 2.0 %collective-permute-done.9.refs_1_ = f32[256,256]{1,0:T(8,128)S(1)} collective-permute-done((f32[256,256]{1,0:T(8,128)}, f32[256,256]{1,0:T(8,128)S(1)}, u32[]{:S(2)}, u32[]{:S(2)}) %collective-permute-start.9) | collective-permute-done | bytes 262176 | tf_op jit(solution)/shard_map/ppermute | solution.py:181
  99.8 1.7 %finish.9.refs_2_ = f32[256,2048]{1,0:T(8,128)} custom-call(s32[2]{0:T(128)S(1)} %copy-done.25, f32[256,128]{1,0:T(8,128)S(1)} %broadcast_in_dim.8.rc.row_coord, f32[256,128]{1,0:T(8,128)S(1)} %broadcast_in_dim.9.rl.row_level, f32[8,256]{1,0:T(8,128)S(1)} %copy-done.20, f32[256,256]{1,0:T(8,128)S(1)} %copy-done.12, ...), custom_call_target="tpu_custom_call", output_to_operand_aliasing={{}: (6, {})} | custom-call | flops 1310720 | bytes 1048576 | tf_op jit(solution)/shard_map/finish/pallas_call | solution.py:135
  101.5 2.5 %finish.10.refs_2_ = f32[256,2048]{1,0:T(8,128)} custom-call(s32[2]{0:T(128)S(1)} %copy-done.26, f32[256,128]{1,0:T(8,128)S(1)} %broadcast_in_dim.8.rc.row_coord, f32[256,128]{1,0:T(8,128)S(1)} %broadcast_in_dim.9.rl.row_level, f32[8,256]{1,0:T(8,128)S(1)} %get-tuple-element.27.cols, f32[256,256]{1,0:T(8,128)S(1)} %copy-done.6, ...), custom_call_target="tpu_custom_call", output_to_operand_aliasing={{}: (6, {})} | custom-call | flops 1310720 | bytes 1048576 | tf_op jit(solution)/shard_map/finish/pallas_call | solution.py:135
  104.1 2.5 %finish.11 = f32[256,2048]{1,0:T(8,128)} custom-call(s32[2]{0:T(128)S(1)} %pad_add_fusion.block, f32[256,128]{1,0:T(8,128)S(1)} %broadcast_in_dim.8.rc.row_coord, f32[256,128]{1,0:T(8,128)S(1)} %broadcast_in_dim.9.rl.row_level, f32[8,256]{1,0:T(8,128)S(1)} %copy-done.16, f32[256,256]{1,0:T(8,128)S(1)} %copy-done.8, ...), custom_call_target="tpu_custom_call", output_to_operand_aliasing={{}: (6, {})} | custom-call | flops 1310720 | bytes 1048576 | tf_op jit(solution)/shard_map/finish/pallas_call | solution.py:135
  (93 shorter events, 21.8 us)
Async XLA Ops:
  4.1 52.5 %collective-permute-start.14 = (bf16[1552,512]{1,0:T(8,128)(2,1)}, bf16[1552,512]{1,0:T(8,128)(2,1)}, u32[]{:S(2)}, u32[]{:S(2)}) collective-permute-start(bf16[1552,512]{1,0:T(8,128)(2,1)} %pad_maximum_fusion), channel_id=1, source_target_pairs={{0,26},{2,0},{4,30},{6,4},{8,2},{10,8},{12,6},{14,12},{16,10},{18,... | collective-permute-start | bytes 4767752 | tf_op jit(solution)/shard_map/ppermute | solution.py:169
  5.3 18.4 %collective-permute-start.10 = (bf16[1552,128]{1,0:T(8,128)(2,1)S(1)}, bf16[1552,128]{1,0:T(8,128)(2,1)}, u32[]{:S(2)}, u32[]{:S(2)}) collective-permute-start(bf16[1552,128]{1,0:T(8,128)(2,1)S(1)} %get-tuple-element.43), channel_id=1, source_target_pairs={{0,4},{2,6},{4,0},{6,2},{8,12},{10,14},{12,8},{14,10},{16,20},{18,... | collective-permute-start | bytes 1191944 | tf_op jit(solution)/shard_map/ppermute | solution.py:169
  5.9 36.6 %collective-permute-start.6 = (bf16[1552,128]{1,0:T(8,128)(2,1)S(1)}, bf16[1552,128]{1,0:T(8,128)(2,1)S(1)}, u32[]{:S(2)}, u32[]{:S(2)}) collective-permute-start(bf16[1552,128]{1,0:T(8,128)(2,1)S(1)} %get-tuple-element.46), channel_id=1, source_target_pairs={{0,4},{2,6},{4,0},{6,2},{8,12},{10,14},{12,8},{14,10},{16,20},{18,... | collective-permute-start | bytes 1191944 | tf_op jit(solution)/shard_map/ppermute | solution.py:169
  7.4 39.2 %collective-permute-start.3 = (bf16[1552,128]{1,0:T(8,128)(2,1)}, bf16[1552,128]{1,0:T(8,128)(2,1)}, u32[]{:S(2)}, u32[]{:S(2)}) collective-permute-start(bf16[1552,128]{1,0:T(8,128)(2,1)} %get-tuple-element.45), channel_id=1, source_target_pairs={{0,28},{2,30},{4,0},{6,2},{8,4},{10,6},{12,8},{14,10},{16,12},{18,... | collective-permute-start | bytes 1191944 | tf_op jit(solution)/shard_map/ppermute | solution.py:169
  7.9 38.7 %collective-permute-start = (bf16[1552,128]{1,0:T(8,128)(2,1)}, bf16[1552,128]{1,0:T(8,128)(2,1)}, u32[]{:S(2)}, u32[]{:S(2)}) collective-permute-start(bf16[1552,128]{1,0:T(8,128)(2,1)} %get-tuple-element.44), channel_id=1, source_target_pairs={{0,28},{2,30},{4,0},{6,2},{8,4},{10,6},{12,8},{14,10},{16,12},{18,... | collective-permute-start | bytes 1191944 | tf_op jit(solution)/shard_map/ppermute | solution.py:169
  23.7 24.5 %collective-permute-start.11 = (bf16[1552,128]{1,0:T(8,128)(2,1)}, bf16[1552,128]{1,0:T(8,128)(2,1)}, u32[]{:S(2)}, u32[]{:S(2)}) collective-permute-start(bf16[1552,128]{1,0:T(8,128)(2,1)} %collective-permute-done.10.refs_0_), channel_id=1, source_target_pairs={{0,2},{2,0},{4,28},{6,30},{8,10},{10,8},{12,4},{14,6},{16,18},{18,... | collective-permute-start | bytes 1191944 | tf_op jit(solution)/shard_map/ppermute | solution.py:169
  42.5 10.8 %collective-permute-start.7 = (bf16[1552,128]{1,0:T(8,128)(2,1)S(1)}, bf16[1552,128]{1,0:T(8,128)(2,1)S(1)}, u32[]{:S(2)}, u32[]{:S(2)}) collective-permute-start(bf16[1552,128]{1,0:T(8,128)(2,1)S(1)} %collective-permute-done.6.refs_0_), channel_id=1, source_target_pairs={{0,2},{2,0},{4,28},{6,30},{8,10},{10,8},{12,4},{14,6},{16,18},{18,... | collective-permute-start | bytes 1191944 | tf_op jit(solution)/shard_map/ppermute | solution.py:169
  46.5 16.7 %collective-permute-start.4 = (bf16[1552,128]{1,0:T(8,128)(2,1)}, bf16[1552,128]{1,0:T(8,128)(2,1)}, u32[]{:S(2)}, u32[]{:S(2)}) collective-permute-start(bf16[1552,128]{1,0:T(8,128)(2,1)} %collective-permute-done.3.refs_0_), channel_id=1, source_target_pairs={{0,2},{2,0},{4,6},{6,4},{8,10},{10,8},{12,14},{14,12},{16,18},{18,... | collective-permute-start | bytes 1191944 | tf_op jit(solution)/shard_map/ppermute | solution.py:169
  46.6 37.5 %collective-permute-start.16 = (f32[256,512]{1,0:T(8,128)}, f32[256,512]{1,0:T(8,128)S(1)}, u32[]{:S(2)}, u32[]{:S(2)}) collective-permute-start(f32[256,512]{1,0:T(8,128)} %get-tuple-element.40), channel_id=1, source_target_pairs={{0,1},{1,0},{2,3},{3,2},{4,5},{5,4},{6,7},{7,6},{8,9},{9,8},{10,11... | collective-permute-start | bytes 1572872 | tf_op jit(solution)/shard_map/ppermute | solution.py:181
  48.2 21.2 %collective-permute-start.1 = (bf16[1552,128]{1,0:T(8,128)(2,1)}, bf16[1552,128]{1,0:T(8,128)(2,1)}, u32[]{:S(2)}, u32[]{:S(2)}) collective-permute-start(bf16[1552,128]{1,0:T(8,128)(2,1)} %collective-permute-done.refs_0_), channel_id=1, source_target_pairs={{0,2},{2,0},{4,6},{6,4},{8,10},{10,8},{12,14},{14,12},{16,18},{18,... | collective-permute-start | bytes 1191944 | tf_op jit(solution)/shard_map/ppermute | solution.py:169
  54.1 19.7 %collective-permute-start.12 = (bf16[1552,128]{1,0:T(8,128)(2,1)}, bf16[1552,128]{1,0:T(8,128)(2,1)}, u32[]{:S(2)}, u32[]{:S(2)}) collective-permute-start(bf16[1552,128]{1,0:T(8,128)(2,1)} %collective-permute-done.11.refs_1_), channel_id=1, source_target_pairs={{4,6},{6,4},{12,14},{14,12},{20,22},{22,20},{28,30},{30,28},{5,7},... | collective-permute-start | bytes 1191944 | tf_op jit(solution)/shard_map/ppermute | solution.py:169
  56.7 22.9 %collective-permute-start.8 = (bf16[1552,128]{1,0:T(8,128)(2,1)}, bf16[1552,128]{1,0:T(8,128)(2,1)}, u32[]{:S(2)}, u32[]{:S(2)}) collective-permute-start(bf16[1552,128]{1,0:T(8,128)(2,1)} %copy-done.3), channel_id=1, source_target_pairs={{4,6},{6,4},{12,14},{14,12},{20,22},{22,20},{28,30},{30,28},{5,7},... | collective-permute-start | bytes 1191944 | tf_op jit(solution)/shard_map/ppermute | solution.py:169
  63.3 6.6 %copy-start.22 = (s32[4]{0:T(128)S(1)}, s32[4]{0:T(128)}, u32[]{:S(2)}) copy-start(s32[4]{0:T(128)} %get-tuple-element.51.place) | copy-start | bytes 52
  63.3 26.3 %collective-permute-start.15 = (f32[256,512]{1,0:T(8,128)}, f32[256,512]{1,0:T(8,128)}, u32[]{:S(2)}, u32[]{:S(2)}) collective-permute-start(f32[256,512]{1,0:T(8,128)} %get-tuple-element.38), channel_id=1, source_target_pairs={{0,1},{1,0},{2,3},{3,2},{4,5},{5,4},{6,7},{7,6},{8,9},{9,8},{10,11... | collective-permute-start | bytes 1572872 | tf_op jit(solution)/shard_map/ppermute | solution.py:181
  69.3 6.0 %copy-start.21 = (s32[4]{0:T(128)S(1)}, s32[4]{0:T(128)}, u32[]{:S(2)}) copy-start(s32[4]{0:T(128)} %get-tuple-element.41.place) | copy-start | bytes 52
  69.4 32.1 %collective-permute-start.5 = (f32[256,256]{1,0:T(8,128)}, f32[256,256]{1,0:T(8,128)}, u32[]{:S(2)}, u32[]{:S(2)}) collective-permute-start(f32[256,256]{1,0:T(8,128)} %get-tuple-element.29), channel_id=1, source_target_pairs={{0,1},{1,0},{2,3},{3,2},{4,5},{5,4},{6,7},{7,6},{8,9},{9,8},{10,11... | collective-permute-start | bytes 786440 | tf_op jit(solution)/shard_map/ppermute | solution.py:181
  73.8 6.3 %copy-start.4 = (bf16[1552,128]{1,0:T(8,128)(2,1)S(1)}, bf16[1552,128]{1,0:T(8,128)(2,1)}, u32[]{:S(2)}) copy-start(bf16[1552,128]{1,0:T(8,128)(2,1)} %copy-done.3) | copy-start | bytes 1191940
  73.8 30.3 %collective-permute-start.2 = (f32[256,256]{1,0:T(8,128)}, f32[256,256]{1,0:T(8,128)}, u32[]{:S(2)}, u32[]{:S(2)}) collective-permute-start(f32[256,256]{1,0:T(8,128)} %get-tuple-element.26), channel_id=1, source_target_pairs={{0,1},{1,0},{2,3},{3,2},{4,5},{5,4},{6,7},{7,6},{8,9},{9,8},{10,11... | collective-permute-start | bytes 786440 | tf_op jit(solution)/shard_map/ppermute | solution.py:181
  79.6 8.5 %copy-start.2 = (f32[256,512]{1,0:T(8,128)S(1)}, f32[256,512]{1,0:T(8,128)}, u32[]{:S(2)}) copy-start(f32[256,512]{1,0:T(8,128)} %copy-done.1) | copy-start | bytes 1572868
  79.6 15.7 %collective-permute-start.13 = (f32[256,256]{1,0:T(8,128)}, f32[256,256]{1,0:T(8,128)}, u32[]{:S(2)}, u32[]{:S(2)}) collective-permute-start(f32[256,256]{1,0:T(8,128)} %get-tuple-element.35), channel_id=1, source_target_pairs={{0,1},{1,0},{2,3},{3,2},{4,5},{5,4},{6,7},{7,6},{8,9},{9,8},{10,11... | collective-permute-start | bytes 786440 | tf_op jit(solution)/shard_map/ppermute | solution.py:181
  84.1 15.7 %collective-permute-start.9 = (f32[256,256]{1,0:T(8,128)}, f32[256,256]{1,0:T(8,128)S(1)}, u32[]{:S(2)}, u32[]{:S(2)}) collective-permute-start(f32[256,256]{1,0:T(8,128)} %get-tuple-element.32), channel_id=1, source_target_pairs={{0,1},{1,0},{2,3},{3,2},{4,5},{5,4},{6,7},{7,6},{8,9},{9,8},{10,11... | collective-permute-start | bytes 786440 | tf_op jit(solution)/shard_map/ppermute | solution.py:181
  89.6 5.7 %copy-start.10 = (f32[256,256]{1,0:T(8,128)S(1)}, f32[256,256]{1,0:T(8,128)}, u32[]{:S(2)}) copy-start(f32[256,256]{1,0:T(8,128)} %copy-done.9) | copy-start | bytes 786436
  89.6 5.7 %copy-start.18 = (f32[8,256]{1,0:T(8,128)S(1)}, f32[8,256]{1,0:T(8,128)}, u32[]{:S(2)}) copy-start(f32[8,256]{1,0:T(8,128)} %copy-done.17) | copy-start | bytes 24580
  89.6 5.7 %copy-start.24 = (s32[2]{0:T(128)S(1)}, s32[2]{0:T(128)}, u32[]{:S(2)}) copy-start(s32[2]{0:T(128)} %pad_add_fusion.8.block) | copy-start | bytes 28
  (20 other events, 33.7 us)

commit v2 on v0

v2 whole, which is shorter than its diff:
```python
import functools

import jax
import jax.numpy as jnp
from jax import lax
from jax.experimental import pallas as pl
from jax.experimental.pallas import tpu as pltpu
from jax.sharding import PartitionSpec as P

PAD = 16
CHUNK = 128
PARAMS = pltpu.CompilerParams(vmem_limit_bytes=32 * 1024 * 1024)
VMEM = pl.BlockSpec(memory_space=pltpu.VMEM)
F32 = jnp.float32


def after(value, *tokens):
    return lax.optimization_barrier((value, *tokens))[0]


def call(kernel, outs, *operands, name, flops=0):
    size = sum(o.size * o.dtype.itemsize for o in (*outs, *operands))
    return pl.pallas_call(
        kernel,
        out_shape=outs,
        in_specs=[VMEM] * len(operands),
        out_specs=[VMEM] * len(outs),
        compiler_params=PARAMS,
        cost_estimate=pl.CostEstimate(flops=1, bytes_accessed=1, transcendentals=0),
        name=name,
    )(*operands)


def gc_taper(r):
    near = 1.0 + r * r * (-5.0 / 3.0 + r * (0.625 + r * (0.5 - 0.25 * r)))
    s = jnp.maximum(r, 1.0)
    far = 4.0 - 5.0 * s + s * s * (5.0 / 3.0 + s * (0.625 + s * (s * (1.0 / 12.0) - 0.5))) - (2.0 / 3.0) / s
    return jnp.where(r <= 1.0, near, jnp.where(r <= 2.0, far, 0.0))


def prepare_kernel(x, coord, low, high, *chunks):
    members, width = x.shape
    first = 4 * width * lax.axis_index("mesh")
    jitter = coord[...] - first - 4 * lax.broadcasted_iota(jnp.int32, (1, width), 1)
    pad = jnp.broadcast_to(jitter.astype(F32), (PAD, width)).astype(x.dtype)
    for i, chunk in enumerate(chunks):
        span = slice(i * CHUNK, (i + 1) * CHUNK)
        chunk[:members, :] = x[:, span]
        chunk[members:, :] = pad[:, span]
    half = width // 2
    for part, span in ((low, slice(0, half)), (high, slice(half, width))):
        part[:members, :] = x[:, span]
        part[members:, :] = pad[:, span]


def own_kernel(x, coord, level, lt, row_coord, row_level, *outs, owned, split):
    members, width = x.shape
    groups = width // owned
    mem = lax.axis_index("mem")
    for part in range(groups):
        if split:
            start = pl.multiple_of(lax.rem(mem + 1 + part, groups) * owned, owned)
        else:
            start = part * owned
        lt[part * owned : (part + 1) * owned, :] = x[:, pl.ds(start, owned)].T
    tile = jnp.dot(lt[...], x[...], preferred_element_type=F32)
    store_rows(tile, outs, 0)
    rows = jnp.concatenate(
        [jnp.broadcast_to(coord[...], (CHUNK, width)), jnp.broadcast_to(level[...], (CHUNK, width))], axis=0
    )
    rows = rows.astype(F32)
    for part in range(groups):

        @pl.when(mem == part)
        def _():
            span = slice(part * owned, (part + 1) * owned)
            row_coord[...] = rows[:CHUNK, span].T
            row_level[...] = 0.05 * rows[CHUNK:, span].T


def store_rows(tile, outs, at):
    first = 0
    for out in outs:
        out[:, at : at + tile.shape[1]] = tile[first : first + out.shape[0]]
        first += out.shape[0]


def own_tile(x, coord, level, owned, rows):
    members, width = x.shape
    return call(
        functools.partial(own_kernel, owned=owned, split=len(rows) > 1),
        [jax.ShapeDtypeStruct((width, members), x.dtype)]
        + [jax.ShapeDtypeStruct((owned, CHUNK), F32)] * 2
        + [jax.ShapeDtypeStruct((r, width), F32) for r in rows],
        x,
        coord,
        level,
        name="own_tile",
        flops=2 * members * width * width,
    )


def panel_kernel(lt, *refs, picks, count, rows):
    panels, cols, outs = refs[:count], refs[count], refs[count + 1 :]
    members = lt.shape[1]

    def run(which):
        chosen = [panels[i] for i in which]
        at = 0
        for panel in chosen:
            wide = panel.shape[1]
            cols[:, at : at + wide] = panel[members:, :].astype(F32)[:8]
            at += wide
        block = jnp.concatenate([panel[:members, :] for panel in chosen], axis=1)
        store_rows(jnp.dot(lt[...], block, preferred_element_type=F32), outs, 0)

    if len(picks) == 1:
        run(picks[0])
    else:
        cross = lax.rem(lax.axis_index("mesh") // 2, 2)
        for value, which in enumerate(picks):
            pl.when(cross == value)(functools.partial(run, which))


def panel_tile(lt, panels, picks, rows):
    wide = sum(panels[i].shape[1] for i in picks[0])
    width, members = lt.shape
    return call(
        functools.partial(panel_kernel, picks=picks, count=len(panels), rows=rows),
        [jax.ShapeDtypeStruct((8, wide), F32)] + [jax.ShapeDtypeStruct((r, wide), F32) for r in rows],
        lt,
        *panels,
        name="panel_tile",
        flops=2 * members * width * wide,
    )


def finish_kernel(row_coord, row_level, *refs, plan, period, width, members, first):
    operands = sum(1 + n for n, _ in plan)
    out, scratch, sems = refs[-3], refs[-2], refs[-1]
    me = lax.axis_index("mesh")
    count = lax.axis_size("mesh")
    odd = lax.rem(me, 2)
    coord, level = row_coord[...], row_level[...]
    steps = {"own": 0, "two": 2, "extra": 1 + 2 * odd, "other": 3 - 2 * odd}
    copies = []
    at, slot = 0, 0
    for n, spans in plan:
        cols, parts = refs[at], refs[at + 1 : at + 1 + n]
        at += 1 + n
        for offset, wide, kind, inside in spans:
            step = steps[kind]
            base = (4 * (lax.rem(me + step, count) * width + inside)).astype(F32)
            for piece in range(0, wide, CHUNK):
                span = slice(offset + piece, offset + piece + CHUNK)
                raw = parts[0][:, span]
                for part in parts[1:]:
                    raw = raw + part[:, span]
                place = 4 * (piece + lax.broadcasted_iota(jnp.int32, (1, CHUNK), 1))
                column = cols[0:1, span] + (base + place.astype(F32))
                gap = jnp.abs(column - coord)
                dist = jnp.minimum(gap, period - gap)
                c = gc_taper(dist * (1.0 / (12 * width))) * (raw * (1.0 / (members - 1)))
                scratch[:, slot * CHUNK : (slot + 1) * CHUNK] = c - jnp.clip(c, -level, level)
                slot += 1
            begin = (slot * CHUNK) - wide
            target = pl.multiple_of(step * width + inside, CHUNK)
            copy = pltpu.make_async_copy(
                scratch.at[:, begin : begin + wide], out.at[:, pl.ds(target, wide)], sems.at[len(copies)]
            )
            copy.start()
            copies.append(copy)
    for copy in copies:
        copy.wait()


def finish(row_coord, row_level, groups, out, shape, period, width, members):
    operands = [row_coord, row_level]
    plan, wide, copies = [], 0, 0
    for cols, parts, spans in groups:
        operands += [cols, *parts]
        plan.append((len(parts), spans))
        wide += sum(s[1] for s in spans)
        copies += len(spans)
    specs = [VMEM] * len(operands)
    aliases = {}
    if out is not None:
        aliases = {len(operands): 0}
        operands.append(out)
        specs.append(pl.BlockSpec(memory_space=pl.ANY))
    owned = shape[0]
    return pl.pallas_call(
        functools.partial(
            finish_kernel, plan=plan, period=period, width=width, members=members, first=out is None
        ),
        out_shape=jax.ShapeDtypeStruct(shape, F32),
        in_specs=specs,
        out_specs=pl.BlockSpec(memory_space=pl.ANY),
        scratch_shapes=[pltpu.VMEM((owned, wide), F32), pltpu.SemaphoreType.DMA((copies,))],
        input_output_aliases=aliases,
        compiler_params=PARAMS,
        cost_estimate=pl.CostEstimate(flops=1, bytes_accessed=1, transcendentals=0),
        name="finish",
    )(*operands)


def per_device(perturbations, node_coord, threshold_level):
    members, width = perturbations.shape
    groups = lax.axis_size("mem")
    count = lax.axis_size("mesh")
    period = 4.0 * width * count
    owned = width // groups
    everyone = members * groups
    split = groups == 2
    rows = [owned] * groups if split else [width]
    shape = (owned, 4 * width)
    coord = node_coord.reshape(1, width)
    levels = threshold_level.reshape(1, width)

    def permute(array, pairs):
        return lax.ppermute(array, "mesh", pairs)

    everywhere = range(count)
    swap_x = [(p, p ^ 2) for p in everywhere]
    relay = [(p, (p - 4) % count) if p % 4 >= 2 else (p, p ^ 1) for p in everywhere]
    far_siblings = [(p, p ^ 1) for p in everywhere if p % 4 >= 2]
    back_two = [(p, (p - 2) % count) for p in everywhere]
    siblings = [(p, p ^ 1) for p in everywhere]
    extra_pairs = [(p, p - 1) if p % 2 else (p, (p - 3) % count) for p in everywhere]

    def reduced(parts):
        if split:
            return [parts[1], lax.ppermute(parts[0], "mem", [(0, 1), (1, 0)])]
        return [lax.psum_scatter(parts[0], "mem", scatter_dimension=0, tiled=True)]

    pieces = width // CHUNK
    relayed = pieces // 2
    low, high, *chunks = call(
        prepare_kernel,
        [jax.ShapeDtypeStruct((members + PAD, width // 2), perturbations.dtype)] * 2
        + [jax.ShapeDtypeStruct((members + PAD, CHUNK), perturbations.dtype)] * pieces,
        perturbations,
        coord,
        name="prepare",
    )
    lt, row_coord, row_level, *own = own_tile(after(perturbations, low), coord, levels, owned, rows)
    own_parts = reduced(own)
    own_done = own_parts[-1]
    own_cols = jnp.concatenate([low[members : members + 8], high[members : members + 8]], axis=1).astype(F32)

    def finished(out, groups):
        return finish(row_coord, row_level, groups, out, shape, period, width, everyone)

    extra = [permute(a, extra_pairs) for a in (low, high)]
    first = [permute(chunks[0], swap_x)]
    first.append(permute(after(chunks[1], first[0], lt), swap_x))
    straight = [permute(after(chunks[2], first[1], own_done), back_two)]
    straight.append(permute(after(chunks[3], straight[0]), back_two))
    passed = [permute(after(a, first[1], own_done), relay) for a in first]

    extra_cols, *extra_parts = panel_tile(after(lt, own_done), extra, [[0, 1]], rows)
    extra_parts = reduced(extra_parts)
    token = extra_parts[-1]

    out = None
    groups = [
        (own_cols, own_parts, [(0, width, "own", 0)]),
        (extra_cols, extra_parts, [(0, width, "extra", 0)]),
    ]
    for i in range(2):
        other = permute(after(straight[i], passed[i], *([cols] if i else [])), siblings)
        far = permute(after(passed[i], *([other, token] if i else [])), far_siblings)
        panels = [first[i], passed[i], far, straight[i], other]
        cols, *parts = panel_tile(after(lt, token), panels, [[0, 1, 3, 4], [1, 2, 3, 4]], rows)
        out = finished(out, [(after(groups[0][0], cols), *groups[0][1:])] + groups[1:])
        spans = []
        for at, index in ((0, i), (2 * CHUNK, i + 2)):
            spans += [(at, CHUNK, "two", index * CHUNK), (at + CHUNK, CHUNK, "other", index * CHUNK)]
        groups = [(cols, reduced(parts), spans)]
        token = groups[0][1][-1]
    return finished(out, groups)


def solution(mesh):
    in_specs = (P("mem", "mesh"), P("mesh"), P("mesh"))
    out_specs = P(("mesh", "mem"), None)
    return jax.shard_map(
        per_device, mesh=mesh, in_specs=in_specs, out_specs=out_specs, check_vma=False
    )
```

time: 122 us -> 78.1 us (0.64); the launches traced: 120 us -> 77.1 us
  waiting for transfers between devices: 81.7 us -> 56.2 us
  between operations: 13.2 us -> 0.13 us
  matrix products: 10 us -> 0 us
  Pallas kernels: 0 us -> 9.39 us
  other arithmetic: 6.3 us -> 0.01 us
  local copies, waits for them, and re-layouts: 1.23 us -> 2.77 us
  starting transfers between devices: 7.16 us -> 8.59 us
    ppermute x6 -> x16, waiting for transfers between devices: 72.7 us -> 56.2 us  [the longest x12 36.3 us: permute(): return lax.ppermute(array, 'mesh', pairs)]
    dot_general x4 -> x0, matrix products: 10 us -> none  [per_device(): lax.dot_general(perturbations, pair[0], (((0,), (0,)), ((), ())), preferr...]
    pallas_call x0 -> x8, Pallas kernels: none -> 9.39 us  [the longest x3 4.96 us: finish(): pl.pallas_call(functools.partial(finish_kernel, plan=plan, period=period,...]
    reduce_scatter x4 -> x0, waiting for transfers between devices: 8.9 us -> none  [per_device(): lax.psum_scatter(lax.dot_general(perturbations, pair[0], (((0,), (0,)), (...]
    sub x1 -> x0, other arithmetic: 6.22 us -> none  [per_device(): return tapered - jnp.clip(tapered, -level, level)]
    unnamed x8 -> x6, local copies, waits for them, and re-layouts: 1.16 us -> 2.77 us
    ppermute x6 -> x16, starting transfers between devices: 7.04 us -> 8.59 us  [the longest x12 6.73 us: permute(): return lax.ppermute(array, 'mesh', pairs)]
  transfers between devices with their start and end apart: 10 -> 16, of which waited for: 7 -> 12; matrix products, arithmetic and copies ran while one was open for 5% -> 0% of each run, Pallas kernels for 0% -> 9%
where the time goes in v2:
time: 78.1 us; the launch traced here: 77.1 us
  waiting for transfers between devices  56.2 us (72%)
  Pallas kernels  9.39 us (12%)
  starting transfers between devices  8.59 us (11%)
  local copies, waits for them, and re-layouts  2.77 us (4%)
    ppermute x12, waiting for transfers between devices, permute(): return lax.ppermute(array, 'mesh', pairs)  36.3 us
    ppermute x4, waiting for transfers between devices, reduced(): return [parts[1], lax.ppermute(parts[0], 'mem', [(0, 1), (1, 0)])]  19.9 us
    ppermute x12, starting transfers between devices, permute(): return lax.ppermute(array, 'mesh', pairs)  6.73 us
    pallas_call x3, Pallas kernels, finish(): pl.pallas_call(functools.partial(finish_kernel, plan=plan, period=period,...  4.96 us
    pallas_call x5, Pallas kernels, call(): pl.pallas_call(kernel, out_shape=outs, in_specs=[VMEM] * len(operands), o...  4.42 us
    unnamed x6, local copies, waits for them, and re-layouts  2.77 us
    ppermute x4, starting transfers between devices, reduced(): return [parts[1], lax.ppermute(parts[0], 'mem', [(0, 1), (1, 0)])]  1.86 us
  transfers between devices with their start and end apart: 16, of which 12 were waited for; matrix products, arithmetic and copies ran while one was open for 0% of the time, Pallas kernels for 9%

profile of v2, /device:TPU:26, one launch (start us, length us, event | category | flops | bytes accessed | tf_op | source)
XLA Modules:
  0.0 77.1 jit_solution(17640409414094542475)
XLA Ops:
  0.0 1.4 %copy-done = bf16[1536,512]{1,0:T(8,128)(2,1)S(1)} copy-done((bf16[1536,512]{1,0:T(8,128)(2,1)S(1)}, bf16[1536,512]{1,0:T(8,128)(2,1)}, u32[]{:S(2)}) %copy-start) | copy-done | bytes 1572888
  1.4 0.7 copy-done.1
  3.8 1.1 %own_tile.1 = (bf16[512,1536]{1,0:T(8,128)(2,1)S(1)}, f32[256,128]{1,0:T(8,128)S(1)}, f32[256,128]{1,0:T(8,128)S(1)}, f32[256,512]{1,0:T(8,128)S(1)}, f32[256,512]{1,0:T(8,128)S(1)}) custom-call(bf16[1536,512]{1,0:T(8,128)(2,1)S(1)} %copy-done, s32[1,512]{1,0:T(1,128)S(1)} %bitcast.3, s32[1,512]{1,0:T(1,128)S(1)} %bitcast.4), custom_call_target="tpu_custom_call" | custom-call | flops 1 | bytes 1 | tf_op jit(solution)/shard_map/own_tile/pallas_call | solution.py:23
  4.8 1.6 %collective-permute-start = (f32[256,512]{1,0:T(8,128)S(1)}, f32[256,512]{1,0:T(8,128)S(1)}, u32[]{:S(2)}, u32[]{:S(2)}) collective-permute-start(f32[256,512]{1,0:T(8,128)S(1)} %get-tuple-element.44), channel_id=1, source_target_pairs={{0,1},{1,0},{2,3},{3,2},{4,5},{5,4},{6,7},{7,6},{8,9},{9,8},{10,11... | collective-permute-start | bytes 1572872 | tf_op jit(solution)/shard_map/ppermute | solution.py:233
  7.1 6.4 %collective-permute-done.4.refs_0_ = bf16[1552,128]{1,0:T(8,128)(2,1)S(1)} collective-permute-done((bf16[1552,128]{1,0:T(8,128)(2,1)S(1)}, bf16[1552,128]{1,0:T(8,128)(2,1)S(1)}, u32[]{:S(2)}, u32[]{:S(2)}) %collective-permute-start.4) | collective-permute-done | bytes 397344 | tf_op jit(solution)/shard_map/ppermute | solution.py:221
  14.0 4.3 %collective-permute-done.refs_2_ = f32[256,512]{1,0:T(8,128)S(1)} collective-permute-done((f32[256,512]{1,0:T(8,128)S(1)}, f32[256,512]{1,0:T(8,128)S(1)}, u32[]{:S(2)}, u32[]{:S(2)}) %collective-permute-start) | collective-permute-done | bytes 524320 | tf_op jit(solution)/shard_map/ppermute | solution.py:233
  18.3 5.3 %collective-permute-done.5.refs_0_ = bf16[1552,128]{1,0:T(8,128)(2,1)S(1)} collective-permute-done((bf16[1552,128]{1,0:T(8,128)(2,1)S(1)}, bf16[1552,128]{1,0:T(8,128)(2,1)S(1)}, u32[]{:S(2)}, u32[]{:S(2)}) %collective-permute-start.5) | collective-permute-done | bytes 397344 | tf_op jit(solution)/shard_map/ppermute | solution.py:221
  24.1 2.9 %collective-permute-done.1.refs_0_ = bf16[1552,256]{1,0:T(8,128)(2,1)S(1)} collective-permute-done((bf16[1552,256]{1,0:T(8,128)(2,1)S(1)}, bf16[1552,256]{1,0:T(8,128)(2,1)S(1)}, u32[]{:S(2)}, u32[]{:S(2)}) %collective-permute-start.1) | collective-permute-done | bytes 794656 | tf_op jit(solution)/shard_map/ppermute | solution.py:221
  27.0 1.0 %panel_tile.3 = (f32[8,512]{1,0:T(8,128)S(1)}, f32[256,512]{1,0:T(8,128)S(1)}, f32[256,512]{1,0:T(8,128)S(1)}) custom-call(bf16[512,1536]{1,0:T(8,128)(2,1)S(1)} %get-tuple-element.57.lt, bf16[1552,256]{1,0:T(8,128)(2,1)S(1)} %collective-permute-done.1.refs_0_, bf16[1552,256]{1,0:T(8,128)(2,1)S(1)} %collective-permute-done.2.refs_1_), custom_call_target="tpu_custom_call" | custom-call | flops 1 | bytes 1 | tf_op jit(solution)/shard_map/panel_tile/pallas_call | solution.py:23
  28.1 8.2 %collective-permute-done.6.refs_1_ = bf16[1552,128]{1,0:T(8,128)(2,1)S(1)} collective-permute-done((bf16[1552,128]{1,0:T(8,128)(2,1)S(1)}, bf16[1552,128]{1,0:T(8,128)(2,1)S(1)}, u32[]{:S(2)}, u32[]{:S(2)}) %collective-permute-start.6) | collective-permute-done | bytes 397344 | tf_op jit(solution)/shard_map/ppermute | solution.py:221
  36.3 1.9 %collective-permute-start.7 = (bf16[1552,128]{1,0:T(8,128)(2,1)S(1)}, bf16[1552,128]{1,0:T(8,128)(2,1)S(1)}, u32[]{:S(2)}, u32[]{:S(2)}) collective-permute-start(bf16[1552,128]{1,0:T(8,128)(2,1)S(1)} %collective-permute-done.6.refs_1_), channel_id=1, source_target_pairs={{4,6},{6,4},{12,14},{14,12},{20,22},{22,20},{28,30},{30,28},{5,7},... | collective-permute-start | bytes 1191944 | tf_op jit(solution)/shard_map/ppermute | solution.py:221
  38.8 2.7 %collective-permute-done.3.refs_5_ = f32[256,512]{1,0:T(8,128)S(1)} collective-permute-done((f32[256,512]{1,0:T(8,128)S(1)}, f32[256,512]{1,0:T(8,128)S(1)}, u32[]{:S(2)}, u32[]{:S(2)}) %collective-permute-start.3) | collective-permute-done | bytes 524320 | tf_op jit(solution)/shard_map/ppermute | solution.py:233
  41.5 1.0 %panel_tile.4 = (f32[8,512]{1,0:T(8,128)S(1)}, f32[256,512]{1,0:T(8,128)S(1)}, f32[256,512]{1,0:T(8,128)S(1)}) custom-call(bf16[512,1536]{1,0:T(8,128)(2,1)S(1)} %get-tuple-element.57.lt, bf16[1552,128]{1,0:T(8,128)(2,1)S(1)} %collective-permute-done.4.refs_0_, bf16[1552,128]{1,0:T(8,128)(2,1)S(1)} %collective-permute-done.6.refs_1_, ...), custom_call_target="tpu_custom_call" | custom-call | flops 1 | bytes 1 | tf_op jit(solution)/shard_map/panel_tile/pallas_call | solution.py:23
  42.5 9.2 %collective-permute-done.11.refs_1_ = bf16[1552,128]{1,0:T(8,128)(2,1)S(1)} collective-permute-done((bf16[1552,128]{1,0:T(8,128)(2,1)S(1)}, bf16[1552,128]{1,0:T(8,128)(2,1)S(1)}, u32[]{:S(2)}, u32[]{:S(2)}) %collective-permute-start.11) | collective-permute-done | bytes 397344 | tf_op jit(solution)/shard_map/ppermute | solution.py:221
  51.7 1.0 %collective-permute-done.12.refs_3_ = bf16[1552,128]{1,0:T(8,128)(2,1)S(1)} collective-permute-done((bf16[1552,128]{1,0:T(8,128)(2,1)S(1)}, bf16[1552,128]{1,0:T(8,128)(2,1)S(1)}, u32[]{:S(2)}, u32[]{:S(2)}) %collective-permute-start.12) | collective-permute-done | bytes 397344 | tf_op jit(solution)/shard_map/ppermute | solution.py:221
  52.7 1.7 %collective-permute-done.13.refs_4_ = bf16[1552,128]{1,0:T(8,128)(2,1)S(1)} collective-permute-done((bf16[1552,128]{1,0:T(8,128)(2,1)S(1)}, bf16[1552,128]{1,0:T(8,128)(2,1)S(1)}, u32[]{:S(2)}, u32[]{:S(2)}) %collective-permute-start.13) | collective-permute-done | bytes 397344 | tf_op jit(solution)/shard_map/ppermute | solution.py:221
  54.4 2.6 %collective-permute-done.10.refs_2_ = f32[256,512]{1,0:T(8,128)S(1)} collective-permute-done((f32[256,512]{1,0:T(8,128)S(1)}, f32[256,512]{1,0:T(8,128)S(1)}, u32[]{:S(2)}, u32[]{:S(2)}) %collective-permute-start.10) | collective-permute-done | bytes 524320 | tf_op jit(solution)/shard_map/ppermute | solution.py:233
  57.1 2.0 %collective-permute-start.14 = (bf16[1552,128]{1,0:T(8,128)(2,1)S(1)}, bf16[1552,128]{1,0:T(8,128)(2,1)S(1)}, u32[]{:S(2)}, u32[]{:S(2)}) collective-permute-start(bf16[1552,128]{1,0:T(8,128)(2,1)S(1)} %collective-permute-done.11.refs_1_), channel_id=1, source_target_pairs={{4,6},{6,4},{12,14},{14,12},{20,22},{22,20},{28,30},{30,28},{5,7},... | collective-permute-start | bytes 1191944 | tf_op jit(solution)/shard_map/ppermute | solution.py:221
  59.1 1.6 %collective-permute-done.14.refs_2_ = bf16[1552,128]{1,0:T(8,128)(2,1)S(1)} collective-permute-done((bf16[1552,128]{1,0:T(8,128)(2,1)S(1)}, bf16[1552,128]{1,0:T(8,128)(2,1)S(1)}, u32[]{:S(2)}, u32[]{:S(2)}) %collective-permute-start.14) | collective-permute-done | bytes 397344 | tf_op jit(solution)/shard_map/ppermute | solution.py:221
  60.7 1.0 %panel_tile.5 = (f32[8,512]{1,0:T(8,128)S(1)}, f32[256,512]{1,0:T(8,128)S(1)}, f32[256,512]{1,0:T(8,128)S(1)}) custom-call(bf16[512,1536]{1,0:T(8,128)(2,1)S(1)} %get-tuple-element.57.lt, bf16[1552,128]{1,0:T(8,128)(2,1)S(1)} %collective-permute-done.5.refs_0_, bf16[1552,128]{1,0:T(8,128)(2,1)S(1)} %collective-permute-done.11.refs_1_, ...), custom_call_target="tpu_custom_call" | custom-call | flops 1 | bytes 1 | tf_op jit(solution)/shard_map/panel_tile/pallas_call | solution.py:23
  61.8 2.2 %finish.3.refs_3_ = f32[256,2048]{1,0:T(8,128)} custom-call(f32[256,128]{1,0:T(8,128)S(1)} %get-tuple-element.41.row_coord, f32[256,128]{1,0:T(8,128)S(1)} %get-tuple-element.42.row_level, f32[8,512]{1,0:T(8,128)S(1)} %maximum_convert_fusion.refs_0_, f32[256,512]{1,0:T(8,128)S(1)} %get-tuple-element.70.refs_1_, f32[256,512]{1,0:T(8,128)S(1)} %collective-permute-done.refs_2_, ...), custom_call_target="tpu_custom_call" | custom-call | flops 1 | bytes 1 | tf_op jit(solution)/shard_map/finish/pallas_call | solution.py:192
  64.0 1.4 %finish.4.refs_3_ = f32[256,2048]{1,0:T(8,128)} custom-call(f32[256,128]{1,0:T(8,128)S(1)} %get-tuple-element.41.row_coord, f32[256,128]{1,0:T(8,128)S(1)} %get-tuple-element.42.row_level, f32[8,512]{1,0:T(8,128)S(1)} %get-tuple-element.67.refs_0_, f32[256,512]{1,0:T(8,128)S(1)} %get-tuple-element.68.refs_1_, ...), custom_call_target="tpu_custom_call", output_to_operand_aliasing={{}: (5, {})} | custom-call | flops 1 | bytes 1 | tf_op jit(solution)/shard_map/finish/pallas_call | solution.py:192
  65.4 10.3 %collective-permute-done.15.refs_2_ = f32[256,512]{1,0:T(8,128)S(1)} collective-permute-done((f32[256,512]{1,0:T(8,128)S(1)}, f32[256,512]{1,0:T(8,128)S(1)}, u32[]{:S(2)}, u32[]{:S(2)}) %collective-permute-start.15) | collective-permute-done | bytes 524320 | tf_op jit(solution)/shard_map/ppermute | solution.py:233
  75.7 1.4 %finish.5 = f32[256,2048]{1,0:T(8,128)} custom-call(f32[256,128]{1,0:T(8,128)S(1)} %get-tuple-element.41.row_coord, f32[256,128]{1,0:T(8,128)S(1)} %get-tuple-element.42.row_level, f32[8,512]{1,0:T(8,128)S(1)} %get-tuple-element.64.refs_0_, f32[256,512]{1,0:T(8,128)S(1)} %get-tuple-element.65.refs_1_, ...), custom_call_target="tpu_custom_call", output_to_operand_aliasing={{}: (5, {})} | custom-call | flops 1 | bytes 1 | tf_op jit(solution)/shard_map/finish/pallas_call | solution.py:192
  (25 shorter events, 4.1 us)
Async XLA Ops:
  0.0 1.4 %copy-start = (bf16[1536,512]{1,0:T(8,128)(2,1)S(1)}, bf16[1536,512]{1,0:T(8,128)(2,1)}, u32[]{:S(2)}) copy-start(bf16[1536,512]{1,0:T(8,128)(2,1)} %x.2) | copy-start | bytes 4718596
  1.4 0.7 copy-start.1
  2.5 11.0 %collective-permute-start.4 = (bf16[1552,128]{1,0:T(8,128)(2,1)S(1)}, bf16[1552,128]{1,0:T(8,128)(2,1)S(1)}, u32[]{:S(2)}, u32[]{:S(2)}) collective-permute-start(bf16[1552,128]{1,0:T(8,128)(2,1)S(1)} %get-tuple-element.49), channel_id=1, source_target_pairs={{0,4},{2,6},{4,0},{6,2},{8,12},{10,14},{12,8},{14,10},{16,20},{18,... | collective-permute-start | bytes 1191944 | tf_op jit(solution)/shard_map/ppermute | solution.py:221
  3.1 0.7 copy-start.2
  4.8 13.4 %collective-permute-start = (f32[256,512]{1,0:T(8,128)S(1)}, f32[256,512]{1,0:T(8,128)S(1)}, u32[]{:S(2)}, u32[]{:S(2)}) collective-permute-start(f32[256,512]{1,0:T(8,128)S(1)} %get-tuple-element.44), channel_id=1, source_target_pairs={{0,1},{1,0},{2,3},{3,2},{4,5},{5,4},{6,7},{7,6},{8,9},{9,8},{10,11... | collective-permute-start | bytes 1572872 | tf_op jit(solution)/shard_map/ppermute | solution.py:233
  6.5 17.6 %collective-permute-start.2 = (bf16[1552,256]{1,0:T(8,128)(2,1)S(1)}, bf16[1552,256]{1,0:T(8,128)(2,1)S(1)}, u32[]{:S(2)}, u32[]{:S(2)}) collective-permute-start(bf16[1552,256]{1,0:T(8,128)(2,1)S(1)} %get-tuple-element.46), channel_id=1, source_target_pairs={{0,26},{2,0},{4,30},{6,4},{8,2},{10,8},{12,6},{14,12},{16,10},{18,... | collective-permute-start | bytes 2383880 | tf_op jit(solution)/shard_map/ppermute | solution.py:221
  6.5 20.5 %collective-permute-start.1 = (bf16[1552,256]{1,0:T(8,128)(2,1)S(1)}, bf16[1552,256]{1,0:T(8,128)(2,1)S(1)}, u32[]{:S(2)}, u32[]{:S(2)}) collective-permute-start(bf16[1552,256]{1,0:T(8,128)(2,1)S(1)} %get-tuple-element.39), channel_id=1, source_target_pairs={{0,26},{2,0},{4,30},{6,4},{8,2},{10,8},{12,6},{14,12},{16,10},{18,... | collective-permute-start | bytes 2383880 | tf_op jit(solution)/shard_map/ppermute | solution.py:221
  13.5 10.1 %collective-permute-start.5 = (bf16[1552,128]{1,0:T(8,128)(2,1)S(1)}, bf16[1552,128]{1,0:T(8,128)(2,1)S(1)}, u32[]{:S(2)}, u32[]{:S(2)}) collective-permute-start(bf16[1552,128]{1,0:T(8,128)(2,1)S(1)} %get-tuple-element.51), channel_id=1, source_target_pairs={{0,4},{2,6},{4,0},{6,2},{8,12},{10,14},{12,8},{14,10},{16,20},{18,... | collective-permute-start | bytes 1191944 | tf_op jit(solution)/shard_map/ppermute | solution.py:221
  23.6 12.7 %collective-permute-start.6 = (bf16[1552,128]{1,0:T(8,128)(2,1)S(1)}, bf16[1552,128]{1,0:T(8,128)(2,1)S(1)}, u32[]{:S(2)}, u32[]{:S(2)}) collective-permute-start(bf16[1552,128]{1,0:T(8,128)(2,1)S(1)} %collective-permute-done.4.refs_0_), channel_id=1, source_target_pairs={{0,2},{2,0},{4,28},{6,30},{8,10},{10,8},{12,4},{14,6},{16,18},{18,... | collective-permute-start | bytes 1191944 | tf_op jit(solution)/shard_map/ppermute | solution.py:221
  24.0 14.2 %collective-permute-start.8 = (bf16[1552,128]{1,0:T(8,128)(2,1)S(1)}, bf16[1552,128]{1,0:T(8,128)(2,1)S(1)}, u32[]{:S(2)}, u32[]{:S(2)}) collective-permute-start(bf16[1552,128]{1,0:T(8,128)(2,1)S(1)} %get-tuple-element.54), channel_id=1, source_target_pairs={{0,28},{2,30},{4,0},{6,2},{8,4},{10,6},{12,8},{14,10},{16,12},{18,... | collective-permute-start | bytes 1191944 | tf_op jit(solution)/shard_map/ppermute | solution.py:221
  28.0 13.5 %collective-permute-start.3 = (f32[256,512]{1,0:T(8,128)S(1)}, f32[256,512]{1,0:T(8,128)S(1)}, u32[]{:S(2)}, u32[]{:S(2)}) collective-permute-start(f32[256,512]{1,0:T(8,128)S(1)} %get-tuple-element.47), channel_id=1, source_target_pairs={{0,1},{1,0},{2,3},{3,2},{4,5},{5,4},{6,7},{7,6},{8,9},{9,8},{10,11... | collective-permute-start | bytes 1572872 | tf_op jit(solution)/shard_map/ppermute | solution.py:233
  36.3 5.2 %collective-permute-start.7 = (bf16[1552,128]{1,0:T(8,128)(2,1)S(1)}, bf16[1552,128]{1,0:T(8,128)(2,1)S(1)}, u32[]{:S(2)}, u32[]{:S(2)}) collective-permute-start(bf16[1552,128]{1,0:T(8,128)(2,1)S(1)} %collective-permute-done.6.refs_1_), channel_id=1, source_target_pairs={{4,6},{6,4},{12,14},{14,12},{20,22},{22,20},{28,30},{30,28},{5,7},... | collective-permute-start | bytes 1191944 | tf_op jit(solution)/shard_map/ppermute | solution.py:221
  38.2 3.3 %collective-permute-start.9 = (bf16[1552,128]{1,0:T(8,128)(2,1)S(1)}, bf16[1552,128]{1,0:T(8,128)(2,1)S(1)}, u32[]{:S(2)}, u32[]{:S(2)}) collective-permute-start(bf16[1552,128]{1,0:T(8,128)(2,1)S(1)} %collective-permute-done.8.refs_3_), channel_id=1, source_target_pairs={{0,2},{2,0},{4,6},{6,4},{8,10},{10,8},{12,14},{14,12},{16,18},{18,... | collective-permute-start | bytes 1191944 | tf_op jit(solution)/shard_map/ppermute | solution.py:221
  38.8 13.0 %collective-permute-start.11 = (bf16[1552,128]{1,0:T(8,128)(2,1)S(1)}, bf16[1552,128]{1,0:T(8,128)(2,1)S(1)}, u32[]{:S(2)}, u32[]{:S(2)}) collective-permute-start(bf16[1552,128]{1,0:T(8,128)(2,1)S(1)} %collective-permute-done.5.refs_0_), channel_id=1, source_target_pairs={{0,2},{2,0},{4,28},{6,30},{8,10},{10,8},{12,4},{14,6},{16,18},{18,... | collective-permute-start | bytes 1191944 | tf_op jit(solution)/shard_map/ppermute | solution.py:221
  38.8 13.9 %collective-permute-start.12 = (bf16[1552,128]{1,0:T(8,128)(2,1)S(1)}, bf16[1552,128]{1,0:T(8,128)(2,1)S(1)}, u32[]{:S(2)}, u32[]{:S(2)}) collective-permute-start(bf16[1552,128]{1,0:T(8,128)(2,1)S(1)} %get-tuple-element.60), channel_id=1, source_target_pairs={{0,28},{2,30},{4,0},{6,2},{8,4},{10,6},{12,8},{14,10},{16,12},{18,... | collective-permute-start | bytes 1191944 | tf_op jit(solution)/shard_map/ppermute | solution.py:221
  42.5 14.6 %collective-permute-start.10 = (f32[256,512]{1,0:T(8,128)S(1)}, f32[256,512]{1,0:T(8,128)S(1)}, u32[]{:S(2)}, u32[]{:S(2)}) collective-permute-start(f32[256,512]{1,0:T(8,128)S(1)} %get-tuple-element.56), channel_id=1, source_target_pairs={{0,1},{1,0},{2,3},{3,2},{4,5},{5,4},{6,7},{7,6},{8,9},{9,8},{10,11... | collective-permute-start | bytes 1572872 | tf_op jit(solution)/shard_map/ppermute | solution.py:233
  52.7 1.7 %collective-permute-start.13 = (bf16[1552,128]{1,0:T(8,128)(2,1)S(1)}, bf16[1552,128]{1,0:T(8,128)(2,1)S(1)}, u32[]{:S(2)}, u32[]{:S(2)}) collective-permute-start(bf16[1552,128]{1,0:T(8,128)(2,1)S(1)} %collective-permute-done.12.refs_3_), channel_id=1, source_target_pairs={{0,2},{2,0},{4,6},{6,4},{8,10},{10,8},{12,14},{14,12},{16,18},{18,... | collective-permute-start | bytes 1191944 | tf_op jit(solution)/shard_map/ppermute | solution.py:221
  57.1 3.6 %collective-permute-start.14 = (bf16[1552,128]{1,0:T(8,128)(2,1)S(1)}, bf16[1552,128]{1,0:T(8,128)(2,1)S(1)}, u32[]{:S(2)}, u32[]{:S(2)}) collective-permute-start(bf16[1552,128]{1,0:T(8,128)(2,1)S(1)} %collective-permute-done.11.refs_1_), channel_id=1, source_target_pairs={{4,6},{6,4},{12,14},{14,12},{20,22},{22,20},{28,30},{30,28},{5,7},... | collective-permute-start | bytes 1191944 | tf_op jit(solution)/shard_map/ppermute | solution.py:221
  61.7 14.0 %collective-permute-start.15 = (f32[256,512]{1,0:T(8,128)S(1)}, f32[256,512]{1,0:T(8,128)S(1)}, u32[]{:S(2)}, u32[]{:S(2)}) collective-permute-start(f32[256,512]{1,0:T(8,128)S(1)} %get-tuple-element.66), channel_id=1, source_target_pairs={{0,1},{1,0},{2,3},{3,2},{4,5},{5,4},{6,7},{7,6},{8,9},{9,8},{10,11... | collective-permute-start | bytes 1572872 | tf_op jit(solution)/shard_map/ppermute | solution.py:233

commit v3 on v2

--- a/solution.py
+++ b/solution.py
@@ -8,6 +8,7 @@
 from jax.sharding import PartitionSpec as P
 
 PAD = 16
+STEPS = 32766.0
 CHUNK = 128
 PARAMS = pltpu.CompilerParams(vmem_limit_bytes=32 * 1024 * 1024)
 VMEM = pl.BlockSpec(memory_space=pltpu.VMEM)
@@ -38,15 +39,11 @@
     return jnp.where(r <= 1.0, near, jnp.where(r <= 2.0, far, 0.0))
 
 
-def prepare_kernel(x, coord, low, high, *chunks):
+def prepare_kernel(x, coord, low, high):
     members, width = x.shape
     first = 4 * width * lax.axis_index("mesh")
     jitter = coord[...] - first - 4 * lax.broadcasted_iota(jnp.int32, (1, width), 1)
     pad = jnp.broadcast_to(jitter.astype(F32), (PAD, width)).astype(x.dtype)
-    for i, chunk in enumerate(chunks):
-        span = slice(i * CHUNK, (i + 1) * CHUNK)
-        chunk[:members, :] = x[:, span]
-        chunk[members:, :] = pad[:, span]
     half = width // 2
     for part, span in ((low, slice(0, half)), (high, slice(half, width))):
         part[:members, :] = x[:, span]
@@ -100,6 +97,36 @@
     )
 
 
+def narrowed(block):
+    top = jnp.maximum(jnp.max(jnp.abs(block), axis=0, keepdims=True), 2.0**-126)
+    power = jnp.ceil(8.0 * jnp.log2(top) + 0.01)
+    steps = jnp.round(block * jnp.exp2(-0.125 * power) * STEPS)
+    return steps.astype(jnp.int32), power.astype(jnp.int32)
+
+
+def widened(steps, power):
+    return (steps.astype(F32) * jnp.exp2(0.125 * power.astype(F32) - 16.0)) * (65536.0 / STEPS)
+
+
+def pack(tile, packed):
+    rows = tile.shape[0]
+    for at in range(0, tile.shape[1] // 2, CHUNK):
+        span = slice(at, at + CHUNK)
+        high, high_power = narrowed(tile[:, 2 * at : 2 * at + CHUNK])
+        low, low_power = narrowed(tile[:, 2 * at + CHUNK : 2 * at + 2 * CHUNK])
+        packed[:rows, span] = (high << 16) | (low & 0xFFFF)
+        packed[rows : rows + 4, span] = jnp.broadcast_to(high_power, (4, CHUNK))
+        packed[rows + 4 :, span] = jnp.broadcast_to(low_power, (4, CHUNK))
+
+
+def unpack(packed, block, rows):
+    span = slice((block // 2) * CHUNK, (block // 2 + 1) * CHUNK)
+    words = packed[:rows, span]
+    if block % 2 == 0:
+        return widened(words >> 16, packed[rows : rows + 1, span])
+    return widened((words << 16) >> 16, packed[rows + 4 : rows + 5, span])
+
+
 def panel_kernel(lt, *refs, picks, count, rows):
     panels, cols, outs = refs[:count], refs[count], refs[count + 1 :]
     members = lt.shape[1]
@@ -112,7 +139,12 @@
             cols[:, at : at + wide] = panel[members:, :].astype(F32)[:8]
             at += wide
         block = jnp.concatenate([panel[:members, :] for panel in chosen], axis=1)
-        store_rows(jnp.dot(lt[...], block, preferred_element_type=F32), outs, 0)
+        tile = jnp.dot(lt[...], block, preferred_element_type=F32)
+        if len(rows) > 1:
+            pack(tile[: rows[0]], outs[0])
+            outs[1][...] = tile[rows[0] :]
+        else:
+            outs[0][...] = tile
 
     if len(picks) == 1:
         run(picks[0])
@@ -127,7 +159,9 @@
     width, members = lt.shape
     return call(
         functools.partial(panel_kernel, picks=picks, count=len(panels), rows=rows),
-        [jax.ShapeDtypeStruct((8, wide), F32)] + [jax.ShapeDtypeStruct((r, wide), F32) for r in rows],
+        [jax.ShapeDtypeStruct((8, wide), F32)]
+        + ([jax.ShapeDtypeStruct((rows[0] + 8, wide // 2), jnp.int32)] if len(rows) > 1 else [])
+        + [jax.ShapeDtypeStruct((rows[-1], wide), F32)],
         lt,
         *panels,
         name="panel_tile",
@@ -155,7 +189,10 @@
                 span = slice(offset + piece, offset + piece + CHUNK)
                 raw = parts[0][:, span]
                 for part in parts[1:]:
-                    raw = raw + part[:, span]
+                    if part.dtype == jnp.int32:
+                        raw = raw + unpack(part, span.start // CHUNK, raw.shape[0])
+                    else:
+                        raw = raw + part[:, span]
                 place = 4 * (piece + lax.broadcasted_iota(jnp.int32, (1, CHUNK), 1))
                 column = cols[0:1, span] + (base + place.astype(F32))
                 gap = jnp.abs(column - coord)
@@ -233,52 +270,54 @@
             return [parts[1], lax.ppermute(parts[0], "mem", [(0, 1), (1, 0)])]
         return [lax.psum_scatter(parts[0], "mem", scatter_dimension=0, tiled=True)]
 
-    pieces = width // CHUNK
-    relayed = pieces // 2
-    low, high, *chunks = call(
+    half = width // 2
+    low, high = call(
         prepare_kernel,
-        [jax.ShapeDtypeStruct((members + PAD, width // 2), perturbations.dtype)] * 2
-        + [jax.ShapeDtypeStruct((members + PAD, CHUNK), perturbations.dtype)] * pieces,
+        [jax.ShapeDtypeStruct((members + PAD, half), perturbations.dtype)] * 2,
         perturbations,
         coord,
         name="prepare",
     )
     lt, row_coord, row_level, *own = own_tile(after(perturbations, low), coord, levels, owned, rows)
     own_parts = reduced(own)
-    own_done = own_parts[-1]
     own_cols = jnp.concatenate([low[members : members + 8], high[members : members + 8]], axis=1).astype(F32)
 
-    def finished(out, groups):
+    first = permute(low, swap_x)
+    extra = [permute(a, extra_pairs) for a in (low, high)]
+    straight = permute(high, back_two)
+    passed = permute(first, relay)
+
+    def tile(panels, picks, *tokens):
+        cols, *parts = panel_tile(after(lt, *tokens), panels, picks, rows)
+        return cols, reduced(parts)
+
+    def finished(out, token, *groups):
+        groups = [(after(groups[0][0], token), *groups[0][1:])] + list(groups[1:])
         return finish(row_coord, row_level, groups, out, shape, period, width, everyone)
 
-    extra = [permute(a, extra_pairs) for a in (low, high)]
-    first = [permute(chunks[0], swap_x)]
-    first.append(permute(after(chunks[1], first[0], lt), swap_x))
-    straight = [permute(after(chunks[2], first[1], own_done), back_two)]
-    straight.append(permute(after(chunks[3], straight[0]), back_two))
-    passed = [permute(after(a, first[1], own_done), relay) for a in first]
-
-    extra_cols, *extra_parts = panel_tile(after(lt, own_done), extra, [[0, 1]], rows)
-    extra_parts = reduced(extra_parts)
-    token = extra_parts[-1]
-
-    out = None
-    groups = [
+    extra_cols, extra_parts = tile(extra, [[0, 1]], own_parts[-1])
+    other = permute(after(straight, extra_parts[-1]), siblings)
+    two_cols, two_parts = tile([straight], [[0]], extra_cols)
+    far = permute(after(passed, two_parts[-1]), far_siblings)
+    other_cols, other_parts = tile([other], [[0]], two_cols)
+    out = finished(
+        None,
+        other_cols,
         (own_cols, own_parts, [(0, width, "own", 0)]),
         (extra_cols, extra_parts, [(0, width, "extra", 0)]),
-    ]
-    for i in range(2):
-        other = permute(after(straight[i], passed[i], *([cols] if i else [])), siblings)
-        far = permute(after(passed[i], *([other, token] if i else [])), far_siblings)
-        panels = [first[i], passed[i], far, straight[i], other]
-        cols, *parts = panel_tile(after(lt, token), panels, [[0, 1, 3, 4], [1, 2, 3, 4]], rows)
-        out = finished(out, [(after(groups[0][0], cols), *groups[0][1:])] + groups[1:])
-        spans = []
-        for at, index in ((0, i), (2 * CHUNK, i + 2)):
-            spans += [(at, CHUNK, "two", index * CHUNK), (at + CHUNK, CHUNK, "other", index * CHUNK)]
-        groups = [(cols, reduced(parts), spans)]
-        token = groups[0][1][-1]
-    return finished(out, groups)
+    )
+    low_cols, low_parts = tile([first, passed, far], [[0, 1], [1, 2]], out, other_parts[-1])
+    out = finished(
+        out,
+        low_cols,
+        (two_cols, two_parts, [(0, half, "two", half)]),
+        (other_cols, other_parts, [(0, half, "other", half)]),
+    )
+    return finished(
+        out,
+        low_cols,
+        (low_cols, low_parts, [(0, half, "two", 0), (half, half, "other", 0)]),
+    )
 
 
 def solution(mesh):

time: 78.1 us -> 70.1 us (0.90)
  waiting for transfers between devices: 56.2 us -> 44.3 us
  starting transfers between devices: 8.59 us -> 13.1 us
    ppermute x4 -> x5, waiting for transfers between devices: 19.9 us -> 11.7 us  [reduced(): return [parts[1], lax.ppermute(parts[0], 'mem', [(0, 1), (1, 0)])]]
    ppermute x4 -> x5, starting transfers between devices: 1.86 us -> 7.99 us  [reduced(): return [parts[1], lax.ppermute(parts[0], 'mem', [(0, 1), (1, 0)])]]
    ppermute x12 -> x7, waiting for transfers between devices: 36.3 us -> 32.6 us  [permute(): return lax.ppermute(array, 'mesh', pairs)]
    ppermute x12 -> x7, starting transfers between devices: 6.73 us -> 5.09 us  [permute(): return lax.ppermute(array, 'mesh', pairs)]
    pallas_call x5 -> x6, Pallas kernels: 4.42 us -> 4.41 us  [call(): pl.pallas_call(kernel, out_shape=outs, in_specs=[VMEM] * len(operands), o...]
  transfers between devices with their start and end apart: 16 -> 12, of which waited for: 12 -> 6; matrix products, arithmetic and copies ran while one was open for 0% -> 0% of each run, Pallas kernels for 9% -> 10%
where the time goes in v3:
time: 70.1 us; the launch traced here: 69.9 us
  waiting for transfers between devices  44.3 us (63%)
  starting transfers between devices  13.1 us (19%)
  Pallas kernels  9.63 us (14%)
  local copies, waits for them, and re-layouts  2.77 us (4%)
    ppermute x7, waiting for transfers between devices, permute(): return lax.ppermute(array, 'mesh', pairs)  32.6 us
    ppermute x5, waiting for transfers between devices, reduced(): return [parts[1], lax.ppermute(parts[0], 'mem', [(0, 1), (1, 0)])]  11.7 us
    ppermute x5, starting transfers between devices, reduced(): return [parts[1], lax.ppermute(parts[0], 'mem', [(0, 1), (1, 0)])]  7.99 us
    pallas_call x3, Pallas kernels, finish(): pl.pallas_call(functools.partial(finish_kernel, plan=plan, period=period,...  5.22 us
    ppermute x7, starting transfers between devices, permute(): return lax.ppermute(array, 'mesh', pairs)  5.09 us
    pallas_call x6, Pallas kernels, call(): pl.pallas_call(kernel, out_shape=outs, in_specs=[VMEM] * len(operands), o...  4.41 us
    unnamed x6, local copies, waits for them, and re-layouts  2.77 us
  transfers between devices with their start and end apart: 12, of which 6 were waited for; matrix products, arithmetic and copies ran while one was open for 0% of the time, Pallas kernels for 10%

profile of v3, /device:TPU:26, one launch (start us, length us, event | category | flops | bytes accessed | tf_op | source)
XLA Modules:
  0.0 69.9 jit_solution(13482682973806325597)
XLA Ops:
  0.0 1.4 %copy-done = bf16[1536,512]{1,0:T(8,128)(2,1)S(1)} copy-done((bf16[1536,512]{1,0:T(8,128)(2,1)S(1)}, bf16[1536,512]{1,0:T(8,128)(2,1)}, u32[]{:S(2)}) %copy-start) | copy-done | bytes 1572888
  1.4 0.7 copy-done.1
  2.2 0.6 collective-permute-start.7
  3.4 0.7 copy-done.2
  4.0 1.1 %own_tile.1 = (bf16[512,1536]{1,0:T(8,128)(2,1)S(1)}, f32[256,128]{1,0:T(8,128)S(1)}, f32[256,128]{1,0:T(8,128)S(1)}, f32[256,512]{1,0:T(8,128)S(1)}, f32[256,512]{1,0:T(8,128)S(1)}) custom-call(bf16[1536,512]{1,0:T(8,128)(2,1)S(1)} %copy-done, s32[1,512]{1,0:T(1,128)S(1)} %bitcast.3, s32[1,512]{1,0:T(1,128)S(1)} %bitcast.4), custom_call_target="tpu_custom_call" | custom-call | flops 1 | bytes 1 | tf_op jit(solution)/shard_map/own_tile/pallas_call | solution.py:24
  5.1 1.6 %collective-permute-start = (f32[256,512]{1,0:T(8,128)S(1)}, f32[256,512]{1,0:T(8,128)S(1)}, u32[]{:S(2)}, u32[]{:S(2)}) collective-permute-start(f32[256,512]{1,0:T(8,128)S(1)} %get-tuple-element.40), channel_id=1, source_target_pairs={{0,1},{1,0},{2,3},{3,2},{4,5},{5,4},{6,7},{7,6},{8,9},{9,8},{10,11... | collective-permute-start | bytes 1572872 | tf_op jit(solution)/shard_map/ppermute | solution.py:270
  6.8 1.5 %collective-permute-start.3 = (bf16[1552,256]{1,0:T(8,128)(2,1)S(1)}, bf16[1552,256]{1,0:T(8,128)(2,1)S(1)}, u32[]{:S(2)}, u32[]{:S(2)}) collective-permute-start(bf16[1552,256]{1,0:T(8,128)(2,1)S(1)} %get-tuple-element.39), channel_id=1, source_target_pairs={{0,28},{2,30},{4,0},{6,2},{8,4},{10,6},{12,8},{14,10},{16,12},{18,... | collective-permute-start | bytes 2383880 | tf_op jit(solution)/shard_map/ppermute | solution.py:258
  8.3 21.9 %collective-permute-done.7.refs_0_ = bf16[1552,256]{1,0:T(8,128)(2,1)S(1)} collective-permute-done((bf16[1552,256]{1,0:T(8,128)(2,1)S(1)}, bf16[1552,256]{1,0:T(8,128)(2,1)S(1)}, u32[]{:S(2)}, u32[]{:S(2)}) %collective-permute-start.7) | collective-permute-done | bytes 794656 | tf_op jit(solution)/shard_map/ppermute | solution.py:258
  30.7 1.0 %panel_tile.4 = (f32[8,512]{1,0:T(8,128)S(1)}, s32[264,256]{1,0:T(8,128)S(1)}, f32[256,512]{1,0:T(8,128)S(1)}) custom-call(bf16[512,1536]{1,0:T(8,128)(2,1)S(1)} %get-tuple-element.53.lt, bf16[1552,256]{1,0:T(8,128)(2,1)S(1)} %collective-permute-done.1.refs_0_, bf16[1552,256]{1,0:T(8,128)(2,1)S(1)} %collective-permute-done.2.refs_1_), custom_call_target="tpu_custom_call" | custom-call | flops 1 | bytes 1 | tf_op jit(solution)/shard_map/panel_tile/pallas_call | solution.py:24
  31.7 1.6 %collective-permute-start.4 = (s32[264,256]{1,0:T(8,128)S(1)}, s32[264,256]{1,0:T(8,128)S(1)}, u32[]{:S(2)}, u32[]{:S(2)}) collective-permute-start(s32[264,256]{1,0:T(8,128)S(1)} %get-tuple-element.46), channel_id=1, source_target_pairs={{0,1},{1,0},{2,3},{3,2},{4,5},{5,4},{6,7},{7,6},{8,9},{9,8},{10,11... | collective-permute-start | bytes 811016 | tf_op jit(solution)/shard_map/ppermute | solution.py:270
  33.3 9.0 %collective-permute-done.3.refs_0_ = bf16[1552,256]{1,0:T(8,128)(2,1)S(1)} collective-permute-done((bf16[1552,256]{1,0:T(8,128)(2,1)S(1)}, bf16[1552,256]{1,0:T(8,128)(2,1)S(1)}, u32[]{:S(2)}, u32[]{:S(2)}) %collective-permute-start.3) | collective-permute-done | bytes 794656 | tf_op jit(solution)/shard_map/ppermute | solution.py:258
  43.0 1.6 %collective-permute-start.9 = (s32[264,128]{1,0:T(8,128)S(1)}, s32[264,128]{1,0:T(8,128)S(1)}, u32[]{:S(2)}, u32[]{:S(2)}) collective-permute-start(s32[264,128]{1,0:T(8,128)S(1)} %get-tuple-element.54), channel_id=1, source_target_pairs={{0,1},{1,0},{2,3},{3,2},{4,5},{5,4},{6,7},{7,6},{8,9},{9,8},{10,11... | collective-permute-start | bytes 405512 | tf_op jit(solution)/shard_map/ppermute | solution.py:270
  44.6 4.4 %collective-permute-done.9.refs_2_ = s32[264,128]{1,0:T(8,128)S(1)} collective-permute-done((s32[264,128]{1,0:T(8,128)S(1)}, s32[264,128]{1,0:T(8,128)S(1)}, u32[]{:S(2)}, u32[]{:S(2)}) %collective-permute-start.9) | collective-permute-done | bytes 135200 | tf_op jit(solution)/shard_map/ppermute | solution.py:270
  49.0 1.6 %collective-permute-done.8.refs_1_ = bf16[1552,256]{1,0:T(8,128)(2,1)S(1)} collective-permute-done((bf16[1552,256]{1,0:T(8,128)(2,1)S(1)}, bf16[1552,256]{1,0:T(8,128)(2,1)S(1)}, u32[]{:S(2)}, u32[]{:S(2)}) %collective-permute-start.8) | collective-permute-done | bytes 794656 | tf_op jit(solution)/shard_map/ppermute | solution.py:258
  50.6 1.9 %collective-permute-start.10 = (bf16[1552,256]{1,0:T(8,128)(2,1)S(1)}, bf16[1552,256]{1,0:T(8,128)(2,1)S(1)}, u32[]{:S(2)}, u32[]{:S(2)}) collective-permute-start(bf16[1552,256]{1,0:T(8,128)(2,1)S(1)} %collective-permute-done.8.refs_1_), channel_id=1, source_target_pairs={{4,6},{6,4},{12,14},{14,12},{20,22},{22,20},{28,30},{30,28},{5,7},... | collective-permute-start | bytes 2383880 | tf_op jit(solution)/shard_map/ppermute | solution.py:258
  52.5 0.6 panel_tile.6
  53.1 1.6 %collective-permute-start.6 = (s32[264,128]{1,0:T(8,128)S(1)}, s32[264,128]{1,0:T(8,128)S(1)}, u32[]{:S(2)}, u32[]{:S(2)}) collective-permute-start(s32[264,128]{1,0:T(8,128)S(1)} %get-tuple-element.52), channel_id=1, source_target_pairs={{0,1},{1,0},{2,3},{3,2},{4,5},{5,4},{6,7},{7,6},{8,9},{9,8},{10,11... | collective-permute-start | bytes 405512 | tf_op jit(solution)/shard_map/ppermute | solution.py:270
  54.7 2.3 %finish.3.refs_6_ = f32[256,2048]{1,0:T(8,128)} custom-call(f32[256,128]{1,0:T(8,128)S(1)} %get-tuple-element.36.row_coord, f32[256,128]{1,0:T(8,128)S(1)} %get-tuple-element.37.row_level, f32[8,512]{1,0:T(8,128)S(1)} %maximum_convert_fusion.refs_0_, f32[256,512]{1,0:T(8,128)S(1)} %get-tuple-element.50.refs_1_, f32[256,512]{1,0:T(8,128)S(1)} %collective-permute-done.refs_2_, ...), custom_call_target="tpu_custom_call" | custom-call | flops 1 | bytes 1 | tf_op jit(solution)/shard_map/finish/pallas_call | solution.py:229
  57.0 2.2 %collective-permute-done.6.refs_5_ = s32[264,128]{1,0:T(8,128)S(1)} collective-permute-done((s32[264,128]{1,0:T(8,128)S(1)}, s32[264,128]{1,0:T(8,128)S(1)}, u32[]{:S(2)}, u32[]{:S(2)}) %collective-permute-start.6) | collective-permute-done | bytes 135200 | tf_op jit(solution)/shard_map/ppermute | solution.py:270
  59.2 1.0 %panel_tile.7 = (f32[8,512]{1,0:T(8,128)S(1)}, s32[264,256]{1,0:T(8,128)S(1)}, f32[256,512]{1,0:T(8,128)S(1)}) custom-call(bf16[512,1536]{1,0:T(8,128)(2,1)S(1)} %get-tuple-element.53.lt, bf16[1552,256]{1,0:T(8,128)(2,1)S(1)} %collective-permute-done.7.refs_0_, bf16[1552,256]{1,0:T(8,128)(2,1)S(1)} %collective-permute-done.8.refs_1_, ...), custom_call_target="tpu_custom_call" | custom-call | flops 1 | bytes 1 | tf_op jit(solution)/shard_map/panel_tile/pallas_call | solution.py:24
  60.2 1.6 %collective-permute-start.11 = (s32[264,256]{1,0:T(8,128)S(1)}, s32[264,256]{1,0:T(8,128)S(1)}, u32[]{:S(2)}, u32[]{:S(2)}) collective-permute-start(s32[264,256]{1,0:T(8,128)S(1)} %get-tuple-element.59), channel_id=1, source_target_pairs={{0,1},{1,0},{2,3},{3,2},{4,5},{5,4},{6,7},{7,6},{8,9},{9,8},{10,11... | collective-permute-start | bytes 811016 | tf_op jit(solution)/shard_map/ppermute | solution.py:270
  61.8 1.5 %finish.4.refs_3_ = f32[256,2048]{1,0:T(8,128)} custom-call(f32[256,128]{1,0:T(8,128)S(1)} %get-tuple-element.36.row_coord, f32[256,128]{1,0:T(8,128)S(1)} %get-tuple-element.37.row_level, f32[8,256]{1,0:T(8,128)S(1)} %get-tuple-element.60.refs_0_, f32[256,256]{1,0:T(8,128)S(1)} %get-tuple-element.61.refs_1_, ...), custom_call_target="tpu_custom_call", output_to_operand_aliasing={{}: (8, {})} | custom-call | flops 1 | bytes 1 | tf_op jit(solution)/shard_map/finish/pallas_call | solution.py:229
  63.3 5.1 %collective-permute-done.11.refs_2_ = s32[264,256]{1,0:T(8,128)S(1)} collective-permute-done((s32[264,256]{1,0:T(8,128)S(1)}, s32[264,256]{1,0:T(8,128)S(1)}, u32[]{:S(2)}, u32[]{:S(2)}) %collective-permute-start.11) | collective-permute-done | bytes 270368 | tf_op jit(solution)/shard_map/ppermute | solution.py:270
  68.4 1.5 %finish.5 = f32[256,2048]{1,0:T(8,128)} custom-call(f32[256,128]{1,0:T(8,128)S(1)} %get-tuple-element.36.row_coord, f32[256,128]{1,0:T(8,128)S(1)} %get-tuple-element.37.row_level, f32[8,512]{1,0:T(8,128)S(1)} %get-tuple-element.57.refs_0_, f32[256,512]{1,0:T(8,128)S(1)} %get-tuple-element.58.refs_1_, ...), custom_call_target="tpu_custom_call", output_to_operand_aliasing={{}: (5, {})} | custom-call | flops 1 | bytes 1 | tf_op jit(solution)/shard_map/finish/pallas_call | solution.py:229
  (18 shorter events, 1.8 us)
Async XLA Ops:
  0.0 1.4 %copy-start = (bf16[1536,512]{1,0:T(8,128)(2,1)S(1)}, bf16[1536,512]{1,0:T(8,128)(2,1)}, u32[]{:S(2)}) copy-start(bf16[1536,512]{1,0:T(8,128)(2,1)} %x.2) | copy-start | bytes 4718596
  1.4 0.7 copy-start.1
  2.2 28.0 %collective-permute-start.7 = (bf16[1552,256]{1,0:T(8,128)(2,1)S(1)}, bf16[1552,256]{1,0:T(8,128)(2,1)S(1)}, u32[]{:S(2)}, u32[]{:S(2)}) collective-permute-start(bf16[1552,256]{1,0:T(8,128)(2,1)S(1)} %get-tuple-element.34), channel_id=1, source_target_pairs={{0,4},{2,6},{4,0},{6,2},{8,12},{10,14},{12,8},{14,10},{16,20},{18,... | collective-permute-start | bytes 2383880 | tf_op jit(solution)/shard_map/ppermute | solution.py:258
  2.8 27.9 %collective-permute-start.1 = (bf16[1552,256]{1,0:T(8,128)(2,1)S(1)}, bf16[1552,256]{1,0:T(8,128)(2,1)S(1)}, u32[]{:S(2)}, u32[]{:S(2)}) collective-permute-start(bf16[1552,256]{1,0:T(8,128)(2,1)S(1)} %get-tuple-element.34), channel_id=1, source_target_pairs={{0,26},{2,0},{4,30},{6,4},{8,2},{10,8},{12,6},{14,12},{16,10},{18,... | collective-permute-start | bytes 2383880 | tf_op jit(solution)/shard_map/ppermute | solution.py:258
  2.8 27.9 %collective-permute-start.2 = (bf16[1552,256]{1,0:T(8,128)(2,1)S(1)}, bf16[1552,256]{1,0:T(8,128)(2,1)S(1)}, u32[]{:S(2)}, u32[]{:S(2)}) collective-permute-start(bf16[1552,256]{1,0:T(8,128)(2,1)S(1)} %get-tuple-element.39), channel_id=1, source_target_pairs={{0,26},{2,0},{4,30},{6,4},{8,2},{10,8},{12,6},{14,12},{16,10},{18,... | collective-permute-start | bytes 2383880 | tf_op jit(solution)/shard_map/ppermute | solution.py:258
  3.4 0.7 copy-start.2
  5.1 25.5 %collective-permute-start = (f32[256,512]{1,0:T(8,128)S(1)}, f32[256,512]{1,0:T(8,128)S(1)}, u32[]{:S(2)}, u32[]{:S(2)}) collective-permute-start(f32[256,512]{1,0:T(8,128)S(1)} %get-tuple-element.40), channel_id=1, source_target_pairs={{0,1},{1,0},{2,3},{3,2},{4,5},{5,4},{6,7},{7,6},{8,9},{9,8},{10,11... | collective-permute-start | bytes 1572872 | tf_op jit(solution)/shard_map/ppermute | solution.py:270
  6.8 35.5 %collective-permute-start.3 = (bf16[1552,256]{1,0:T(8,128)(2,1)S(1)}, bf16[1552,256]{1,0:T(8,128)(2,1)S(1)}, u32[]{:S(2)}, u32[]{:S(2)}) collective-permute-start(bf16[1552,256]{1,0:T(8,128)(2,1)S(1)} %get-tuple-element.39), channel_id=1, source_target_pairs={{0,28},{2,30},{4,0},{6,2},{8,4},{10,6},{12,8},{14,10},{16,12},{18,... | collective-permute-start | bytes 2383880 | tf_op jit(solution)/shard_map/ppermute | solution.py:258
  30.2 20.4 %collective-permute-start.8 = (bf16[1552,256]{1,0:T(8,128)(2,1)S(1)}, bf16[1552,256]{1,0:T(8,128)(2,1)S(1)}, u32[]{:S(2)}, u32[]{:S(2)}) collective-permute-start(bf16[1552,256]{1,0:T(8,128)(2,1)S(1)} %collective-permute-done.7.refs_0_), channel_id=1, source_target_pairs={{0,2},{2,0},{4,28},{6,30},{8,10},{10,8},{12,4},{14,6},{16,18},{18,... | collective-permute-start | bytes 2383880 | tf_op jit(solution)/shard_map/ppermute | solution.py:258
  31.7 11.2 %collective-permute-start.4 = (s32[264,256]{1,0:T(8,128)S(1)}, s32[264,256]{1,0:T(8,128)S(1)}, u32[]{:S(2)}, u32[]{:S(2)}) collective-permute-start(s32[264,256]{1,0:T(8,128)S(1)} %get-tuple-element.46), channel_id=1, source_target_pairs={{0,1},{1,0},{2,3},{3,2},{4,5},{5,4},{6,7},{7,6},{8,9},{9,8},{10,11... | collective-permute-start | bytes 811016 | tf_op jit(solution)/shard_map/ppermute | solution.py:270
  42.9 9.6 %collective-permute-start.5 = (bf16[1552,256]{1,0:T(8,128)(2,1)S(1)}, bf16[1552,256]{1,0:T(8,128)(2,1)S(1)}, u32[]{:S(2)}, u32[]{:S(2)}) collective-permute-start(bf16[1552,256]{1,0:T(8,128)(2,1)S(1)} %collective-permute-done.3.refs_0_), channel_id=1, source_target_pairs={{0,2},{2,0},{4,6},{6,4},{8,10},{10,8},{12,14},{14,12},{16,18},{18,... | collective-permute-start | bytes 2383880 | tf_op jit(solution)/shard_map/ppermute | solution.py:258
  43.0 6.0 %collective-permute-start.9 = (s32[264,128]{1,0:T(8,128)S(1)}, s32[264,128]{1,0:T(8,128)S(1)}, u32[]{:S(2)}, u32[]{:S(2)}) collective-permute-start(s32[264,128]{1,0:T(8,128)S(1)} %get-tuple-element.54), channel_id=1, source_target_pairs={{0,1},{1,0},{2,3},{3,2},{4,5},{5,4},{6,7},{7,6},{8,9},{9,8},{10,11... | collective-permute-start | bytes 405512 | tf_op jit(solution)/shard_map/ppermute | solution.py:270
  50.6 8.6 %collective-permute-start.10 = (bf16[1552,256]{1,0:T(8,128)(2,1)S(1)}, bf16[1552,256]{1,0:T(8,128)(2,1)S(1)}, u32[]{:S(2)}, u32[]{:S(2)}) collective-permute-start(bf16[1552,256]{1,0:T(8,128)(2,1)S(1)} %collective-permute-done.8.refs_1_), channel_id=1, source_target_pairs={{4,6},{6,4},{12,14},{14,12},{20,22},{22,20},{28,30},{30,28},{5,7},... | collective-permute-start | bytes 2383880 | tf_op jit(solution)/shard_map/ppermute | solution.py:258
  53.1 6.1 %collective-permute-start.6 = (s32[264,128]{1,0:T(8,128)S(1)}, s32[264,128]{1,0:T(8,128)S(1)}, u32[]{:S(2)}, u32[]{:S(2)}) collective-permute-start(s32[264,128]{1,0:T(8,128)S(1)} %get-tuple-element.52), channel_id=1, source_target_pairs={{0,1},{1,0},{2,3},{3,2},{4,5},{5,4},{6,7},{7,6},{8,9},{9,8},{10,11... | collective-permute-start | bytes 405512 | tf_op jit(solution)/shard_map/ppermute | solution.py:270
  60.2 8.2 %collective-permute-start.11 = (s32[264,256]{1,0:T(8,128)S(1)}, s32[264,256]{1,0:T(8,128)S(1)}, u32[]{:S(2)}, u32[]{:S(2)}) collective-permute-start(s32[264,256]{1,0:T(8,128)S(1)} %get-tuple-element.59), channel_id=1, source_target_pairs={{0,1},{1,0},{2,3},{3,2},{4,5},{5,4},{6,7},{7,6},{8,9},{9,8},{10,11... | collective-permute-start | bytes 811016 | tf_op jit(solution)/shard_map/ppermute | solution.py:270

commit v4 on v3

--- a/solution.py
+++ b/solution.py
@@ -284,40 +284,33 @@
 
     first = permute(low, swap_x)
     extra = [permute(a, extra_pairs) for a in (low, high)]
-    straight = permute(high, back_two)
+    straight = permute(after(high, first), back_two)
     passed = permute(first, relay)
 
     def tile(panels, picks, *tokens):
-        cols, *parts = panel_tile(after(lt, *tokens), panels, picks, rows)
-        return cols, reduced(parts)
+        return panel_tile(after(lt, *tokens), panels, picks, rows)
 
     def finished(out, token, *groups):
         groups = [(after(groups[0][0], token), *groups[0][1:])] + list(groups[1:])
         return finish(row_coord, row_level, groups, out, shape, period, width, everyone)
 
-    extra_cols, extra_parts = tile(extra, [[0, 1]], own_parts[-1])
+    extra_cols, *extra_parts = tile(extra, [[0, 1]], own_parts[-1])
+    extra_parts = reduced(extra_parts)
     other = permute(after(straight, extra_parts[-1]), siblings)
-    two_cols, two_parts = tile([straight], [[0]], extra_cols)
-    far = permute(after(passed, two_parts[-1]), far_siblings)
-    other_cols, other_parts = tile([other], [[0]], two_cols)
+    far = permute(passed, far_siblings)
+    two_cols, *two_parts = tile([first, passed, straight], [[0, 2], [1, 2]], extra_cols)
+    two_parts = reduced(two_parts)
     out = finished(
         None,
-        other_cols,
+        two_cols,
         (own_cols, own_parts, [(0, width, "own", 0)]),
         (extra_cols, extra_parts, [(0, width, "extra", 0)]),
     )
-    low_cols, low_parts = tile([first, passed, far], [[0, 1], [1, 2]], out, other_parts[-1])
-    out = finished(
-        out,
-        low_cols,
-        (two_cols, two_parts, [(0, half, "two", half)]),
-        (other_cols, other_parts, [(0, half, "other", half)]),
-    )
-    return finished(
-        out,
-        low_cols,
-        (low_cols, low_parts, [(0, half, "two", 0), (half, half, "other", 0)]),
-    )
+    other_cols, *other_parts = tile([passed, far, other], [[0, 2], [1, 2]], two_cols)
+    other_parts[0] = after(other_parts[0], out, two_parts[-1])
+    other_parts = reduced(other_parts)
+    out = finished(out, other_cols, (two_cols, two_parts, [(0, width, "two", 0)]))
+    return finished(out, other_cols, (other_cols, other_parts, [(0, width, "other", 0)]))
 
 
 def solution(mesh):

time: 70.1 us -> 64.4 us (0.919)
  waiting for transfers between devices: 44.3 us -> 40.7 us
  starting transfers between devices: 13.1 us -> 11 us
    ppermute x7, waiting for transfers between devices: 32.6 us -> 25.2 us  [permute(): return lax.ppermute(array, 'mesh', pairs)]
    ppermute x5 -> x4, waiting for transfers between devices: 11.7 us -> 15.5 us  [reduced(): return [parts[1], lax.ppermute(parts[0], 'mem', [(0, 1), (1, 0)])]]
    ppermute x5 -> x4, starting transfers between devices: 7.99 us -> 6.34 us  [reduced(): return [parts[1], lax.ppermute(parts[0], 'mem', [(0, 1), (1, 0)])]]
    pallas_call x6 -> x5, Pallas kernels: 4.41 us -> 4.28 us  [call(): pl.pallas_call(kernel, out_shape=outs, in_specs=[VMEM] * len(operands), o...]
  transfers between devices with their start and end apart: 12 -> 11, of which waited for: 6 -> 5; matrix products, arithmetic and copies ran while one was open for 0% -> 0% of each run, Pallas kernels for 10% -> 12%
where the time goes in v4:
time: 64.4 us; the launch traced here: 64.2 us
  waiting for transfers between devices  40.7 us (63%)
  starting transfers between devices  11 us (17%)
  Pallas kernels  9.68 us (15%)
  local copies, waits for them, and re-layouts  2.77 us (4%)
    ppermute x7, waiting for transfers between devices, permute(): return lax.ppermute(array, 'mesh', pairs)  25.2 us
    ppermute x4, waiting for transfers between devices, reduced(): return [parts[1], lax.ppermute(parts[0], 'mem', [(0, 1), (1, 0)])]  15.5 us
    ppermute x4, starting transfers between devices, reduced(): return [parts[1], lax.ppermute(parts[0], 'mem', [(0, 1), (1, 0)])]  6.34 us
    pallas_call x3, Pallas kernels, finish(): pl.pallas_call(functools.partial(finish_kernel, plan=plan, period=period,...  5.41 us
    ppermute x7, starting transfers between devices, permute(): return lax.ppermute(array, 'mesh', pairs)  4.62 us
    pallas_call x5, Pallas kernels, call(): pl.pallas_call(kernel, out_shape=outs, in_specs=[VMEM] * len(operands), o...  4.28 us
    unnamed x6, local copies, waits for them, and re-layouts  2.77 us
  transfers between devices with their start and end apart: 11, of which 5 were waited for; matrix products, arithmetic and copies ran while one was open for 0% of the time, Pallas kernels for 12%

profile of v4, /device:TPU:26, one launch (start us, length us, event | category | flops | bytes accessed | tf_op | source)
XLA Modules:
  0.0 64.2 jit_solution(5902446764304778181)
XLA Ops:
  0.0 1.4 %copy-done = bf16[1536,512]{1,0:T(8,128)(2,1)S(1)} copy-done((bf16[1536,512]{1,0:T(8,128)(2,1)S(1)}, bf16[1536,512]{1,0:T(8,128)(2,1)}, u32[]{:S(2)}) %copy-start) | copy-done | bytes 1572888
  1.4 0.7 %copy-done.1 = s32[512]{0:T(512)S(1)} copy-done((s32[512]{0:T(512)S(1)}, s32[512]{0:T(512)}, u32[]{:S(2)}) %copy-start.1) | copy-done | bytes 2072
  2.2 0.6 collective-permute-start.3
  2.8 0.6 collective-permute-start.1
  3.4 0.7 %copy-done.2 = s32[512]{0:T(512)S(1)} copy-done((s32[512]{0:T(512)S(1)}, s32[512]{0:T(512)}, u32[]{:S(2)}) %copy-start.2) | copy-done | bytes 2072
  4.0 1.1 %own_tile.1 = (bf16[512,1536]{1,0:T(8,128)(2,1)S(1)}, f32[256,128]{1,0:T(8,128)S(1)}, f32[256,128]{1,0:T(8,128)S(1)}, f32[256,512]{1,0:T(8,128)S(1)}, f32[256,512]{1,0:T(8,128)S(1)}) custom-call(bf16[1536,512]{1,0:T(8,128)(2,1)S(1)} %copy-done, s32[1,512]{1,0:T(1,128)S(1)} %bitcast.3, s32[1,512]{1,0:T(1,128)S(1)} %bitcast.4), custom_call_target="tpu_custom_call" | custom-call | flops 1 | bytes 1 | tf_op jit(solution)/shard_map/own_tile/pallas_call | solution.py:24
  5.1 1.6 %collective-permute-start = (f32[256,512]{1,0:T(8,128)S(1)}, f32[256,512]{1,0:T(8,128)S(1)}, u32[]{:S(2)}, u32[]{:S(2)}) collective-permute-start(f32[256,512]{1,0:T(8,128)S(1)} %get-tuple-element.36), channel_id=1, source_target_pairs={{0,1},{1,0},{2,3},{3,2},{4,5},{5,4},{6,7},{7,6},{8,9},{9,8},{10,11... | collective-permute-start | bytes 1572872 | tf_op jit(solution)/shard_map/ppermute | solution.py:270
  6.8 14.9 %collective-permute-done.3.refs_0_ = bf16[1552,256]{1,0:T(8,128)(2,1)S(1)} collective-permute-done((bf16[1552,256]{1,0:T(8,128)(2,1)S(1)}, bf16[1552,256]{1,0:T(8,128)(2,1)S(1)}, u32[]{:S(2)}, u32[]{:S(2)}) %collective-permute-start.3) | collective-permute-done | bytes 794656 | tf_op jit(solution)/shard_map/ppermute | solution.py:258
  21.7 0.5 collective-permute-start.5
  22.7 1.0 %panel_tile.3 = (f32[8,512]{1,0:T(8,128)S(1)}, s32[264,256]{1,0:T(8,128)S(1)}, f32[256,512]{1,0:T(8,128)S(1)}) custom-call(bf16[512,1536]{1,0:T(8,128)(2,1)S(1)} %get-tuple-element.43.lt, bf16[1552,256]{1,0:T(8,128)(2,1)S(1)} %collective-permute-done.1.refs_0_, bf16[1552,256]{1,0:T(8,128)(2,1)S(1)} %collective-permute-done.2.refs_1_), custom_call_target="tpu_custom_call" | custom-call | flops 1 | bytes 1 | tf_op jit(solution)/shard_map/panel_tile/pallas_call | solution.py:24
  23.7 1.6 %collective-permute-start.7 = (s32[264,256]{1,0:T(8,128)S(1)}, s32[264,256]{1,0:T(8,128)S(1)}, u32[]{:S(2)}, u32[]{:S(2)}) collective-permute-start(s32[264,256]{1,0:T(8,128)S(1)} %get-tuple-element.44), channel_id=1, source_target_pairs={{0,1},{1,0},{2,3},{3,2},{4,5},{5,4},{6,7},{7,6},{8,9},{9,8},{10,11... | collective-permute-start | bytes 811016 | tf_op jit(solution)/shard_map/ppermute | solution.py:270
  25.3 7.4 %collective-permute-done.7.refs_5_ = s32[264,256]{1,0:T(8,128)S(1)} collective-permute-done((s32[264,256]{1,0:T(8,128)S(1)}, s32[264,256]{1,0:T(8,128)S(1)}, u32[]{:S(2)}, u32[]{:S(2)}) %collective-permute-start.7) | collective-permute-done | bytes 270368 | tf_op jit(solution)/shard_map/ppermute | solution.py:270
  32.8 10.2 %collective-permute-done.5.refs_2_ = bf16[1552,256]{1,0:T(8,128)(2,1)S(1)} collective-permute-done((bf16[1552,256]{1,0:T(8,128)(2,1)S(1)}, bf16[1552,256]{1,0:T(8,128)(2,1)S(1)}, u32[]{:S(2)}, u32[]{:S(2)}) %collective-permute-start.5) | collective-permute-done | bytes 794656 | tf_op jit(solution)/shard_map/ppermute | solution.py:258
  43.0 1.9 %collective-permute-start.6 = (bf16[1552,256]{1,0:T(8,128)(2,1)S(1)}, bf16[1552,256]{1,0:T(8,128)(2,1)S(1)}, u32[]{:S(2)}, u32[]{:S(2)}) collective-permute-start(bf16[1552,256]{1,0:T(8,128)(2,1)S(1)} %collective-permute-done.4.refs_1_.refs_0_), channel_id=1, source_target_pairs={{4,6},{6,4},{12,14},{14,12},{20,22},{22,20},{28,30},{30,28},{5,7},... | collective-permute-start | bytes 2383880 | tf_op jit(solution)/shard_map/ppermute | solution.py:258
  44.9 0.6 collective-permute-start.8
  45.5 1.0 %panel_tile.4 = (f32[8,512]{1,0:T(8,128)S(1)}, s32[264,256]{1,0:T(8,128)S(1)}, f32[256,512]{1,0:T(8,128)S(1)}) custom-call(bf16[512,1536]{1,0:T(8,128)(2,1)S(1)} %get-tuple-element.43.lt, bf16[1552,256]{1,0:T(8,128)(2,1)S(1)} %collective-permute-done.3.refs_0_, bf16[1552,256]{1,0:T(8,128)(2,1)S(1)} %collective-permute-done.4.refs_1_.refs_0_, ...), custom_call_target="tpu_custom_call" | custom-call | flops 1 | bytes 1 | tf_op jit(solution)/shard_map/panel_tile/pallas_call | solution.py:24
  46.5 1.6 %collective-permute-start.9 = (s32[264,256]{1,0:T(8,128)S(1)}, s32[264,256]{1,0:T(8,128)S(1)}, u32[]{:S(2)}, u32[]{:S(2)}) collective-permute-start(s32[264,256]{1,0:T(8,128)S(1)} %get-tuple-element.53), channel_id=1, source_target_pairs={{0,1},{1,0},{2,3},{3,2},{4,5},{5,4},{6,7},{7,6},{8,9},{9,8},{10,11... | collective-permute-start | bytes 811016 | tf_op jit(solution)/shard_map/ppermute | solution.py:270
  48.1 2.3 %finish.3.refs_3_ = f32[256,2048]{1,0:T(8,128)} custom-call(f32[256,128]{1,0:T(8,128)S(1)} %get-tuple-element.33.row_coord, f32[256,128]{1,0:T(8,128)S(1)} %get-tuple-element.34.row_level, f32[8,512]{1,0:T(8,128)S(1)} %maximum_convert_fusion.refs_0_, f32[256,512]{1,0:T(8,128)S(1)} %get-tuple-element.51.refs_1_, f32[256,512]{1,0:T(8,128)S(1)} %collective-permute-done.refs_2_, ...), custom_call_target="tpu_custom_call" | custom-call | flops 1 | bytes 1 | tf_op jit(solution)/shard_map/finish/pallas_call | solution.py:229
  50.4 1.0 %panel_tile.5 = (f32[8,512]{1,0:T(8,128)S(1)}, s32[264,256]{1,0:T(8,128)S(1)}, f32[256,512]{1,0:T(8,128)S(1)}) custom-call(bf16[512,1536]{1,0:T(8,128)(2,1)S(1)} %get-tuple-element.43.lt, bf16[1552,256]{1,0:T(8,128)(2,1)S(1)} %collective-permute-done.4.refs_1_.refs_0_, bf16[1552,256]{1,0:T(8,128)(2,1)S(1)} %collective-permute-done.6.refs_1_, ...), custom_call_target="tpu_custom_call" | custom-call | flops 1 | bytes 1 | tf_op jit(solution)/shard_map/panel_tile/pallas_call | solution.py:24
  51.5 3.6 %collective-permute-done.9.refs_2_ = s32[264,256]{1,0:T(8,128)S(1)} collective-permute-done((s32[264,256]{1,0:T(8,128)S(1)}, s32[264,256]{1,0:T(8,128)S(1)}, u32[]{:S(2)}, u32[]{:S(2)}) %collective-permute-start.9) | collective-permute-done | bytes 270368 | tf_op jit(solution)/shard_map/ppermute | solution.py:270
  55.0 1.5 %collective-permute-start.10 = (s32[264,256]{1,0:T(8,128)S(1)}, s32[264,256]{1,0:T(8,128)S(1)}, u32[]{:S(2)}, u32[]{:S(2)}) collective-permute-start(s32[264,256]{1,0:T(8,128)S(1)} %get-tuple-element.54), channel_id=1, source_target_pairs={{0,1},{1,0},{2,3},{3,2},{4,5},{5,4},{6,7},{7,6},{8,9},{9,8},{10,11... | collective-permute-start | bytes 811016 | tf_op jit(solution)/shard_map/ppermute | solution.py:270
  56.5 1.6 %finish.4.refs_3_ = f32[256,2048]{1,0:T(8,128)} custom-call(f32[256,128]{1,0:T(8,128)S(1)} %get-tuple-element.33.row_coord, f32[256,128]{1,0:T(8,128)S(1)} %get-tuple-element.34.row_level, f32[8,512]{1,0:T(8,128)S(1)} %get-tuple-element.55.refs_0_, f32[256,512]{1,0:T(8,128)S(1)} %get-tuple-element.56.refs_1_, ...), custom_call_target="tpu_custom_call", output_to_operand_aliasing={{}: (5, {})} | custom-call | flops 1 | bytes 1 | tf_op jit(solution)/shard_map/finish/pallas_call | solution.py:229
  58.1 4.5 %collective-permute-done.10.refs_2_ = s32[264,256]{1,0:T(8,128)S(1)} collective-permute-done((s32[264,256]{1,0:T(8,128)S(1)}, s32[264,256]{1,0:T(8,128)S(1)}, u32[]{:S(2)}, u32[]{:S(2)}) %collective-permute-start.10) | collective-permute-done | bytes 270368 | tf_op jit(solution)/shard_map/ppermute | solution.py:270
  62.6 1.6 %finish.5 = f32[256,2048]{1,0:T(8,128)} custom-call(f32[256,128]{1,0:T(8,128)S(1)} %get-tuple-element.33.row_coord, f32[256,128]{1,0:T(8,128)S(1)} %get-tuple-element.34.row_level, f32[8,512]{1,0:T(8,128)S(1)} %get-tuple-element.47.refs_0_, f32[256,512]{1,0:T(8,128)S(1)} %get-tuple-element.48.refs_1_, ...), custom_call_target="tpu_custom_call", output_to_operand_aliasing={{}: (5, {})} | custom-call | flops 1 | bytes 1 | tf_op jit(solution)/shard_map/finish/pallas_call | solution.py:229
  (15 shorter events, 0.6 us)
Async XLA Ops:
  0.0 1.4 %copy-start = (bf16[1536,512]{1,0:T(8,128)(2,1)S(1)}, bf16[1536,512]{1,0:T(8,128)(2,1)}, u32[]{:S(2)}) copy-start(bf16[1536,512]{1,0:T(8,128)(2,1)} %x.2) | copy-start | bytes 4718596
  1.4 0.7 %copy-start.1 = (s32[512]{0:T(512)S(1)}, s32[512]{0:T(512)}, u32[]{:S(2)}) copy-start(s32[512]{0:T(512)} %param.4) | copy-start | bytes 6148
  2.2 19.5 %collective-permute-start.3 = (bf16[1552,256]{1,0:T(8,128)(2,1)S(1)}, bf16[1552,256]{1,0:T(8,128)(2,1)S(1)}, u32[]{:S(2)}, u32[]{:S(2)}) collective-permute-start(bf16[1552,256]{1,0:T(8,128)(2,1)S(1)} %get-tuple-element.31), channel_id=1, source_target_pairs={{0,4},{2,6},{4,0},{6,2},{8,12},{10,14},{12,8},{14,10},{16,20},{18,... | collective-permute-start | bytes 2383880 | tf_op jit(solution)/shard_map/ppermute | solution.py:258
  2.8 19.9 %collective-permute-start.2 = (bf16[1552,256]{1,0:T(8,128)(2,1)S(1)}, bf16[1552,256]{1,0:T(8,128)(2,1)S(1)}, u32[]{:S(2)}, u32[]{:S(2)}) collective-permute-start(bf16[1552,256]{1,0:T(8,128)(2,1)S(1)} %get-tuple-element.41), channel_id=1, source_target_pairs={{0,26},{2,0},{4,30},{6,4},{8,2},{10,8},{12,6},{14,12},{16,10},{18,... | collective-permute-start | bytes 2383880 | tf_op jit(solution)/shard_map/ppermute | solution.py:258
  2.8 19.9 %collective-permute-start.1 = (bf16[1552,256]{1,0:T(8,128)(2,1)S(1)}, bf16[1552,256]{1,0:T(8,128)(2,1)S(1)}, u32[]{:S(2)}, u32[]{:S(2)}) collective-permute-start(bf16[1552,256]{1,0:T(8,128)(2,1)S(1)} %get-tuple-element.31), channel_id=1, source_target_pairs={{0,26},{2,0},{4,30},{6,4},{8,2},{10,8},{12,6},{14,12},{16,10},{18,... | collective-permute-start | bytes 2383880 | tf_op jit(solution)/shard_map/ppermute | solution.py:258
  3.4 0.7 %copy-start.2 = (s32[512]{0:T(512)S(1)}, s32[512]{0:T(512)}, u32[]{:S(2)}) copy-start(s32[512]{0:T(512)} %param.5) | copy-start | bytes 6148
  5.1 17.6 %collective-permute-start = (f32[256,512]{1,0:T(8,128)S(1)}, f32[256,512]{1,0:T(8,128)S(1)}, u32[]{:S(2)}, u32[]{:S(2)}) collective-permute-start(f32[256,512]{1,0:T(8,128)S(1)} %get-tuple-element.36), channel_id=1, source_target_pairs={{0,1},{1,0},{2,3},{3,2},{4,5},{5,4},{6,7},{7,6},{8,9},{9,8},{10,11... | collective-permute-start | bytes 1572872 | tf_op jit(solution)/shard_map/ppermute | solution.py:270
  21.7 21.3 %collective-permute-start.5 = (bf16[1552,256]{1,0:T(8,128)(2,1)S(1)}, bf16[1552,256]{1,0:T(8,128)(2,1)S(1)}, u32[]{:S(2)}, u32[]{:S(2)}) collective-permute-start(bf16[1552,256]{1,0:T(8,128)(2,1)S(1)} %get-tuple-element.41), channel_id=1, source_target_pairs={{0,28},{2,30},{4,0},{6,2},{8,4},{10,6},{12,8},{14,10},{16,12},{18,... | collective-permute-start | bytes 2383880 | tf_op jit(solution)/shard_map/ppermute | solution.py:258
  22.3 20.8 %collective-permute-start.4 = (bf16[1552,256]{1,0:T(8,128)(2,1)S(1)}, bf16[1552,256]{1,0:T(8,128)(2,1)S(1)}, u32[]{:S(2)}, u32[]{:S(2)}) collective-permute-start(bf16[1552,256]{1,0:T(8,128)(2,1)S(1)} %collective-permute-done.3.refs_0_), channel_id=1, source_target_pairs={{0,2},{2,0},{4,28},{6,30},{8,10},{10,8},{12,4},{14,6},{16,18},{18,... | collective-permute-start | bytes 2383880 | tf_op jit(solution)/shard_map/ppermute | solution.py:258
  23.7 9.0 %collective-permute-start.7 = (s32[264,256]{1,0:T(8,128)S(1)}, s32[264,256]{1,0:T(8,128)S(1)}, u32[]{:S(2)}, u32[]{:S(2)}) collective-permute-start(s32[264,256]{1,0:T(8,128)S(1)} %get-tuple-element.44), channel_id=1, source_target_pairs={{0,1},{1,0},{2,3},{3,2},{4,5},{5,4},{6,7},{7,6},{8,9},{9,8},{10,11... | collective-permute-start | bytes 811016 | tf_op jit(solution)/shard_map/ppermute | solution.py:270
  43.0 7.4 %collective-permute-start.6 = (bf16[1552,256]{1,0:T(8,128)(2,1)S(1)}, bf16[1552,256]{1,0:T(8,128)(2,1)S(1)}, u32[]{:S(2)}, u32[]{:S(2)}) collective-permute-start(bf16[1552,256]{1,0:T(8,128)(2,1)S(1)} %collective-permute-done.4.refs_1_.refs_0_), channel_id=1, source_target_pairs={{4,6},{6,4},{12,14},{14,12},{20,22},{22,20},{28,30},{30,28},{5,7},... | collective-permute-start | bytes 2383880 | tf_op jit(solution)/shard_map/ppermute | solution.py:258
  44.9 5.5 %collective-permute-start.8 = (bf16[1552,256]{1,0:T(8,128)(2,1)S(1)}, bf16[1552,256]{1,0:T(8,128)(2,1)S(1)}, u32[]{:S(2)}, u32[]{:S(2)}) collective-permute-start(bf16[1552,256]{1,0:T(8,128)(2,1)S(1)} %collective-permute-done.5.refs_2_), channel_id=1, source_target_pairs={{0,2},{2,0},{4,6},{6,4},{8,10},{10,8},{12,14},{14,12},{16,18},{18,... | collective-permute-start | bytes 2383880 | tf_op jit(solution)/shard_map/ppermute | solution.py:258
  46.5 8.5 %collective-permute-start.9 = (s32[264,256]{1,0:T(8,128)S(1)}, s32[264,256]{1,0:T(8,128)S(1)}, u32[]{:S(2)}, u32[]{:S(2)}) collective-permute-start(s32[264,256]{1,0:T(8,128)S(1)} %get-tuple-element.53), channel_id=1, source_target_pairs={{0,1},{1,0},{2,3},{3,2},{4,5},{5,4},{6,7},{7,6},{8,9},{9,8},{10,11... | collective-permute-start | bytes 811016 | tf_op jit(solution)/shard_map/ppermute | solution.py:270
  55.0 7.6 %collective-permute-start.10 = (s32[264,256]{1,0:T(8,128)S(1)}, s32[264,256]{1,0:T(8,128)S(1)}, u32[]{:S(2)}, u32[]{:S(2)}) collective-permute-start(s32[264,256]{1,0:T(8,128)S(1)} %get-tuple-element.54), channel_id=1, source_target_pairs={{0,1},{1,0},{2,3},{3,2},{4,5},{5,4},{6,7},{7,6},{8,9},{9,8},{10,11... | collective-permute-start | bytes 811016 | tf_op jit(solution)/shard_map/ppermute | solution.py:270

commit v5 on v4

--- a/solution.py
+++ b/solution.py
@@ -39,29 +39,40 @@
     return jnp.where(r <= 1.0, near, jnp.where(r <= 2.0, far, 0.0))
 
 
-def prepare_kernel(x, coord, low, high):
+def prepare_kernel(x, coord, high):
     members, width = x.shape
+    half = width // 2
     first = 4 * width * lax.axis_index("mesh")
     jitter = coord[...] - first - 4 * lax.broadcasted_iota(jnp.int32, (1, width), 1)
-    pad = jnp.broadcast_to(jitter.astype(F32), (PAD, width)).astype(x.dtype)
+    jitter = jitter.astype(F32)
+    high[:members, :] = x[:, half:]
+    high[members:, :] = jnp.concatenate(
+        [jnp.broadcast_to(jitter[:, :half], (PAD // 2, half)), jnp.broadcast_to(jitter[:, half:], (PAD // 2, half))],
+        axis=0,
+    ).astype(x.dtype)
+
+
+def prepare(x, coord):
+    members, width = x.shape
+    half = jax.ShapeDtypeStruct((members + PAD, width // 2), x.dtype)
+    return call(prepare_kernel, [half], x, coord, name="prepare")[0]
+
+
+def own_kernel(low, high, coord, level, lt, row_coord, row_level, *outs, owned, split):
+    width, members = lt.shape
+    groups = width // owned
     half = width // 2
-    for part, span in ((low, slice(0, half)), (high, slice(half, width))):
-        part[:members, :] = x[:, span]
-        part[members:, :] = pad[:, span]
-
-
-def own_kernel(x, coord, level, lt, row_coord, row_level, *outs, owned, split):
-    members, width = x.shape
-    groups = width // owned
     mem = lax.axis_index("mem")
-    for part in range(groups):
+    for at, part in ((0, low), (half, high)):
+        columns = part[:members, :].T
         if split:
-            start = pl.multiple_of(lax.rem(mem + 1 + part, groups) * owned, owned)
+            begin = lax.rem(mem + 1 + at // half, 2) * half
+            lt[pl.ds(pl.multiple_of(begin, half), half), :] = columns
         else:
-            start = part * owned
-        lt[part * owned : (part + 1) * owned, :] = x[:, pl.ds(start, owned)].T
-    tile = jnp.dot(lt[...], x[...], preferred_element_type=F32)
-    store_rows(tile, outs, 0)
+            lt[at : at + half, :] = columns
+    for at, part in ((0, low), (half, high)):
+        tile = jnp.dot(lt[...], part[:members, :], preferred_element_type=F32)
+        store_rows(tile, outs, at)
     rows = jnp.concatenate(
         [jnp.broadcast_to(coord[...], (CHUNK, width)), jnp.broadcast_to(level[...], (CHUNK, width))], axis=0
     )
@@ -82,14 +93,15 @@
         first += out.shape[0]
 
 
-def own_tile(x, coord, level, owned, rows):
-    members, width = x.shape
+def own_tile(low, high, coord, level, owned, rows):
+    members, width = low.shape[0], 2 * low.shape[1]
     return call(
         functools.partial(own_kernel, owned=owned, split=len(rows) > 1),
-        [jax.ShapeDtypeStruct((width, members), x.dtype)]
+        [jax.ShapeDtypeStruct((width, members), low.dtype)]
         + [jax.ShapeDtypeStruct((owned, CHUNK), F32)] * 2
         + [jax.ShapeDtypeStruct((r, width), F32) for r in rows],
-        x,
+        low,
+        high,
         coord,
         level,
         name="own_tile",
@@ -127,17 +139,22 @@
     return widened((words << 16) >> 16, packed[rows + 4 : rows + 5, span])
 
 
-def panel_kernel(lt, *refs, picks, count, rows):
+def panel_kernel(lt, *refs, picks, count, rows, keep):
     panels, cols, outs = refs[:count], refs[count], refs[count + 1 :]
     members = lt.shape[1]
 
     def run(which):
         chosen = [panels[i] for i in which]
-        at = 0
-        for panel in chosen:
-            wide = panel.shape[1]
-            cols[:, at : at + wide] = panel[members:, :].astype(F32)[:8]
-            at += wide
+        half = cols.shape[1] // 2
+        pad = [chosen[-1][members:, :].astype(F32)] * 2
+        if len(chosen) == 1:
+            pad = [pad[0][:, :half], pad[0][:, half:]]
+        cols[:, :half] = pad[0][: PAD // 2]
+        cols[:, half:] = pad[1][PAD // 2 :]
+        if keep:
+            for at, panel in zip((0, half), chosen):
+                outs[-1][:members, at : at + half] = panel[:members, :]
+                outs[-1][members:, at : at + half] = chosen[-1][members:, :]
         block = jnp.concatenate([panel[:members, :] for panel in chosen], axis=1)
         tile = jnp.dot(lt[...], block, preferred_element_type=F32)
         if len(rows) > 1:
@@ -154,14 +171,15 @@
             pl.when(cross == value)(functools.partial(run, which))
 
 
-def panel_tile(lt, panels, picks, rows):
+def panel_tile(lt, panels, picks, rows, keep=False):
     wide = sum(panels[i].shape[1] for i in picks[0])
     width, members = lt.shape
     return call(
-        functools.partial(panel_kernel, picks=picks, count=len(panels), rows=rows),
+        functools.partial(panel_kernel, picks=picks, count=len(panels), rows=rows, keep=keep),
         [jax.ShapeDtypeStruct((8, wide), F32)]
         + ([jax.ShapeDtypeStruct((rows[0] + 8, wide // 2), jnp.int32)] if len(rows) > 1 else [])
-        + [jax.ShapeDtypeStruct((rows[-1], wide), F32)],
+        + [jax.ShapeDtypeStruct((rows[-1], wide), F32)]
+        + ([jax.ShapeDtypeStruct((members + PAD, wide), lt.dtype)] if keep else []),
         lt,
         *panels,
         name="panel_tile",
@@ -259,8 +277,7 @@
 
     everywhere = range(count)
     swap_x = [(p, p ^ 2) for p in everywhere]
-    relay = [(p, (p - 4) % count) if p % 4 >= 2 else (p, p ^ 1) for p in everywhere]
-    far_siblings = [(p, p ^ 1) for p in everywhere if p % 4 >= 2]
+    relay = [(p, (p - 4) % count) for p in everywhere if p % 4 >= 2]
     back_two = [(p, (p - 2) % count) for p in everywhere]
     siblings = [(p, p ^ 1) for p in everywhere]
     extra_pairs = [(p, p - 1) if p % 2 else (p, (p - 3) % count) for p in everywhere]
@@ -271,24 +288,19 @@
         return [lax.psum_scatter(parts[0], "mem", scatter_dimension=0, tiled=True)]
 
     half = width // 2
-    low, high = call(
-        prepare_kernel,
-        [jax.ShapeDtypeStruct((members + PAD, half), perturbations.dtype)] * 2,
-        perturbations,
-        coord,
-        name="prepare",
-    )
-    lt, row_coord, row_level, *own = own_tile(after(perturbations, low), coord, levels, owned, rows)
+    low = perturbations[:, :half]
+    high = prepare(after(perturbations, low), coord)
+    lt, row_coord, row_level, *own = own_tile(low, high, coord, levels, owned, rows)
     own_parts = reduced(own)
-    own_cols = jnp.concatenate([low[members : members + 8], high[members : members + 8]], axis=1).astype(F32)
+    own_cols = jnp.concatenate([high[members : members + PAD // 2], high[members + PAD // 2 :]], axis=1).astype(F32)
 
     first = permute(low, swap_x)
     extra = [permute(a, extra_pairs) for a in (low, high)]
     straight = permute(after(high, first), back_two)
     passed = permute(first, relay)
 
-    def tile(panels, picks, *tokens):
-        return panel_tile(after(lt, *tokens), panels, picks, rows)
+    def tile(panels, picks, *tokens, keep=False):
+        return panel_tile(after(lt, *tokens), panels, picks, rows, keep)
 
     def finished(out, token, *groups):
         groups = [(after(groups[0][0], token), *groups[0][1:])] + list(groups[1:])
@@ -296,18 +308,16 @@
 
     extra_cols, *extra_parts = tile(extra, [[0, 1]], own_parts[-1])
     extra_parts = reduced(extra_parts)
-    other = permute(after(straight, extra_parts[-1]), siblings)
-    far = permute(passed, far_siblings)
-    two_cols, *two_parts = tile([first, passed, straight], [[0, 2], [1, 2]], extra_cols)
-    two_parts = reduced(two_parts)
     out = finished(
         None,
-        two_cols,
+        extra_cols,
         (own_cols, own_parts, [(0, width, "own", 0)]),
         (extra_cols, extra_parts, [(0, width, "extra", 0)]),
     )
-    other_cols, *other_parts = tile([passed, far, other], [[0, 2], [1, 2]], two_cols)
-    other_parts[0] = after(other_parts[0], out, two_parts[-1])
+    two_cols, *two_parts, two = tile([first, passed, straight], [[0, 2], [1, 2]], out, keep=True)
+    two_parts = reduced(two_parts)
+    other = permute(two, siblings)
+    other_cols, *other_parts = tile([other], [[0]])
     other_parts = reduced(other_parts)
     out = finished(out, other_cols, (two_cols, two_parts, [(0, width, "two", 0)]))
     return finished(out, other_cols, (other_cols, other_parts, [(0, width, "other", 0)]))

time: 64.4 us -> 60.6 us (0.941)
  waiting for transfers between devices: 40.7 us -> 37.9 us
  local copies, waits for them, and re-layouts: 2.77 us -> 1.99 us
    unnamed x6, local copies, waits for them, and re-layouts: 2.77 us -> 0.69 us
    ppermute x7 -> x6, waiting for transfers between devices: 25.2 us -> 23.5 us  [permute(): return lax.ppermute(array, 'mesh', pairs)]
    slice x2, local copies, waits for them, and re-layouts: 0.01 us -> 1.3 us  [the longest x1 1.3 us: per_device(): low = perturbations[:, :half]]
    ppermute x4, waiting for transfers between devices: 15.5 us -> 14.4 us  [reduced(): return [parts[1], lax.ppermute(parts[0], 'mem', [(0, 1), (1, 0)])]]
    ppermute x7 -> x6, starting transfers between devices: 4.62 us -> 4.16 us  [permute(): return lax.ppermute(array, 'mesh', pairs)]
  transfers between devices with their start and end apart: 11 -> 10, of which waited for: 5 -> 6; matrix products, arithmetic and copies ran while one was open for 0% -> 0% of each run, Pallas kernels for 12% -> 12%
where the time goes in v5:
time: 60.6 us; the launch traced here: 60.5 us
  waiting for transfers between devices  37.9 us (63%)
  starting transfers between devices  10.6 us (17%)
  Pallas kernels  9.88 us (16%)
  local copies, waits for them, and re-layouts  1.99 us (3%)
    ppermute x6, waiting for transfers between devices, permute(): return lax.ppermute(array, 'mesh', pairs)  23.5 us
    ppermute x4, waiting for transfers between devices, reduced(): return [parts[1], lax.ppermute(parts[0], 'mem', [(0, 1), (1, 0)])]  14.4 us
    ppermute x4, starting transfers between devices, reduced(): return [parts[1], lax.ppermute(parts[0], 'mem', [(0, 1), (1, 0)])]  6.4 us
    pallas_call x3, Pallas kernels, finish(): pl.pallas_call(functools.partial(finish_kernel, plan=plan, period=period,...  5.41 us
    pallas_call x5, Pallas kernels, call(): pl.pallas_call(kernel, out_shape=outs, in_specs=[VMEM] * len(operands), o...  4.47 us
    ppermute x6, starting transfers between devices, permute(): return lax.ppermute(array, 'mesh', pairs)  4.16 us
    slice x1, local copies, waits for them, and re-layouts, per_device(): low = perturbations[:, :half]  1.3 us
  transfers between devices with their start and end apart: 10, of which 6 were waited for; matrix products, arithmetic and copies ran while one was open for 0% of the time, Pallas kernels for 12%

profile of v5, /device:TPU:26, one launch (start us, length us, event | category | flops | bytes accessed | tf_op | source)
XLA Modules:
  0.0 60.5 jit_solution(13472010780454861850)
XLA Ops:
  0.0 1.3 %slice.9.low = bf16[1536,256]{1,0:T(8,128)(2,1)S(1)} slice(bf16[1536,512]{1,0:T(8,128)(2,1)} %x), slice={[0:1536], [0:256]} | slice | bytes 1572864 | tf_op jit(solution)/shard_map/slice | solution.py:291
  1.3 0.6 collective-permute-start.4
  1.9 0.7 %copy-done.1 = s32[512]{0:T(512)S(1)} copy-done((s32[512]{0:T(512)S(1)}, s32[512]{0:T(512)}, u32[]{:S(2)}) %copy-start.1) | copy-done | bytes 2072
  2.7 0.6 collective-permute-start.1
  3.3 1.2 %own_tile.1 = (bf16[512,1536]{1,0:T(8,128)(2,1)S(1)}, f32[256,128]{1,0:T(8,128)S(1)}, f32[256,128]{1,0:T(8,128)S(1)}, f32[256,512]{1,0:T(8,128)S(1)}, f32[256,512]{1,0:T(8,128)S(1)}) custom-call(bf16[1536,256]{1,0:T(8,128)(2,1)S(1)} %slice.9.low, bf16[1552,256]{1,0:T(8,128)(2,1)S(1)} %prepare.1.high, s32[1,512]{1,0:T(1,128)S(1)} %bitcast.3, s32[1,512]{1,0:T(1,128)S(1)} %bitcast.4), custom_call_target="tpu_custom_call" | custom-call | flops 1 | bytes 1 | tf_op jit(solution)/shard_map/own_tile/pallas_call | solution.py:24
  4.5 1.6 %collective-permute-start = (f32[256,512]{1,0:T(8,128)S(1)}, f32[256,512]{1,0:T(8,128)S(1)}, u32[]{:S(2)}, u32[]{:S(2)}) collective-permute-start(f32[256,512]{1,0:T(8,128)S(1)} %get-tuple-element.31), channel_id=1, source_target_pairs={{0,1},{1,0},{2,3},{3,2},{4,5},{5,4},{6,7},{7,6},{8,9},{9,8},{10,11... | collective-permute-start | bytes 1572872 | tf_op jit(solution)/shard_map/ppermute | solution.py:287
  6.2 14.5 %collective-permute-done.4.refs_0_ = bf16[1536,256]{1,0:T(8,128)(2,1)S(1)} collective-permute-done((bf16[1536,256]{1,0:T(8,128)(2,1)S(1)}, bf16[1536,256]{1,0:T(8,128)(2,1)S(1)}, u32[]{:S(2)}, u32[]{:S(2)}) %collective-permute-start.4) | collective-permute-done | bytes 786464 | tf_op jit(solution)/shard_map/ppermute | solution.py:276
  20.7 0.5 collective-permute-start.6
  21.2 2.3 %collective-permute-start.5 = (bf16[1536,256]{1,0:T(8,128)(2,1)S(1)}, bf16[1536,256]{1,0:T(8,128)(2,1)S(1)}, u32[]{:S(2)}, u32[]{:S(2)}) collective-permute-start(bf16[1536,256]{1,0:T(8,128)(2,1)S(1)} %collective-permute-done.4.refs_0_), channel_id=1, source_target_pairs={{4,28},{6,30},{12,4},{14,6},{20,12},{22,14},{28,20},{30,22},{5,29}... | collective-permute-start | bytes 2359304 | tf_op jit(solution)/shard_map/ppermute | solution.py:276
  23.6 1.0 %panel_tile.3 = (f32[8,512]{1,0:T(8,128)S(1)}, s32[264,256]{1,0:T(8,128)S(1)}, f32[256,512]{1,0:T(8,128)S(1)}) custom-call(bf16[512,1536]{1,0:T(8,128)(2,1)S(1)} %get-tuple-element.38.lt, bf16[1536,256]{1,0:T(8,128)(2,1)S(1)} %collective-permute-done.1.refs_0_, bf16[1552,256]{1,0:T(8,128)(2,1)S(1)} %collective-permute-done.2.refs_1_), custom_call_target="tpu_custom_call" | custom-call | flops 1 | bytes 1 | tf_op jit(solution)/shard_map/panel_tile/pallas_call | solution.py:24
  24.6 1.6 %collective-permute-start.3 = (s32[264,256]{1,0:T(8,128)S(1)}, s32[264,256]{1,0:T(8,128)S(1)}, u32[]{:S(2)}, u32[]{:S(2)}) collective-permute-start(s32[264,256]{1,0:T(8,128)S(1)} %get-tuple-element.37), channel_id=1, source_target_pairs={{0,1},{1,0},{2,3},{3,2},{4,5},{5,4},{6,7},{7,6},{8,9},{9,8},{10,11... | collective-permute-start | bytes 811016 | tf_op jit(solution)/shard_map/ppermute | solution.py:287
  26.2 7.3 %collective-permute-done.3.refs_5_ = s32[264,256]{1,0:T(8,128)S(1)} collective-permute-done((s32[264,256]{1,0:T(8,128)S(1)}, s32[264,256]{1,0:T(8,128)S(1)}, u32[]{:S(2)}, u32[]{:S(2)}) %collective-permute-start.3) | collective-permute-done | bytes 270368 | tf_op jit(solution)/shard_map/ppermute | solution.py:287
  33.5 2.3 %finish.3.refs_3_ = f32[256,2048]{1,0:T(8,128)} custom-call(f32[256,128]{1,0:T(8,128)S(1)} %get-tuple-element.28.row_coord, f32[256,128]{1,0:T(8,128)S(1)} %get-tuple-element.29.row_level, f32[8,512]{1,0:T(8,128)S(1)} %maximum_convert_fusion.refs_0_, f32[256,512]{1,0:T(8,128)S(1)} %get-tuple-element.35.refs_1_, f32[256,512]{1,0:T(8,128)S(1)} %collective-permute-done.refs_2_, ...), custom_call_target="tpu_custom_call" | custom-call | flops 1 | bytes 1 | tf_op jit(solution)/shard_map/finish/pallas_call | solution.py:247
  35.8 7.2 %collective-permute-done.5.refs_1_ = bf16[1536,256]{1,0:T(8,128)(2,1)S(1)} collective-permute-done((bf16[1536,256]{1,0:T(8,128)(2,1)S(1)}, bf16[1536,256]{1,0:T(8,128)(2,1)S(1)}, u32[]{:S(2)}, u32[]{:S(2)}) %collective-permute-start.5) | collective-permute-done | bytes 786464 | tf_op jit(solution)/shard_map/ppermute | solution.py:276
  43.0 1.1 %panel_tile.4 = (f32[8,512]{1,0:T(8,128)S(1)}, s32[264,256]{1,0:T(8,128)S(1)}, f32[256,512]{1,0:T(8,128)S(1)}, bf16[1552,512]{1,0:T(8,128)(2,1)S(1)}) custom-call(bf16[512,1536]{1,0:T(8,128)(2,1)S(1)} %get-tuple-element.38.lt, bf16[1536,256]{1,0:T(8,128)(2,1)S(1)} %collective-permute-done.4.refs_0_, bf16[1536,256]{1,0:T(8,128)(2,1)S(1)} %collective-permute-done.5.refs_1_, ...), custom_call_target="tpu_custom_call" | custom-call | flops 1 | bytes 1 | tf_op jit(solution)/shard_map/panel_tile/pallas_call | solution.py:24
  44.1 0.1 collective-permute-start.7
  44.2 1.6 %collective-permute-start.9 = (s32[264,256]{1,0:T(8,128)S(1)}, s32[264,256]{1,0:T(8,128)S(1)}, u32[]{:S(2)}, u32[]{:S(2)}) collective-permute-start(s32[264,256]{1,0:T(8,128)S(1)} %get-tuple-element.48), channel_id=1, source_target_pairs={{0,1},{1,0},{2,3},{3,2},{4,5},{5,4},{6,7},{7,6},{8,9},{9,8},{10,11... | collective-permute-start | bytes 811016 | tf_op jit(solution)/shard_map/ppermute | solution.py:287
  45.8 1.8 %collective-permute-done.7.refs_0_ = bf16[1552,512]{1,0:T(8,128)(2,1)S(1)} collective-permute-done((bf16[1552,512]{1,0:T(8,128)(2,1)S(1)}, bf16[1552,512]{1,0:T(8,128)(2,1)S(1)}, u32[]{:S(2)}, u32[]{:S(2)}) %collective-permute-start.7) | collective-permute-done | bytes 1589280 | tf_op jit(solution)/shard_map/ppermute | solution.py:276
  47.6 1.0 %panel_tile.5 = (f32[8,512]{1,0:T(8,128)S(1)}, s32[264,256]{1,0:T(8,128)S(1)}, f32[256,512]{1,0:T(8,128)S(1)}) custom-call(bf16[512,1536]{1,0:T(8,128)(2,1)S(1)} %get-tuple-element.38.lt, bf16[1552,512]{1,0:T(8,128)(2,1)S(1)} %collective-permute-done.7.refs_0_), custom_call_target="tpu_custom_call" | custom-call | flops 1 | bytes 1 | tf_op jit(solution)/shard_map/panel_tile/pallas_call | solution.py:24
  48.6 1.6 %collective-permute-start.8 = (s32[264,256]{1,0:T(8,128)S(1)}, s32[264,256]{1,0:T(8,128)S(1)}, u32[]{:S(2)}, u32[]{:S(2)}) collective-permute-start(s32[264,256]{1,0:T(8,128)S(1)} %get-tuple-element.44), channel_id=1, source_target_pairs={{0,1},{1,0},{2,3},{3,2},{4,5},{5,4},{6,7},{7,6},{8,9},{9,8},{10,11... | collective-permute-start | bytes 811016 | tf_op jit(solution)/shard_map/ppermute | solution.py:287
  50.2 3.3 %collective-permute-done.9.refs_2_ = s32[264,256]{1,0:T(8,128)S(1)} collective-permute-done((s32[264,256]{1,0:T(8,128)S(1)}, s32[264,256]{1,0:T(8,128)S(1)}, u32[]{:S(2)}, u32[]{:S(2)}) %collective-permute-start.9) | collective-permute-done | bytes 270368 | tf_op jit(solution)/shard_map/ppermute | solution.py:287
  53.6 1.6 %finish.4.refs_3_ = f32[256,2048]{1,0:T(8,128)} custom-call(f32[256,128]{1,0:T(8,128)S(1)} %get-tuple-element.28.row_coord, f32[256,128]{1,0:T(8,128)S(1)} %get-tuple-element.29.row_level, f32[8,512]{1,0:T(8,128)S(1)} %get-tuple-element.46.refs_0_, f32[256,512]{1,0:T(8,128)S(1)} %get-tuple-element.47.refs_1_, ...), custom_call_target="tpu_custom_call", output_to_operand_aliasing={{}: (5, {})} | custom-call | flops 1 | bytes 1 | tf_op jit(solution)/shard_map/finish/pallas_call | solution.py:247
  55.1 3.8 %collective-permute-done.8.refs_2_ = s32[264,256]{1,0:T(8,128)S(1)} collective-permute-done((s32[264,256]{1,0:T(8,128)S(1)}, s32[264,256]{1,0:T(8,128)S(1)}, u32[]{:S(2)}, u32[]{:S(2)}) %collective-permute-start.8) | collective-permute-done | bytes 270368 | tf_op jit(solution)/shard_map/ppermute | solution.py:287
  58.9 1.6 %finish.5 = f32[256,2048]{1,0:T(8,128)} custom-call(f32[256,128]{1,0:T(8,128)S(1)} %get-tuple-element.28.row_coord, f32[256,128]{1,0:T(8,128)S(1)} %get-tuple-element.29.row_level, f32[8,512]{1,0:T(8,128)S(1)} %get-tuple-element.42.refs_0_, f32[256,512]{1,0:T(8,128)S(1)} %get-tuple-element.43.refs_1_, ...), custom_call_target="tpu_custom_call", output_to_operand_aliasing={{}: (5, {})} | custom-call | flops 1 | bytes 1 | tf_op jit(solution)/shard_map/finish/pallas_call | solution.py:247
  (13 shorter events, 0.1 us)
Async XLA Ops:
  0.0 1.9 %copy-start = (bf16[1536,512]{1,0:T(8,128)(2,1)S(1)}, bf16[1536,512]{1,0:T(8,128)(2,1)}, u32[]{:S(2)}) copy-start(bf16[1536,512]{1,0:T(8,128)(2,1)} %x) | copy-start | bytes 4718596
  1.3 19.3 %collective-permute-start.4 = (bf16[1536,256]{1,0:T(8,128)(2,1)S(1)}, bf16[1536,256]{1,0:T(8,128)(2,1)S(1)}, u32[]{:S(2)}, u32[]{:S(2)}) collective-permute-start(bf16[1536,256]{1,0:T(8,128)(2,1)S(1)} %slice.9.low), channel_id=1, source_target_pairs={{0,4},{2,6},{4,0},{6,2},{8,12},{10,14},{12,8},{14,10},{16,20},{18,... | collective-permute-start | bytes 2359304 | tf_op jit(solution)/shard_map/ppermute | solution.py:276
  1.9 0.7 %copy-start.1 = (s32[512]{0:T(512)S(1)}, s32[512]{0:T(512)}, u32[]{:S(2)}) copy-start(s32[512]{0:T(512)} %param.4) | copy-start | bytes 6148
  2.6 0.7 %copy-start.2 = (s32[512]{0:T(512)S(1)}, s32[512]{0:T(512)}, u32[]{:S(2)}) copy-start(s32[512]{0:T(512)} %param.5) | copy-start | bytes 6148
  2.7 20.9 %collective-permute-start.2 = (bf16[1552,256]{1,0:T(8,128)(2,1)S(1)}, bf16[1552,256]{1,0:T(8,128)(2,1)S(1)}, u32[]{:S(2)}, u32[]{:S(2)}) collective-permute-start(bf16[1552,256]{1,0:T(8,128)(2,1)S(1)} %prepare.1.high), channel_id=1, source_target_pairs={{0,26},{2,0},{4,30},{6,4},{8,2},{10,8},{12,6},{14,12},{16,10},{18,... | collective-permute-start | bytes 2383880 | tf_op jit(solution)/shard_map/ppermute | solution.py:276
  2.7 20.8 %collective-permute-start.1 = (bf16[1536,256]{1,0:T(8,128)(2,1)S(1)}, bf16[1536,256]{1,0:T(8,128)(2,1)S(1)}, u32[]{:S(2)}, u32[]{:S(2)}) collective-permute-start(bf16[1536,256]{1,0:T(8,128)(2,1)S(1)} %slice.9.low), channel_id=1, source_target_pairs={{0,26},{2,0},{4,30},{6,4},{8,2},{10,8},{12,6},{14,12},{16,10},{18,... | collective-permute-start | bytes 2359304 | tf_op jit(solution)/shard_map/ppermute | solution.py:276
  4.5 19.0 %collective-permute-start = (f32[256,512]{1,0:T(8,128)S(1)}, f32[256,512]{1,0:T(8,128)S(1)}, u32[]{:S(2)}, u32[]{:S(2)}) collective-permute-start(f32[256,512]{1,0:T(8,128)S(1)} %get-tuple-element.31), channel_id=1, source_target_pairs={{0,1},{1,0},{2,3},{3,2},{4,5},{5,4},{6,7},{7,6},{8,9},{9,8},{10,11... | collective-permute-start | bytes 1572872 | tf_op jit(solution)/shard_map/ppermute | solution.py:287
  20.7 22.3 %collective-permute-start.6 = (bf16[1552,256]{1,0:T(8,128)(2,1)S(1)}, bf16[1552,256]{1,0:T(8,128)(2,1)S(1)}, u32[]{:S(2)}, u32[]{:S(2)}) collective-permute-start(bf16[1552,256]{1,0:T(8,128)(2,1)S(1)} %prepare.1.high), channel_id=1, source_target_pairs={{0,28},{2,30},{4,0},{6,2},{8,4},{10,6},{12,8},{14,10},{16,12},{18,... | collective-permute-start | bytes 2383880 | tf_op jit(solution)/shard_map/ppermute | solution.py:276
  21.2 21.8 %collective-permute-start.5 = (bf16[1536,256]{1,0:T(8,128)(2,1)S(1)}, bf16[1536,256]{1,0:T(8,128)(2,1)S(1)}, u32[]{:S(2)}, u32[]{:S(2)}) collective-permute-start(bf16[1536,256]{1,0:T(8,128)(2,1)S(1)} %collective-permute-done.4.refs_0_), channel_id=1, source_target_pairs={{4,28},{6,30},{12,4},{14,6},{20,12},{22,14},{28,20},{30,22},{5,29}... | collective-permute-start | bytes 2359304 | tf_op jit(solution)/shard_map/ppermute | solution.py:276
  24.6 8.9 %collective-permute-start.3 = (s32[264,256]{1,0:T(8,128)S(1)}, s32[264,256]{1,0:T(8,128)S(1)}, u32[]{:S(2)}, u32[]{:S(2)}) collective-permute-start(s32[264,256]{1,0:T(8,128)S(1)} %get-tuple-element.37), channel_id=1, source_target_pairs={{0,1},{1,0},{2,3},{3,2},{4,5},{5,4},{6,7},{7,6},{8,9},{9,8},{10,11... | collective-permute-start | bytes 811016 | tf_op jit(solution)/shard_map/ppermute | solution.py:287
  44.1 3.5 %collective-permute-start.7 = (bf16[1552,512]{1,0:T(8,128)(2,1)S(1)}, bf16[1552,512]{1,0:T(8,128)(2,1)S(1)}, u32[]{:S(2)}, u32[]{:S(2)}) collective-permute-start(bf16[1552,512]{1,0:T(8,128)(2,1)S(1)} %get-tuple-element.40), channel_id=1, source_target_pairs={{0,2},{2,0},{4,6},{6,4},{8,10},{10,8},{12,14},{14,12},{16,18},{18,... | collective-permute-start | bytes 4767752 | tf_op jit(solution)/shard_map/ppermute | solution.py:276
  44.2 9.3 %collective-permute-start.9 = (s32[264,256]{1,0:T(8,128)S(1)}, s32[264,256]{1,0:T(8,128)S(1)}, u32[]{:S(2)}, u32[]{:S(2)}) collective-permute-start(s32[264,256]{1,0:T(8,128)S(1)} %get-tuple-element.48), channel_id=1, source_target_pairs={{0,1},{1,0},{2,3},{3,2},{4,5},{5,4},{6,7},{7,6},{8,9},{9,8},{10,11... | collective-permute-start | bytes 811016 | tf_op jit(solution)/shard_map/ppermute | solution.py:287
  48.6 10.2 %collective-permute-start.8 = (s32[264,256]{1,0:T(8,128)S(1)}, s32[264,256]{1,0:T(8,128)S(1)}, u32[]{:S(2)}, u32[]{:S(2)}) collective-permute-start(s32[264,256]{1,0:T(8,128)S(1)} %get-tuple-element.44), channel_id=1, source_target_pairs={{0,1},{1,0},{2,3},{3,2},{4,5},{5,4},{6,7},{7,6},{8,9},{9,8},{10,11... | collective-permute-start | bytes 811016 | tf_op jit(solution)/shard_map/ppermute | solution.py:287

commit v6 on v5

--- a/solution.py
+++ b/solution.py
@@ -187,42 +187,54 @@
     )
 
 
-def finish_kernel(row_coord, row_level, *refs, plan, period, width, members, first):
-    operands = sum(1 + n for n, _ in plan)
+def panel_steps():
+    odd = lax.rem(lax.axis_index("mesh"), 2)
+    return {"own": 0, "two": 2, "extra": 1 + 2 * odd, "other": 3 - 2 * odd}
+
+
+def weight(offsets, row_coord, step, first, period, width, members):
+    panel = lax.rem(lax.axis_index("mesh") + step, lax.axis_size("mesh"))
+    base = (4 * (panel * width + first)).astype(F32)
+    place = 4 * lax.broadcasted_iota(jnp.int32, (1, CHUNK), 1)
+    gap = jnp.abs(offsets + (base + place.astype(F32)) - row_coord)
+    dist = jnp.minimum(gap, period - gap)
+    return gc_taper(dist * (1.0 / (12 * width))) * (1.0 / (members - 1))
+
+
+def weigh_kernel(row_coord, cols, out, *, kind, period, width, members):
+    step = panel_steps()[kind]
+    for at in range(0, out.shape[1], CHUNK):
+        span = slice(at, at + CHUNK)
+        out[:, span] = weight(cols[0:1, span], row_coord[...], step, at, period, width, members)
+
+
+def finish_kernel(row_coord, row_level, *refs, plan, period, width, members):
     out, scratch, sems = refs[-3], refs[-2], refs[-1]
-    me = lax.axis_index("mesh")
-    count = lax.axis_size("mesh")
-    odd = lax.rem(me, 2)
+    steps = panel_steps()
     coord, level = row_coord[...], row_level[...]
-    steps = {"own": 0, "two": 2, "extra": 1 + 2 * odd, "other": 3 - 2 * odd}
     copies = []
-    at, slot = 0, 0
-    for n, spans in plan:
+    at = 0
+    for n, kind in plan:
         cols, parts = refs[at], refs[at + 1 : at + 1 + n]
         at += 1 + n
-        for offset, wide, kind, inside in spans:
-            step = steps[kind]
-            base = (4 * (lax.rem(me + step, count) * width + inside)).astype(F32)
-            for piece in range(0, wide, CHUNK):
-                span = slice(offset + piece, offset + piece + CHUNK)
-                raw = parts[0][:, span]
-                for part in parts[1:]:
-                    if part.dtype == jnp.int32:
-                        raw = raw + unpack(part, span.start // CHUNK, raw.shape[0])
-                    else:
-                        raw = raw + part[:, span]
-                place = 4 * (piece + lax.broadcasted_iota(jnp.int32, (1, CHUNK), 1))
-                column = cols[0:1, span] + (base + place.astype(F32))
-                gap = jnp.abs(column - coord)
-                dist = jnp.minimum(gap, period - gap)
-                c = gc_taper(dist * (1.0 / (12 * width))) * (raw * (1.0 / (members - 1)))
-                scratch[:, slot * CHUNK : (slot + 1) * CHUNK] = c - jnp.clip(c, -level, level)
-                slot += 1
-            begin = (slot * CHUNK) - wide
-            target = pl.multiple_of(step * width + inside, CHUNK)
-            copy = pltpu.make_async_copy(
-                scratch.at[:, begin : begin + wide], out.at[:, pl.ds(target, wide)], sems.at[len(copies)]
-            )
+        step = steps[kind]
+        for begin in range(0, width, CHUNK):
+            span = slice(begin, begin + CHUNK)
+            slot = len(copies)
+            raw = parts[0][:, span]
+            for part in parts[1:]:
+                if part.dtype == jnp.int32:
+                    raw = raw + unpack(part, begin // CHUNK, raw.shape[0])
+                else:
+                    raw = raw + part[:, span]
+            if cols.shape[0] == out.shape[0]:
+                scale = cols[:, span]
+            else:
+                scale = weight(cols[0:1, span], coord, step, begin, period, width, members)
+            c = scale * raw
+            scratch[slot] = c - jnp.clip(c, -level, level)
+            target = pl.multiple_of(step * width + begin, CHUNK)
+            copy = pltpu.make_async_copy(scratch.at[slot], out.at[:, pl.ds(target, CHUNK)], sems.at[slot])
             copy.start()
             copies.append(copy)
     for copy in copies:
@@ -231,27 +243,23 @@
 
 def finish(row_coord, row_level, groups, out, shape, period, width, members):
     operands = [row_coord, row_level]
-    plan, wide, copies = [], 0, 0
-    for cols, parts, spans in groups:
+    plan = []
+    for cols, parts, kind in groups:
         operands += [cols, *parts]
-        plan.append((len(parts), spans))
-        wide += sum(s[1] for s in spans)
-        copies += len(spans)
+        plan.append((len(parts), kind))
+    copies = len(plan) * (width // CHUNK)
     specs = [VMEM] * len(operands)
     aliases = {}
     if out is not None:
         aliases = {len(operands): 0}
         operands.append(out)
         specs.append(pl.BlockSpec(memory_space=pl.ANY))
-    owned = shape[0]
     return pl.pallas_call(
-        functools.partial(
-            finish_kernel, plan=plan, period=period, width=width, members=members, first=out is None
-        ),
+        functools.partial(finish_kernel, plan=plan, period=period, width=width, members=members),
         out_shape=jax.ShapeDtypeStruct(shape, F32),
         in_specs=specs,
         out_specs=pl.BlockSpec(memory_space=pl.ANY),
-        scratch_shapes=[pltpu.VMEM((owned, wide), F32), pltpu.SemaphoreType.DMA((copies,))],
+        scratch_shapes=[pltpu.VMEM((copies, shape[0], CHUNK), F32), pltpu.SemaphoreType.DMA((copies,))],
         input_output_aliases=aliases,
         compiler_params=PARAMS,
         cost_estimate=pl.CostEstimate(flops=1, bytes_accessed=1, transcendentals=0),
@@ -308,19 +316,21 @@
 
     extra_cols, *extra_parts = tile(extra, [[0, 1]], own_parts[-1])
     extra_parts = reduced(extra_parts)
-    out = finished(
-        None,
-        extra_cols,
-        (own_cols, own_parts, [(0, width, "own", 0)]),
-        (extra_cols, extra_parts, [(0, width, "extra", 0)]),
-    )
+    out = finished(None, extra_cols, (own_cols, own_parts, "own"), (extra_cols, extra_parts, "extra"))
     two_cols, *two_parts, two = tile([first, passed, straight], [[0, 2], [1, 2]], out, keep=True)
     two_parts = reduced(two_parts)
     other = permute(two, siblings)
     other_cols, *other_parts = tile([other], [[0]])
     other_parts = reduced(other_parts)
-    out = finished(out, other_cols, (two_cols, two_parts, [(0, width, "two", 0)]))
-    return finished(out, other_cols, (other_cols, other_parts, [(0, width, "other", 0)]))
+    weights = call(
+        functools.partial(weigh_kernel, kind="other", period=period, width=width, members=everyone),
+        [jax.ShapeDtypeStruct((owned, width), F32)],
+        row_coord,
+        other_cols,
+        name="weigh",
+    )[0]
+    out = finished(out, weights, (two_cols, two_parts, "two"))
+    return finished(out, other_cols, (weights, other_parts, "other"))
 
 
 def solution(mesh):

time: 60.6 us -> 60 us (0.990)
    pallas_call x3, Pallas kernels: 5.41 us -> 4.54 us  [finish(): pl.pallas_call(functools.partial(finish_kernel, plan=plan, period=period,...]
    pallas_call x5 -> x6, Pallas kernels: 4.47 us -> 5.06 us  [call(): pl.pallas_call(kernel, out_shape=outs, in_specs=[VMEM] * len(operands), o...]
  transfers between devices with their start and end apart: 10 -> 10, of which waited for: 6 -> 6; matrix products, arithmetic and copies ran while one was open for 0% -> 0% of each run, Pallas kernels for 12% -> 13%
where the time goes in v6:
time: 60 us; the launch traced here: 59.8 us
  waiting for transfers between devices  37.5 us (62%)
  starting transfers between devices  10.6 us (18%)
  Pallas kernels  9.59 us (16%)
  local copies, waits for them, and re-layouts  1.99 us (3%)
    ppermute x6, waiting for transfers between devices, permute(): return lax.ppermute(array, 'mesh', pairs)  23.6 us
    ppermute x4, waiting for transfers between devices, reduced(): return [parts[1], lax.ppermute(parts[0], 'mem', [(0, 1), (1, 0)])]  13.9 us
    ppermute x4, starting transfers between devices, reduced(): return [parts[1], lax.ppermute(parts[0], 'mem', [(0, 1), (1, 0)])]  6.4 us
    pallas_call x6, Pallas kernels, call(): pl.pallas_call(kernel, out_shape=outs, in_specs=[VMEM] * len(operands), o...  5.06 us
    pallas_call x3, Pallas kernels, finish(): pl.pallas_call(functools.partial(finish_kernel, plan=plan, period=period,...  4.54 us
    ppermute x6, starting transfers between devices, permute(): return lax.ppermute(array, 'mesh', pairs)  4.16 us
    slice x1, local copies, waits for them, and re-layouts, per_device(): low = perturbations[:, :half]  1.3 us
  transfers between devices with their start and end apart: 10, of which 6 were waited for; matrix products, arithmetic and copies ran while one was open for 0% of the time, Pallas kernels for 13%

profile of v6, /device:TPU:26, one launch (start us, length us, event | category | flops | bytes accessed | tf_op | source)
XLA Modules:
  0.0 59.8 jit_solution(7296288512699883383)
XLA Ops:
  0.0 1.3 %slice.9.low = bf16[1536,256]{1,0:T(8,128)(2,1)S(1)} slice(bf16[1536,512]{1,0:T(8,128)(2,1)} %x), slice={[0:1536], [0:256]} | slice | bytes 1572864 | tf_op jit(solution)/shard_map/slice | solution.py:299
  1.3 0.6 %collective-permute-start.4 = (bf16[1536,256]{1,0:T(8,128)(2,1)S(1)}, bf16[1536,256]{1,0:T(8,128)(2,1)S(1)}, u32[]{:S(2)}, u32[]{:S(2)}) collective-permute-start(bf16[1536,256]{1,0:T(8,128)(2,1)S(1)} %slice.9.low), channel_id=1, source_target_pairs={{0,4},{2,6},{4,0},{6,2},{8,12},{10,14},{12,8},{14,10},{16,20},{18,... | collective-permute-start | bytes 2359304 | tf_op jit(solution)/shard_map/ppermute | solution.py:284
  1.9 0.7 %copy-done.1 = s32[512]{0:T(512)S(1)} copy-done((s32[512]{0:T(512)S(1)}, s32[512]{0:T(512)}, u32[]{:S(2)}) %copy-start.1) | copy-done | bytes 2072
  2.7 0.6 collective-permute-start.1
  3.3 1.2 %own_tile.1 = (bf16[512,1536]{1,0:T(8,128)(2,1)S(1)}, f32[256,128]{1,0:T(8,128)S(1)}, f32[256,128]{1,0:T(8,128)S(1)}, f32[256,512]{1,0:T(8,128)S(1)}, f32[256,512]{1,0:T(8,128)S(1)}) custom-call(bf16[1536,256]{1,0:T(8,128)(2,1)S(1)} %slice.9.low, bf16[1552,256]{1,0:T(8,128)(2,1)S(1)} %prepare.1.high, s32[1,512]{1,0:T(1,128)S(1)} %bitcast.3, s32[1,512]{1,0:T(1,128)S(1)} %bitcast.4), custom_call_target="tpu_custom_call" | custom-call | flops 1 | bytes 1 | tf_op jit(solution)/shard_map/own_tile/pallas_call | solution.py:24
  4.5 1.6 %collective-permute-start = (f32[256,512]{1,0:T(8,128)S(1)}, f32[256,512]{1,0:T(8,128)S(1)}, u32[]{:S(2)}, u32[]{:S(2)}) collective-permute-start(f32[256,512]{1,0:T(8,128)S(1)} %get-tuple-element.31), channel_id=1, source_target_pairs={{0,1},{1,0},{2,3},{3,2},{4,5},{5,4},{6,7},{7,6},{8,9},{9,8},{10,11... | collective-permute-start | bytes 1572872 | tf_op jit(solution)/shard_map/ppermute | solution.py:295
  6.2 14.5 %collective-permute-done.4.refs_0_ = bf16[1536,256]{1,0:T(8,128)(2,1)S(1)} collective-permute-done((bf16[1536,256]{1,0:T(8,128)(2,1)S(1)}, bf16[1536,256]{1,0:T(8,128)(2,1)S(1)}, u32[]{:S(2)}, u32[]{:S(2)}) %collective-permute-start.4) | collective-permute-done | bytes 786464 | tf_op jit(solution)/shard_map/ppermute | solution.py:284
  20.7 0.5 collective-permute-start.6
  21.2 2.3 %collective-permute-start.5 = (bf16[1536,256]{1,0:T(8,128)(2,1)S(1)}, bf16[1536,256]{1,0:T(8,128)(2,1)S(1)}, u32[]{:S(2)}, u32[]{:S(2)}) collective-permute-start(bf16[1536,256]{1,0:T(8,128)(2,1)S(1)} %collective-permute-done.4.refs_0_), channel_id=1, source_target_pairs={{4,28},{6,30},{12,4},{14,6},{20,12},{22,14},{28,20},{30,22},{5,29}... | collective-permute-start | bytes 2359304 | tf_op jit(solution)/shard_map/ppermute | solution.py:284
  23.6 1.0 %panel_tile.3 = (f32[8,512]{1,0:T(8,128)S(1)}, s32[264,256]{1,0:T(8,128)S(1)}, f32[256,512]{1,0:T(8,128)S(1)}) custom-call(bf16[512,1536]{1,0:T(8,128)(2,1)S(1)} %get-tuple-element.38.lt, bf16[1536,256]{1,0:T(8,128)(2,1)S(1)} %collective-permute-done.1.refs_0_, bf16[1552,256]{1,0:T(8,128)(2,1)S(1)} %collective-permute-done.2.refs_1_), custom_call_target="tpu_custom_call" | custom-call | flops 1 | bytes 1 | tf_op jit(solution)/shard_map/panel_tile/pallas_call | solution.py:24
  24.6 1.6 %collective-permute-start.3 = (s32[264,256]{1,0:T(8,128)S(1)}, s32[264,256]{1,0:T(8,128)S(1)}, u32[]{:S(2)}, u32[]{:S(2)}) collective-permute-start(s32[264,256]{1,0:T(8,128)S(1)} %get-tuple-element.37), channel_id=1, source_target_pairs={{0,1},{1,0},{2,3},{3,2},{4,5},{5,4},{6,7},{7,6},{8,9},{9,8},{10,11... | collective-permute-start | bytes 811016 | tf_op jit(solution)/shard_map/ppermute | solution.py:295
  26.2 7.3 %collective-permute-done.3.refs_5_ = s32[264,256]{1,0:T(8,128)S(1)} collective-permute-done((s32[264,256]{1,0:T(8,128)S(1)}, s32[264,256]{1,0:T(8,128)S(1)}, u32[]{:S(2)}, u32[]{:S(2)}) %collective-permute-start.3) | collective-permute-done | bytes 270368 | tf_op jit(solution)/shard_map/ppermute | solution.py:295
  33.5 2.2 %finish.3.refs_3_ = f32[256,2048]{1,0:T(8,128)} custom-call(f32[256,128]{1,0:T(8,128)S(1)} %get-tuple-element.28.row_coord, f32[256,128]{1,0:T(8,128)S(1)} %get-tuple-element.29.row_level, f32[8,512]{1,0:T(8,128)S(1)} %maximum_convert_fusion.refs_0_, f32[256,512]{1,0:T(8,128)S(1)} %get-tuple-element.35.refs_1_, f32[256,512]{1,0:T(8,128)S(1)} %collective-permute-done.refs_2_, ...), custom_call_target="tpu_custom_call" | custom-call | flops 1 | bytes 1 | tf_op jit(solution)/shard_map/finish/pallas_call | solution.py:257
  35.7 7.3 %collective-permute-done.5.refs_1_ = bf16[1536,256]{1,0:T(8,128)(2,1)S(1)} collective-permute-done((bf16[1536,256]{1,0:T(8,128)(2,1)S(1)}, bf16[1536,256]{1,0:T(8,128)(2,1)S(1)}, u32[]{:S(2)}, u32[]{:S(2)}) %collective-permute-start.5) | collective-permute-done | bytes 786464 | tf_op jit(solution)/shard_map/ppermute | solution.py:284
  43.0 1.1 %panel_tile.4 = (f32[8,512]{1,0:T(8,128)S(1)}, s32[264,256]{1,0:T(8,128)S(1)}, f32[256,512]{1,0:T(8,128)S(1)}, bf16[1552,512]{1,0:T(8,128)(2,1)S(1)}) custom-call(bf16[512,1536]{1,0:T(8,128)(2,1)S(1)} %get-tuple-element.38.lt, bf16[1536,256]{1,0:T(8,128)(2,1)S(1)} %collective-permute-done.4.refs_0_, bf16[1536,256]{1,0:T(8,128)(2,1)S(1)} %collective-permute-done.5.refs_1_, ...), custom_call_target="tpu_custom_call" | custom-call | flops 1 | bytes 1 | tf_op jit(solution)/shard_map/panel_tile/pallas_call | solution.py:24
  44.2 1.6 %collective-permute-start.9 = (s32[264,256]{1,0:T(8,128)S(1)}, s32[264,256]{1,0:T(8,128)S(1)}, u32[]{:S(2)}, u32[]{:S(2)}) collective-permute-start(s32[264,256]{1,0:T(8,128)S(1)} %get-tuple-element.48), channel_id=1, source_target_pairs={{0,1},{1,0},{2,3},{3,2},{4,5},{5,4},{6,7},{7,6},{8,9},{9,8},{10,11... | collective-permute-start | bytes 811016 | tf_op jit(solution)/shard_map/ppermute | solution.py:295
  45.8 1.8 %collective-permute-done.7.refs_0_ = bf16[1552,512]{1,0:T(8,128)(2,1)S(1)} collective-permute-done((bf16[1552,512]{1,0:T(8,128)(2,1)S(1)}, bf16[1552,512]{1,0:T(8,128)(2,1)S(1)}, u32[]{:S(2)}, u32[]{:S(2)}) %collective-permute-start.7) | collective-permute-done | bytes 1589280 | tf_op jit(solution)/shard_map/ppermute | solution.py:284
  47.6 1.0 %panel_tile.5 = (f32[8,512]{1,0:T(8,128)S(1)}, s32[264,256]{1,0:T(8,128)S(1)}, f32[256,512]{1,0:T(8,128)S(1)}) custom-call(bf16[512,1536]{1,0:T(8,128)(2,1)S(1)} %get-tuple-element.38.lt, bf16[1552,512]{1,0:T(8,128)(2,1)S(1)} %collective-permute-done.7.refs_0_), custom_call_target="tpu_custom_call" | custom-call | flops 1 | bytes 1 | tf_op jit(solution)/shard_map/panel_tile/pallas_call | solution.py:24
  48.7 1.6 %collective-permute-start.8 = (s32[264,256]{1,0:T(8,128)S(1)}, s32[264,256]{1,0:T(8,128)S(1)}, u32[]{:S(2)}, u32[]{:S(2)}) collective-permute-start(s32[264,256]{1,0:T(8,128)S(1)} %get-tuple-element.44), channel_id=1, source_target_pairs={{0,1},{1,0},{2,3},{3,2},{4,5},{5,4},{6,7},{7,6},{8,9},{9,8},{10,11... | collective-permute-start | bytes 811016 | tf_op jit(solution)/shard_map/ppermute | solution.py:295
  50.2 0.6 weigh.1.refs_0_
  50.8 2.7 %collective-permute-done.9.refs_2_ = s32[264,256]{1,0:T(8,128)S(1)} collective-permute-done((s32[264,256]{1,0:T(8,128)S(1)}, s32[264,256]{1,0:T(8,128)S(1)}, u32[]{:S(2)}, u32[]{:S(2)}) %collective-permute-start.9) | collective-permute-done | bytes 270368 | tf_op jit(solution)/shard_map/ppermute | solution.py:295
  53.6 1.5 %finish.4.refs_3_ = f32[256,2048]{1,0:T(8,128)} custom-call(f32[256,128]{1,0:T(8,128)S(1)} %get-tuple-element.28.row_coord, f32[256,128]{1,0:T(8,128)S(1)} %get-tuple-element.29.row_level, f32[8,512]{1,0:T(8,128)S(1)} %get-tuple-element.46.refs_0_, f32[256,512]{1,0:T(8,128)S(1)} %get-tuple-element.47.refs_1_, ...), custom_call_target="tpu_custom_call", output_to_operand_aliasing={{}: (5, {})} | custom-call | flops 1 | bytes 1 | tf_op jit(solution)/shard_map/finish/pallas_call | solution.py:257
  55.0 3.9 %collective-permute-done.8.refs_2_ = s32[264,256]{1,0:T(8,128)S(1)} collective-permute-done((s32[264,256]{1,0:T(8,128)S(1)}, s32[264,256]{1,0:T(8,128)S(1)}, u32[]{:S(2)}, u32[]{:S(2)}) %collective-permute-start.8) | collective-permute-done | bytes 270368 | tf_op jit(solution)/shard_map/ppermute | solution.py:295
  58.9 0.9 %finish.5 = f32[256,2048]{1,0:T(8,128)} custom-call(f32[256,128]{1,0:T(8,128)S(1)} %get-tuple-element.28.row_coord, f32[256,128]{1,0:T(8,128)S(1)} %get-tuple-element.29.row_level, f32[256,512]{1,0:T(8,128)S(1)} %weigh.1.refs_0_, f32[256,512]{1,0:T(8,128)S(1)} %get-tuple-element.43.refs_1_, ...), custom_call_target="tpu_custom_call", output_to_operand_aliasing={{}: (5, {})} | custom-call | flops 1 | bytes 1 | tf_op jit(solution)/shard_map/finish/pallas_call | solution.py:257
  (14 shorter events, 0.2 us)
Async XLA Ops:
  0.0 1.9 %copy-start = (bf16[1536,512]{1,0:T(8,128)(2,1)S(1)}, bf16[1536,512]{1,0:T(8,128)(2,1)}, u32[]{:S(2)}) copy-start(bf16[1536,512]{1,0:T(8,128)(2,1)} %x) | copy-start | bytes 4718596
  1.3 19.3 %collective-permute-start.4 = (bf16[1536,256]{1,0:T(8,128)(2,1)S(1)}, bf16[1536,256]{1,0:T(8,128)(2,1)S(1)}, u32[]{:S(2)}, u32[]{:S(2)}) collective-permute-start(bf16[1536,256]{1,0:T(8,128)(2,1)S(1)} %slice.9.low), channel_id=1, source_target_pairs={{0,4},{2,6},{4,0},{6,2},{8,12},{10,14},{12,8},{14,10},{16,20},{18,... | collective-permute-start | bytes 2359304 | tf_op jit(solution)/shard_map/ppermute | solution.py:284
  1.9 0.7 %copy-start.1 = (s32[512]{0:T(512)S(1)}, s32[512]{0:T(512)}, u32[]{:S(2)}) copy-start(s32[512]{0:T(512)} %param.4) | copy-start | bytes 6148
  2.6 0.7 %copy-start.2 = (s32[512]{0:T(512)S(1)}, s32[512]{0:T(512)}, u32[]{:S(2)}) copy-start(s32[512]{0:T(512)} %param.5) | copy-start | bytes 6148
  2.7 20.9 %collective-permute-start.2 = (bf16[1552,256]{1,0:T(8,128)(2,1)S(1)}, bf16[1552,256]{1,0:T(8,128)(2,1)S(1)}, u32[]{:S(2)}, u32[]{:S(2)}) collective-permute-start(bf16[1552,256]{1,0:T(8,128)(2,1)S(1)} %prepare.1.high), channel_id=1, source_target_pairs={{0,26},{2,0},{4,30},{6,4},{8,2},{10,8},{12,6},{14,12},{16,10},{18,... | collective-permute-start | bytes 2383880 | tf_op jit(solution)/shard_map/ppermute | solution.py:284
  2.7 20.8 %collective-permute-start.1 = (bf16[1536,256]{1,0:T(8,128)(2,1)S(1)}, bf16[1536,256]{1,0:T(8,128)(2,1)S(1)}, u32[]{:S(2)}, u32[]{:S(2)}) collective-permute-start(bf16[1536,256]{1,0:T(8,128)(2,1)S(1)} %slice.9.low), channel_id=1, source_target_pairs={{0,26},{2,0},{4,30},{6,4},{8,2},{10,8},{12,6},{14,12},{16,10},{18,... | collective-permute-start | bytes 2359304 | tf_op jit(solution)/shard_map/ppermute | solution.py:284
  4.5 19.0 %collective-permute-start = (f32[256,512]{1,0:T(8,128)S(1)}, f32[256,512]{1,0:T(8,128)S(1)}, u32[]{:S(2)}, u32[]{:S(2)}) collective-permute-start(f32[256,512]{1,0:T(8,128)S(1)} %get-tuple-element.31), channel_id=1, source_target_pairs={{0,1},{1,0},{2,3},{3,2},{4,5},{5,4},{6,7},{7,6},{8,9},{9,8},{10,11... | collective-permute-start | bytes 1572872 | tf_op jit(solution)/shard_map/ppermute | solution.py:295
  20.7 22.3 %collective-permute-start.6 = (bf16[1552,256]{1,0:T(8,128)(2,1)S(1)}, bf16[1552,256]{1,0:T(8,128)(2,1)S(1)}, u32[]{:S(2)}, u32[]{:S(2)}) collective-permute-start(bf16[1552,256]{1,0:T(8,128)(2,1)S(1)} %prepare.1.high), channel_id=1, source_target_pairs={{0,28},{2,30},{4,0},{6,2},{8,4},{10,6},{12,8},{14,10},{16,12},{18,... | collective-permute-start | bytes 2383880 | tf_op jit(solution)/shard_map/ppermute | solution.py:284
  21.2 21.8 %collective-permute-start.5 = (bf16[1536,256]{1,0:T(8,128)(2,1)S(1)}, bf16[1536,256]{1,0:T(8,128)(2,1)S(1)}, u32[]{:S(2)}, u32[]{:S(2)}) collective-permute-start(bf16[1536,256]{1,0:T(8,128)(2,1)S(1)} %collective-permute-done.4.refs_0_), channel_id=1, source_target_pairs={{4,28},{6,30},{12,4},{14,6},{20,12},{22,14},{28,20},{30,22},{5,29}... | collective-permute-start | bytes 2359304 | tf_op jit(solution)/shard_map/ppermute | solution.py:284
  24.6 8.9 %collective-permute-start.3 = (s32[264,256]{1,0:T(8,128)S(1)}, s32[264,256]{1,0:T(8,128)S(1)}, u32[]{:S(2)}, u32[]{:S(2)}) collective-permute-start(s32[264,256]{1,0:T(8,128)S(1)} %get-tuple-element.37), channel_id=1, source_target_pairs={{0,1},{1,0},{2,3},{3,2},{4,5},{5,4},{6,7},{7,6},{8,9},{9,8},{10,11... | collective-permute-start | bytes 811016 | tf_op jit(solution)/shard_map/ppermute | solution.py:295
  44.1 3.5 %collective-permute-start.7 = (bf16[1552,512]{1,0:T(8,128)(2,1)S(1)}, bf16[1552,512]{1,0:T(8,128)(2,1)S(1)}, u32[]{:S(2)}, u32[]{:S(2)}) collective-permute-start(bf16[1552,512]{1,0:T(8,128)(2,1)S(1)} %get-tuple-element.40), channel_id=1, source_target_pairs={{0,2},{2,0},{4,6},{6,4},{8,10},{10,8},{12,14},{14,12},{16,18},{18,... | collective-permute-start | bytes 4767752 | tf_op jit(solution)/shard_map/ppermute | solution.py:284
  44.2 9.3 %collective-permute-start.9 = (s32[264,256]{1,0:T(8,128)S(1)}, s32[264,256]{1,0:T(8,128)S(1)}, u32[]{:S(2)}, u32[]{:S(2)}) collective-permute-start(s32[264,256]{1,0:T(8,128)S(1)} %get-tuple-element.48), channel_id=1, source_target_pairs={{0,1},{1,0},{2,3},{3,2},{4,5},{5,4},{6,7},{7,6},{8,9},{9,8},{10,11... | collective-permute-start | bytes 811016 | tf_op jit(solution)/shard_map/ppermute | solution.py:295
  48.7 10.2 %collective-permute-start.8 = (s32[264,256]{1,0:T(8,128)S(1)}, s32[264,256]{1,0:T(8,128)S(1)}, u32[]{:S(2)}, u32[]{:S(2)}) collective-permute-start(s32[264,256]{1,0:T(8,128)S(1)} %get-tuple-element.44), channel_id=1, source_target_pairs={{0,1},{1,0},{2,3},{3,2},{4,5},{5,4},{6,7},{7,6},{8,9},{9,8},{10,11... | collective-permute-start | bytes 811016 | tf_op jit(solution)/shard_map/ppermute | solution.py:295

commit v7 on v6

--- a/solution.py
+++ b/solution.py
@@ -39,7 +39,7 @@
     return jnp.where(r <= 1.0, near, jnp.where(r <= 2.0, far, 0.0))
 
 
-def prepare_kernel(x, coord, high):
+def prepare_kernel(x, coord, high, *parts):
     members, width = x.shape
     half = width // 2
     first = 4 * width * lax.axis_index("mesh")
@@ -50,12 +50,24 @@
         [jnp.broadcast_to(jitter[:, :half], (PAD // 2, half)), jnp.broadcast_to(jitter[:, half:], (PAD // 2, half))],
         axis=0,
     ).astype(x.dtype)
+    cut_kernel(high, *parts)
+
+
+def cut_kernel(whole, *parts):
+    wide = parts[0].shape[1]
+    for i, part in enumerate(parts):
+        part[...] = whole[:, i * wide : (i + 1) * wide]
+
+
+def cut(panel):
+    half = jax.ShapeDtypeStruct((panel.shape[0], panel.shape[1] // 2), panel.dtype)
+    return call(cut_kernel, [half] * 2, panel, name="cut")
 
 
 def prepare(x, coord):
     members, width = x.shape
-    half = jax.ShapeDtypeStruct((members + PAD, width // 2), x.dtype)
-    return call(prepare_kernel, [half], x, coord, name="prepare")[0]
+    outs = [jax.ShapeDtypeStruct((members + PAD, w), x.dtype) for w in (width // 2, width // 4, width // 4)]
+    return call(prepare_kernel, outs, x, coord, name="prepare")
 
 
 def own_kernel(low, high, coord, level, lt, row_coord, row_level, *outs, owned, split):
@@ -139,7 +151,7 @@
     return widened((words << 16) >> 16, packed[rows + 4 : rows + 5, span])
 
 
-def panel_kernel(lt, *refs, picks, count, rows, keep):
+def panel_kernel(lt, *refs, picks, count, rows, pieces):
     panels, cols, outs = refs[:count], refs[count], refs[count + 1 :]
     members = lt.shape[1]
 
@@ -151,11 +163,55 @@
             pad = [pad[0][:, :half], pad[0][:, half:]]
         cols[:, :half] = pad[0][: PAD // 2]
         cols[:, half:] = pad[1][PAD // 2 :]
-        if keep:
-            for at, panel in zip((0, half), chosen):
-                outs[-1][:members, at : at + half] = panel[:members, :]
-                outs[-1][members:, at : at + half] = chosen[-1][members:, :]
         block = jnp.concatenate([panel[:members, :] for panel in chosen], axis=1)
+        tile = jnp.dot(lt[...], block, preferred_element_type=F32)
+        if len(rows) > 1:
+            wide = tile.shape[1] // pieces
+            for i in range(pieces):
+                pack(tile[: rows[0], i * wide : (i + 1) * wide], outs[i])
+            outs[pieces][...] = tile[rows[0] :]
+        else:
+            outs[0][...] = tile
+
+    if len(picks) == 1:
+        run(picks[0])
+    else:
+        cross = lax.rem(lax.axis_index("mesh") // 2, 2)
+        for value, which in enumerate(picks):
+            pl.when(cross == value)(functools.partial(run, which))
+
+
+def panel_tile(lt, panels, picks, rows, pieces=1):
+    wide = sum(panels[i].shape[1] for i in picks[0])
+    width, members = lt.shape
+    outs = [jax.ShapeDtypeStruct((8, wide), F32)]
+    if len(rows) > 1:
+        outs += [jax.ShapeDtypeStruct((rows[0] + 8, wide // 2 // pieces), jnp.int32)] * pieces
+    outs.append(jax.ShapeDtypeStruct((rows[-1], wide), F32))
+    return call(
+        functools.partial(panel_kernel, picks=picks, count=len(panels), rows=rows, pieces=pieces),
+        outs,
+        lt,
+        *panels,
+        name="panel_tile",
+    )
+
+
+def last_kernel(lt, near0, near1, far0, far1, straight0, straight1, cols, *refs, rows):
+    outs, whole = refs[:-1], refs[-1]
+    members = lt.shape[1]
+    wide = near0.shape[1]
+
+    def run(low0, low1):
+        pad0, pad1 = straight0[members:, :], straight1[members:, :]
+        for i, (panel, pad) in enumerate(((low0, pad0), (low1, pad1), (straight0, pad0), (straight1, pad1))):
+            span = slice(i * wide, (i + 1) * wide)
+            whole[:members, span] = panel[:members, :]
+            whole[members:, span] = pad
+        pad1 = pad1.astype(F32)
+        cols[:, :wide] = pad1[: PAD // 2]
+        cols[:, wide:] = pad1[PAD // 2 :]
+        block = jnp.concatenate([low1[...], straight1[:members, :]], axis=1)
         tile = jnp.dot(lt[...], block, preferred_element_type=F32)
         if len(rows) > 1:
             pack(tile[: rows[0]], outs[0])
@@ -163,27 +219,22 @@
         else:
             outs[0][...] = tile
 
-    if len(picks) == 1:
-        run(picks[0])
-    else:
-        cross = lax.rem(lax.axis_index("mesh") // 2, 2)
-        for value, which in enumerate(picks):
-            pl.when(cross == value)(functools.partial(run, which))
-
-
-def panel_tile(lt, panels, picks, rows, keep=False):
-    wide = sum(panels[i].shape[1] for i in picks[0])
+    cross = lax.rem(lax.axis_index("mesh") // 2, 2)
+    pl.when(cross == 0)(lambda: run(near0, near1))
+    pl.when(cross == 1)(lambda: run(far0, far1))
+
+
+def last_tile(lt, panels, rows):
     width, members = lt.shape
+    wide = width // 2
     return call(
-        functools.partial(panel_kernel, picks=picks, count=len(panels), rows=rows, keep=keep),
+        functools.partial(last_kernel, rows=rows),
         [jax.ShapeDtypeStruct((8, wide), F32)]
         + ([jax.ShapeDtypeStruct((rows[0] + 8, wide // 2), jnp.int32)] if len(rows) > 1 else [])
-        + [jax.ShapeDtypeStruct((rows[-1], wide), F32)]
-        + ([jax.ShapeDtypeStruct((members + PAD, wide), lt.dtype)] if keep else []),
+        + [jax.ShapeDtypeStruct((rows[-1], wide), F32), jax.ShapeDtypeStruct((members + PAD, width), lt.dtype)],
         lt,
         *panels,
-        name="panel_tile",
-        flops=2 * members * width * wide,
+        name="last_tile",
     )
 
 
@@ -214,17 +265,19 @@
     coord, level = row_coord[...], row_level[...]
     copies = []
     at = 0
-    for n, kind in plan:
+    for n, kind, starts in plan:
         cols, parts = refs[at], refs[at + 1 : at + 1 + n]
         at += 1 + n
         step = steps[kind]
-        for begin in range(0, width, CHUNK):
-            span = slice(begin, begin + CHUNK)
+        for block, begin in enumerate(starts):
+            span = slice(block * CHUNK, (block + 1) * CHUNK)
             slot = len(copies)
             raw = parts[0][:, span]
-            for part in parts[1:]:
+            if len(parts) > 1:
+                share = len(starts) // (len(parts) - 1)
+                part = parts[1 + block // share]
                 if part.dtype == jnp.int32:
-                    raw = raw + unpack(part, begin // CHUNK, raw.shape[0])
+                    raw = raw + unpack(part, block % share, raw.shape[0])
                 else:
                     raw = raw + part[:, span]
             if cols.shape[0] == out.shape[0]:
@@ -244,10 +297,10 @@
 def finish(row_coord, row_level, groups, out, shape, period, width, members):
     operands = [row_coord, row_level]
     plan = []
-    for cols, parts, kind in groups:
+    for cols, parts, kind, starts in groups:
         operands += [cols, *parts]
-        plan.append((len(parts), kind))
-    copies = len(plan) * (width // CHUNK)
+        plan.append((len(parts), kind, starts))
+    copies = sum(len(starts) for _, _, starts in plan)
     specs = [VMEM] * len(operands)
     aliases = {}
     if out is not None:
@@ -292,23 +345,24 @@
 
     def reduced(parts):
         if split:
-            return [parts[1], lax.ppermute(parts[0], "mem", [(0, 1), (1, 0)])]
+            return [parts[-1]] + [lax.ppermute(a, "mem", [(0, 1), (1, 0)]) for a in parts[:-1]]
         return [lax.psum_scatter(parts[0], "mem", scatter_dimension=0, tiled=True)]
 
     half = width // 2
     low = perturbations[:, :half]
-    high = prepare(after(perturbations, low), coord)
+    high, *highs = prepare(after(perturbations, low), coord)
     lt, row_coord, row_level, *own = own_tile(low, high, coord, levels, owned, rows)
     own_parts = reduced(own)
     own_cols = jnp.concatenate([high[members : members + PAD // 2], high[members + PAD // 2 :]], axis=1).astype(F32)
 
     first = permute(low, swap_x)
     extra = [permute(a, extra_pairs) for a in (low, high)]
-    straight = permute(after(high, first), back_two)
-    passed = permute(first, relay)
-
-    def tile(panels, picks, *tokens, keep=False):
-        return panel_tile(after(lt, *tokens), panels, picks, rows, keep)
+    straight = [permute(after(a, first), back_two) for a in highs]
+    near = cut(first)
+    passed = [permute(a, relay) for a in near]
+
+    def tile(panels, picks, *tokens, pieces=1):
+        return panel_tile(after(lt, *tokens), panels, picks, rows, pieces)
 
     def finished(out, token, *groups):
         groups = [(after(groups[0][0], token), *groups[0][1:])] + list(groups[1:])
@@ -316,11 +370,14 @@
 
     extra_cols, *extra_parts = tile(extra, [[0, 1]], own_parts[-1])
     extra_parts = reduced(extra_parts)
-    out = finished(None, extra_cols, (own_cols, own_parts, "own"), (extra_cols, extra_parts, "extra"))
-    two_cols, *two_parts, two = tile([first, passed, straight], [[0, 2], [1, 2]], out, keep=True)
-    two_parts = reduced(two_parts)
+    early_cols, *early_parts = tile([near[0], passed[0], straight[0]], [[0, 2], [1, 2]], extra_cols)
+    early_parts = reduced(early_parts)
+    whole = [i * CHUNK for i in range(width // CHUNK)]
+    out = finished(None, early_cols, (own_cols, own_parts, "own", whole), (extra_cols, extra_parts, "extra", whole))
+    late_cols, *late_parts, two = last_tile(after(lt, out, early_parts[-1]), [*near, *passed, *straight], rows)
+    late_parts = reduced(late_parts)
     other = permute(two, siblings)
-    other_cols, *other_parts = tile([other], [[0]])
+    other_cols, *other_parts = tile([other], [[0]], pieces=2)
     other_parts = reduced(other_parts)
     weights = call(
         functools.partial(weigh_kernel, kind="other", period=period, width=width, members=everyone),
@@ -329,8 +386,13 @@
         other_cols,
         name="weigh",
     )[0]
-    out = finished(out, weights, (two_cols, two_parts, "two"))
-    return finished(out, other_cols, (weights, other_parts, "other"))
+    out = finished(
+        out,
+        weights,
+        (early_cols, early_parts, "two", [0, half]),
+        (late_cols, late_parts, "two", [CHUNK, half + CHUNK]),
+    )
+    return finished(out, other_cols, (weights, other_parts, "other", whole))
 
 
 def solution(mesh):

time: 60 us -> 58.3 us (0.972)
  waiting for transfers between devices: 37.5 us -> 29.2 us
  starting transfers between devices: 10.6 us -> 15.1 us
  local copies, waits for them, and re-layouts: 1.99 us -> 3.35 us
  Pallas kernels: 9.59 us -> 10.2 us
    ppermute x4 -> x6, waiting for transfers between devices: 13.9 us -> 5.72 us  [reduced(): lax.ppermute(a, 'mem', [(0, 1), (1, 0)])]
    ppermute x6 -> x8, starting transfers between devices: 4.16 us -> 6.59 us  [permute(): return lax.ppermute(array, 'mesh', pairs)]
    ppermute x4 -> x6, starting transfers between devices: 6.4 us -> 8.51 us  [reduced(): lax.ppermute(a, 'mem', [(0, 1), (1, 0)])]
    unnamed x6 -> x8, local copies, waits for them, and re-layouts: 0.69 us -> 2.05 us
    pallas_call x6 -> x8, Pallas kernels: 5.06 us -> 5.65 us  [call(): pl.pallas_call(kernel, out_shape=outs, in_specs=[VMEM] * len(operands), o...]
    ppermute x6 -> x8, waiting for transfers between devices: 23.6 us -> 23.5 us  [permute(): return lax.ppermute(array, 'mesh', pairs)]
  transfers between devices with their start and end apart: 10 -> 14, of which waited for: 6 -> 7; matrix products, arithmetic and copies ran while one was open for 0% -> 0% of each run, Pallas kernels for 13% -> 15%
where the time goes in v7:
time: 58.3 us; the launch traced here: 58.1 us
  waiting for transfers between devices  29.2 us (50%)
  starting transfers between devices  15.1 us (26%)
  Pallas kernels  10.2 us (17%)
  local copies, waits for them, and re-layouts  3.35 us (6%)
    ppermute x8, waiting for transfers between devices, permute(): return lax.ppermute(array, 'mesh', pairs)  23.5 us
    ppermute x6, starting transfers between devices, reduced(): lax.ppermute(a, 'mem', [(0, 1), (1, 0)])  8.51 us
    ppermute x8, starting transfers between devices, permute(): return lax.ppermute(array, 'mesh', pairs)  6.59 us
    ppermute x6, waiting for transfers between devices, reduced(): lax.ppermute(a, 'mem', [(0, 1), (1, 0)])  5.72 us
    pallas_call x8, Pallas kernels, call(): pl.pallas_call(kernel, out_shape=outs, in_specs=[VMEM] * len(operands), o...  5.65 us
    pallas_call x3, Pallas kernels, finish(): pl.pallas_call(functools.partial(finish_kernel, plan=plan, period=period,...  4.56 us
    unnamed x8, local copies, waits for them, and re-layouts  2.05 us
    slice x1, local copies, waits for them, and re-layouts, per_device(): low = perturbations[:, :half]  1.3 us
  transfers between devices with their start and end apart: 14, of which 7 were waited for; matrix products, arithmetic and copies ran while one was open for 0% of the time, Pallas kernels for 15%

profile of v7, /device:TPU:26, one launch (start us, length us, event | category | flops | bytes accessed | tf_op | source)
XLA Modules:
  0.0 58.1 jit_solution(9862256390517934591)
XLA Ops:
  0.0 1.3 %slice.9.low = bf16[1536,256]{1,0:T(8,128)(2,1)S(1)} slice(bf16[1536,512]{1,0:T(8,128)(2,1)} %x), slice={[0:1536], [0:256]} | slice | bytes 1572864 | tf_op jit(solution)/shard_map/slice | solution.py:352
  1.9 0.7 %copy-done.1 = s32[512]{0:T(512)S(1)} copy-done((s32[512]{0:T(512)S(1)}, s32[512]{0:T(512)}, u32[]{:S(2)}) %copy-start.1) | copy-done | bytes 2072
  3.4 0.7 %copy-done.2 = s32[512]{0:T(512)S(1)} copy-done((s32[512]{0:T(512)S(1)}, s32[512]{0:T(512)}, u32[]{:S(2)}) %copy-start.2) | copy-done | bytes 2072
  4.1 0.7 %copy-done.3 = s32[512]{0:T(512)S(1)} copy-done((s32[512]{0:T(512)S(1)}, s32[512]{0:T(512)}, u32[]{:S(2)}) %copy-start.3) | copy-done | bytes 2072
  4.8 1.2 %own_tile.1 = (bf16[512,1536]{1,0:T(8,128)(2,1)S(1)}, f32[256,128]{1,0:T(8,128)S(1)}, f32[256,128]{1,0:T(8,128)S(1)}, f32[256,512]{1,0:T(8,128)S(1)}, f32[256,512]{1,0:T(8,128)S(1)}) custom-call(bf16[1536,256]{1,0:T(8,128)(2,1)S(1)} %slice.9.low, bf16[1552,256]{1,0:T(8,128)(2,1)S(1)} %get-tuple-element.39.high, s32[1,512]{1,0:T(1,128)S(1)} %bitcast.3, ...), custom_call_target="tpu_custom_call" | custom-call | flops 1 | bytes 1 | tf_op jit(solution)/shard_map/own_tile/pallas_call | solution.py:24
  6.0 1.7 %collective-permute-start = (f32[256,512]{1,0:T(8,128)S(1)}, f32[256,512]{1,0:T(8,128)S(1)}, u32[]{:S(2)}, u32[]{:S(2)}) collective-permute-start(f32[256,512]{1,0:T(8,128)S(1)} %get-tuple-element.43), channel_id=1, source_target_pairs={{0,1},{1,0},{2,3},{3,2},{4,5},{5,4},{6,7},{7,6},{8,9},{9,8},{10,11... | collective-permute-start | bytes 1572872 | tf_op jit(solution)/shard_map/ppermute | solution.py:348
  7.7 13.0 %collective-permute-done.3.whole = bf16[1536,256]{1,0:T(8,128)(2,1)S(1)} collective-permute-done((bf16[1536,256]{1,0:T(8,128)(2,1)S(1)}, bf16[1536,256]{1,0:T(8,128)(2,1)S(1)}, u32[]{:S(2)}, u32[]{:S(2)}) %collective-permute-start.3) | collective-permute-done | bytes 786464 | tf_op jit(solution)/shard_map/ppermute | solution.py:337
  21.3 2.4 %collective-permute-start.4 = (bf16[1536,128]{1,0:T(8,128)(2,1)S(1)}, bf16[1536,128]{1,0:T(8,128)(2,1)S(1)}, u32[]{:S(2)}, u32[]{:S(2)}) collective-permute-start(bf16[1536,128]{1,0:T(8,128)(2,1)S(1)} %get-tuple-element.47.refs_0_.near0), channel_id=1, source_target_pairs={{4,28},{6,30},{12,4},{14,6},{20,12},{22,14},{28,20},{30,22},{5,29}... | collective-permute-start | bytes 1179656 | tf_op jit(solution)/shard_map/ppermute | solution.py:337
  23.8 2.4 %collective-permute-start.8 = (bf16[1536,128]{1,0:T(8,128)(2,1)S(1)}, bf16[1536,128]{1,0:T(8,128)(2,1)S(1)}, u32[]{:S(2)}, u32[]{:S(2)}) collective-permute-start(bf16[1536,128]{1,0:T(8,128)(2,1)S(1)} %get-tuple-element.57.near1), channel_id=1, source_target_pairs={{4,28},{6,30},{12,4},{14,6},{20,12},{22,14},{28,20},{30,22},{5,29}... | collective-permute-start | bytes 1179656 | tf_op jit(solution)/shard_map/ppermute | solution.py:337
  26.2 1.0 %panel_tile.3 = (f32[8,512]{1,0:T(8,128)S(1)}, s32[264,256]{1,0:T(8,128)S(1)}, f32[256,512]{1,0:T(8,128)S(1)}) custom-call(bf16[512,1536]{1,0:T(8,128)(2,1)S(1)} %get-tuple-element.56.lt, bf16[1536,256]{1,0:T(8,128)(2,1)S(1)} %collective-permute-done.1.refs_0_, bf16[1552,256]{1,0:T(8,128)(2,1)S(1)} %collective-permute-done.2.refs_1_), custom_call_target="tpu_custom_call" | custom-call | flops 1 | bytes 1 | tf_op jit(solution)/shard_map/panel_tile/pallas_call | solution.py:24
  27.2 1.6 %collective-permute-start.6 = (s32[264,256]{1,0:T(8,128)S(1)}, s32[264,256]{1,0:T(8,128)S(1)}, u32[]{:S(2)}, u32[]{:S(2)}) collective-permute-start(s32[264,256]{1,0:T(8,128)S(1)} %get-tuple-element.54), channel_id=1, source_target_pairs={{0,1},{1,0},{2,3},{3,2},{4,5},{5,4},{6,7},{7,6},{8,9},{9,8},{10,11... | collective-permute-start | bytes 811016 | tf_op jit(solution)/shard_map/ppermute | solution.py:348
  28.8 8.3 %collective-permute-done.4.refs_1_.far0 = bf16[1536,128]{1,0:T(8,128)(2,1)S(1)} collective-permute-done((bf16[1536,128]{1,0:T(8,128)(2,1)S(1)}, bf16[1536,128]{1,0:T(8,128)(2,1)S(1)}, u32[]{:S(2)}, u32[]{:S(2)}) %collective-permute-start.4) | collective-permute-done | bytes 393248 | tf_op jit(solution)/shard_map/ppermute | solution.py:337
  37.7 1.6 %collective-permute-start.7 = (s32[264,128]{1,0:T(8,128)S(1)}, s32[264,128]{1,0:T(8,128)S(1)}, u32[]{:S(2)}, u32[]{:S(2)}) collective-permute-start(s32[264,128]{1,0:T(8,128)S(1)} %get-tuple-element.55), channel_id=1, source_target_pairs={{0,1},{1,0},{2,3},{3,2},{4,5},{5,4},{6,7},{7,6},{8,9},{9,8},{10,11... | collective-permute-start | bytes 405512 | tf_op jit(solution)/shard_map/ppermute | solution.py:348
  39.3 2.2 %finish.3.refs_6_ = f32[256,2048]{1,0:T(8,128)} custom-call(f32[256,128]{1,0:T(8,128)S(1)} %get-tuple-element.40.row_coord, f32[256,128]{1,0:T(8,128)S(1)} %get-tuple-element.41.row_level, f32[8,512]{1,0:T(8,128)S(1)} %maximum_convert_fusion.refs_0_, f32[256,512]{1,0:T(8,128)S(1)} %get-tuple-element.52.refs_1_, f32[256,512]{1,0:T(8,128)S(1)} %collective-permute-done.refs_2_, ...), custom_call_target="tpu_custom_call" | custom-call | flops 1 | bytes 1 | tf_op jit(solution)/shard_map/finish/pallas_call | solution.py:310
  41.5 1.3 %collective-permute-done.7.refs_2_ = s32[264,128]{1,0:T(8,128)S(1)} collective-permute-done((s32[264,128]{1,0:T(8,128)S(1)}, s32[264,128]{1,0:T(8,128)S(1)}, u32[]{:S(2)}, u32[]{:S(2)}) %collective-permute-start.7) | collective-permute-done | bytes 135200 | tf_op jit(solution)/shard_map/ppermute | solution.py:348
  43.2 0.9 %last_tile.1 = (f32[8,256]{1,0:T(8,128)S(1)}, s32[264,128]{1,0:T(8,128)S(1)}, f32[256,256]{1,0:T(8,128)S(1)}, bf16[1552,512]{1,0:T(8,128)(2,1)S(1)}) custom-call(bf16[512,1536]{1,0:T(8,128)(2,1)S(1)} %get-tuple-element.56.lt, bf16[1536,128]{1,0:T(8,128)(2,1)S(1)} %get-tuple-element.47.refs_0_.near0, bf16[1536,128]{1,0:T(8,128)(2,1)S(1)} %get-tuple-element.57.near1, ...), custom_call_target="tpu_custom_call" | custom-call | flops 1 | bytes 1 | tf_op jit(solution)/shard_map/last_tile/pallas_call | solution.py:24
  44.1 1.6 %collective-permute-start.13 = (s32[264,128]{1,0:T(8,128)S(1)}, s32[264,128]{1,0:T(8,128)S(1)}, u32[]{:S(2)}, u32[]{:S(2)}) collective-permute-start(s32[264,128]{1,0:T(8,128)S(1)} %get-tuple-element.70), channel_id=1, source_target_pairs={{0,1},{1,0},{2,3},{3,2},{4,5},{5,4},{6,7},{7,6},{8,9},{9,8},{10,11... | collective-permute-start | bytes 405512 | tf_op jit(solution)/shard_map/ppermute | solution.py:348
  45.7 1.8 %collective-permute-done.10.refs_0_ = bf16[1552,512]{1,0:T(8,128)(2,1)S(1)} collective-permute-done((bf16[1552,512]{1,0:T(8,128)(2,1)S(1)}, bf16[1552,512]{1,0:T(8,128)(2,1)S(1)}, u32[]{:S(2)}, u32[]{:S(2)}) %collective-permute-start.10) | collective-permute-done | bytes 1589280 | tf_op jit(solution)/shard_map/ppermute | solution.py:337
  47.5 1.0 %panel_tile.5 = (f32[8,512]{1,0:T(8,128)S(1)}, s32[264,128]{1,0:T(8,128)S(1)}, s32[264,128]{1,0:T(8,128)S(1)}, f32[256,512]{1,0:T(8,128)S(1)}) custom-call(bf16[512,1536]{1,0:T(8,128)(2,1)S(1)} %get-tuple-element.56.lt, bf16[1552,512]{1,0:T(8,128)(2,1)S(1)} %collective-permute-done.10.refs_0_), custom_call_target="tpu_custom_call" | custom-call | flops 1 | bytes 1 | tf_op jit(solution)/shard_map/panel_tile/pallas_call | solution.py:24
  48.6 1.6 %collective-permute-start.11 = (s32[264,128]{1,0:T(8,128)S(1)}, s32[264,128]{1,0:T(8,128)S(1)}, u32[]{:S(2)}, u32[]{:S(2)}) collective-permute-start(s32[264,128]{1,0:T(8,128)S(1)} %get-tuple-element.64), channel_id=1, source_target_pairs={{0,1},{1,0},{2,3},{3,2},{4,5},{5,4},{6,7},{7,6},{8,9},{9,8},{10,11... | collective-permute-start | bytes 405512 | tf_op jit(solution)/shard_map/ppermute | solution.py:348
  51.2 1.5 %finish.4.refs_4_ = f32[256,2048]{1,0:T(8,128)} custom-call(f32[256,128]{1,0:T(8,128)S(1)} %get-tuple-element.40.row_coord, f32[256,128]{1,0:T(8,128)S(1)} %get-tuple-element.41.row_level, f32[8,256]{1,0:T(8,128)S(1)} %get-tuple-element.66.refs_0_, f32[256,256]{1,0:T(8,128)S(1)} %get-tuple-element.67.refs_1_, ...), custom_call_target="tpu_custom_call", output_to_operand_aliasing={{}: (8, {})} | custom-call | flops 1 | bytes 1 | tf_op jit(solution)/shard_map/finish/pallas_call | solution.py:310
  52.7 2.3 %collective-permute-done.11.refs_2_ = s32[264,128]{1,0:T(8,128)S(1)} collective-permute-done((s32[264,128]{1,0:T(8,128)S(1)}, s32[264,128]{1,0:T(8,128)S(1)}, u32[]{:S(2)}, u32[]{:S(2)}) %collective-permute-start.11) | collective-permute-done | bytes 135200 | tf_op jit(solution)/shard_map/ppermute | solution.py:348
  55.1 2.1 %collective-permute-done.12.refs_3_ = s32[264,128]{1,0:T(8,128)S(1)} collective-permute-done((s32[264,128]{1,0:T(8,128)S(1)}, s32[264,128]{1,0:T(8,128)S(1)}, u32[]{:S(2)}, u32[]{:S(2)}) %collective-permute-start.12) | collective-permute-done | bytes 135200 | tf_op jit(solution)/shard_map/ppermute | solution.py:348
  57.1 0.9 %finish.5 = f32[256,2048]{1,0:T(8,128)} custom-call(f32[256,128]{1,0:T(8,128)S(1)} %get-tuple-element.40.row_coord, f32[256,128]{1,0:T(8,128)S(1)} %get-tuple-element.41.row_level, f32[256,512]{1,0:T(8,128)S(1)} %weigh.1.refs_0_, f32[256,512]{1,0:T(8,128)S(1)} %get-tuple-element.63.refs_1_, ...), custom_call_target="tpu_custom_call", output_to_operand_aliasing={{}: (6, {})} | custom-call | flops 1 | bytes 1 | tf_op jit(solution)/shard_map/finish/pallas_call | solution.py:310
  (26 shorter events, 4.3 us)
Async XLA Ops:
  0.0 1.9 %copy-start = (bf16[1536,512]{1,0:T(8,128)(2,1)S(1)}, bf16[1536,512]{1,0:T(8,128)(2,1)}, u32[]{:S(2)}) copy-start(bf16[1536,512]{1,0:T(8,128)(2,1)} %x) | copy-start | bytes 4718596
  1.3 19.3 %collective-permute-start.3 = (bf16[1536,256]{1,0:T(8,128)(2,1)S(1)}, bf16[1536,256]{1,0:T(8,128)(2,1)S(1)}, u32[]{:S(2)}, u32[]{:S(2)}) collective-permute-start(bf16[1536,256]{1,0:T(8,128)(2,1)S(1)} %slice.9.low), channel_id=1, source_target_pairs={{0,4},{2,6},{4,0},{6,2},{8,12},{10,14},{12,8},{14,10},{16,20},{18,... | collective-permute-start | bytes 2359304 | tf_op jit(solution)/shard_map/ppermute | solution.py:337
  1.9 21.9 %collective-permute-start.1 = (bf16[1536,256]{1,0:T(8,128)(2,1)S(1)}, bf16[1536,256]{1,0:T(8,128)(2,1)S(1)}, u32[]{:S(2)}, u32[]{:S(2)}) collective-permute-start(bf16[1536,256]{1,0:T(8,128)(2,1)S(1)} %slice.9.low), channel_id=1, source_target_pairs={{0,26},{2,0},{4,30},{6,4},{8,2},{10,8},{12,6},{14,12},{16,10},{18,... | collective-permute-start | bytes 2359304 | tf_op jit(solution)/shard_map/ppermute | solution.py:337
  1.9 0.7 %copy-start.1 = (s32[512]{0:T(512)S(1)}, s32[512]{0:T(512)}, u32[]{:S(2)}) copy-start(s32[512]{0:T(512)} %param.4) | copy-start | bytes 6148
  2.8 23.4 %collective-permute-start.2 = (bf16[1552,256]{1,0:T(8,128)(2,1)S(1)}, bf16[1552,256]{1,0:T(8,128)(2,1)S(1)}, u32[]{:S(2)}, u32[]{:S(2)}) collective-permute-start(bf16[1552,256]{1,0:T(8,128)(2,1)S(1)} %get-tuple-element.39.high), channel_id=1, source_target_pairs={{0,26},{2,0},{4,30},{6,4},{8,2},{10,8},{12,6},{14,12},{16,10},{18,... | collective-permute-start | bytes 2383880 | tf_op jit(solution)/shard_map/ppermute | solution.py:337
  3.4 0.7 %copy-start.2 = (s32[512]{0:T(512)S(1)}, s32[512]{0:T(512)}, u32[]{:S(2)}) copy-start(s32[512]{0:T(512)} %param.4) | copy-start | bytes 6148
  4.1 0.7 %copy-start.3 = (s32[512]{0:T(512)S(1)}, s32[512]{0:T(512)}, u32[]{:S(2)}) copy-start(s32[512]{0:T(512)} %param.5) | copy-start | bytes 6148
  6.0 17.7 %collective-permute-start = (f32[256,512]{1,0:T(8,128)S(1)}, f32[256,512]{1,0:T(8,128)S(1)}, u32[]{:S(2)}, u32[]{:S(2)}) collective-permute-start(f32[256,512]{1,0:T(8,128)S(1)} %get-tuple-element.43), channel_id=1, source_target_pairs={{0,1},{1,0},{2,3},{3,2},{4,5},{5,4},{6,7},{7,6},{8,9},{9,8},{10,11... | collective-permute-start | bytes 1572872 | tf_op jit(solution)/shard_map/ppermute | solution.py:348
  20.7 16.4 %collective-permute-start.5 = (bf16[1552,128]{1,0:T(8,128)(2,1)S(1)}, bf16[1552,128]{1,0:T(8,128)(2,1)S(1)}, u32[]{:S(2)}, u32[]{:S(2)}) collective-permute-start(bf16[1552,128]{1,0:T(8,128)(2,1)S(1)} %get-tuple-element.49), channel_id=1, source_target_pairs={{0,28},{2,30},{4,0},{6,2},{8,4},{10,6},{12,8},{14,10},{16,12},{18,... | collective-permute-start | bytes 1191944 | tf_op jit(solution)/shard_map/ppermute | solution.py:337
  21.3 15.7 %collective-permute-start.4 = (bf16[1536,128]{1,0:T(8,128)(2,1)S(1)}, bf16[1536,128]{1,0:T(8,128)(2,1)S(1)}, u32[]{:S(2)}, u32[]{:S(2)}) collective-permute-start(bf16[1536,128]{1,0:T(8,128)(2,1)S(1)} %get-tuple-element.47.refs_0_.near0), channel_id=1, source_target_pairs={{4,28},{6,30},{12,4},{14,6},{20,12},{22,14},{28,20},{30,22},{5,29}... | collective-permute-start | bytes 1179656 | tf_op jit(solution)/shard_map/ppermute | solution.py:337
  23.7 19.4 %collective-permute-start.9 = (bf16[1552,128]{1,0:T(8,128)(2,1)S(1)}, bf16[1552,128]{1,0:T(8,128)(2,1)S(1)}, u32[]{:S(2)}, u32[]{:S(2)}) collective-permute-start(bf16[1552,128]{1,0:T(8,128)(2,1)S(1)} %get-tuple-element.59), channel_id=1, source_target_pairs={{0,28},{2,30},{4,0},{6,2},{8,4},{10,6},{12,8},{14,10},{16,12},{18,... | collective-permute-start | bytes 1191944 | tf_op jit(solution)/shard_map/ppermute | solution.py:337
  23.8 19.4 %collective-permute-start.8 = (bf16[1536,128]{1,0:T(8,128)(2,1)S(1)}, bf16[1536,128]{1,0:T(8,128)(2,1)S(1)}, u32[]{:S(2)}, u32[]{:S(2)}) collective-permute-start(bf16[1536,128]{1,0:T(8,128)(2,1)S(1)} %get-tuple-element.57.near1), channel_id=1, source_target_pairs={{4,28},{6,30},{12,4},{14,6},{20,12},{22,14},{28,20},{30,22},{5,29}... | collective-permute-start | bytes 1179656 | tf_op jit(solution)/shard_map/ppermute | solution.py:337
  27.2 12.1 %collective-permute-start.6 = (s32[264,256]{1,0:T(8,128)S(1)}, s32[264,256]{1,0:T(8,128)S(1)}, u32[]{:S(2)}, u32[]{:S(2)}) collective-permute-start(s32[264,256]{1,0:T(8,128)S(1)} %get-tuple-element.54), channel_id=1, source_target_pairs={{0,1},{1,0},{2,3},{3,2},{4,5},{5,4},{6,7},{7,6},{8,9},{9,8},{10,11... | collective-permute-start | bytes 811016 | tf_op jit(solution)/shard_map/ppermute | solution.py:348
  37.7 5.1 %collective-permute-start.7 = (s32[264,128]{1,0:T(8,128)S(1)}, s32[264,128]{1,0:T(8,128)S(1)}, u32[]{:S(2)}, u32[]{:S(2)}) collective-permute-start(s32[264,128]{1,0:T(8,128)S(1)} %get-tuple-element.55), channel_id=1, source_target_pairs={{0,1},{1,0},{2,3},{3,2},{4,5},{5,4},{6,7},{7,6},{8,9},{9,8},{10,11... | collective-permute-start | bytes 405512 | tf_op jit(solution)/shard_map/ppermute | solution.py:348
  44.0 3.5 %collective-permute-start.10 = (bf16[1552,512]{1,0:T(8,128)(2,1)S(1)}, bf16[1552,512]{1,0:T(8,128)(2,1)S(1)}, u32[]{:S(2)}, u32[]{:S(2)}) collective-permute-start(bf16[1552,512]{1,0:T(8,128)(2,1)S(1)} %get-tuple-element.60), channel_id=1, source_target_pairs={{0,2},{2,0},{4,6},{6,4},{8,10},{10,8},{12,14},{14,12},{16,18},{18,... | collective-permute-start | bytes 4767752 | tf_op jit(solution)/shard_map/ppermute | solution.py:337
  44.1 7.1 %collective-permute-start.13 = (s32[264,128]{1,0:T(8,128)S(1)}, s32[264,128]{1,0:T(8,128)S(1)}, u32[]{:S(2)}, u32[]{:S(2)}) collective-permute-start(s32[264,128]{1,0:T(8,128)S(1)} %get-tuple-element.70), channel_id=1, source_target_pairs={{0,1},{1,0},{2,3},{3,2},{4,5},{5,4},{6,7},{7,6},{8,9},{9,8},{10,11... | collective-permute-start | bytes 405512 | tf_op jit(solution)/shard_map/ppermute | solution.py:348
  48.6 6.5 %collective-permute-start.11 = (s32[264,128]{1,0:T(8,128)S(1)}, s32[264,128]{1,0:T(8,128)S(1)}, u32[]{:S(2)}, u32[]{:S(2)}) collective-permute-start(s32[264,128]{1,0:T(8,128)S(1)} %get-tuple-element.64), channel_id=1, source_target_pairs={{0,1},{1,0},{2,3},{3,2},{4,5},{5,4},{6,7},{7,6},{8,9},{9,8},{10,11... | collective-permute-start | bytes 405512 | tf_op jit(solution)/shard_map/ppermute | solution.py:348
  50.2 7.0 %collective-permute-start.12 = (s32[264,128]{1,0:T(8,128)S(1)}, s32[264,128]{1,0:T(8,128)S(1)}, u32[]{:S(2)}, u32[]{:S(2)}) collective-permute-start(s32[264,128]{1,0:T(8,128)S(1)} %get-tuple-element.65), channel_id=1, source_target_pairs={{0,1},{1,0},{2,3},{3,2},{4,5},{5,4},{6,7},{7,6},{8,9},{9,8},{10,11... | collective-permute-start | bytes 405512 | tf_op jit(solution)/shard_map/ppermute | solution.py:348

commit v8 on v6

--- a/solution.py
+++ b/solution.py
@@ -39,7 +39,7 @@
     return jnp.where(r <= 1.0, near, jnp.where(r <= 2.0, far, 0.0))
 
 
-def prepare_kernel(x, coord, high):
+def prepare_kernel(x, coord, high, *parts):
     members, width = x.shape
     half = width // 2
     first = 4 * width * lax.axis_index("mesh")
@@ -50,12 +50,24 @@
         [jnp.broadcast_to(jitter[:, :half], (PAD // 2, half)), jnp.broadcast_to(jitter[:, half:], (PAD // 2, half))],
         axis=0,
     ).astype(x.dtype)
+    cut_kernel(high, *parts)
+
+
+def cut_kernel(whole, *parts):
+    wide = parts[0].shape[1]
+    for i, part in enumerate(parts):
+        part[...] = whole[:, i * wide : (i + 1) * wide]
+
+
+def cut(panel):
+    half = jax.ShapeDtypeStruct((panel.shape[0], panel.shape[1] // 2), panel.dtype)
+    return call(cut_kernel, [half] * 2, panel, name="cut")
 
 
 def prepare(x, coord):
     members, width = x.shape
-    half = jax.ShapeDtypeStruct((members + PAD, width // 2), x.dtype)
-    return call(prepare_kernel, [half], x, coord, name="prepare")[0]
+    outs = [jax.ShapeDtypeStruct((members + PAD, w), x.dtype) for w in (width // 2, width // 4, width // 4)]
+    return call(prepare_kernel, outs, x, coord, name="prepare")
 
 
 def own_kernel(low, high, coord, level, lt, row_coord, row_level, *outs, owned, split):
@@ -183,7 +195,6 @@
         lt,
         *panels,
         name="panel_tile",
-        flops=2 * members * width * wide,
     )
 
 
@@ -201,11 +212,11 @@
     return gc_taper(dist * (1.0 / (12 * width))) * (1.0 / (members - 1))
 
 
-def weigh_kernel(row_coord, cols, out, *, kind, period, width, members):
+def weigh_kernel(row_coord, cols, out, *, kind, starts, period, width, members):
     step = panel_steps()[kind]
-    for at in range(0, out.shape[1], CHUNK):
-        span = slice(at, at + CHUNK)
-        out[:, span] = weight(cols[0:1, span], row_coord[...], step, at, period, width, members)
+    for block, begin in enumerate(starts):
+        span = slice(block * CHUNK, (block + 1) * CHUNK)
+        out[:, span] = weight(cols[0:1, span], row_coord[...], step, begin, period, width, members)
 
 
 def finish_kernel(row_coord, row_level, *refs, plan, period, width, members):
@@ -214,17 +225,19 @@
     coord, level = row_coord[...], row_level[...]
     copies = []
     at = 0
-    for n, kind in plan:
+    for n, kind, starts in plan:
         cols, parts = refs[at], refs[at + 1 : at + 1 + n]
         at += 1 + n
         step = steps[kind]
-        for begin in range(0, width, CHUNK):
-            span = slice(begin, begin + CHUNK)
+        for block, begin in enumerate(starts):
+            span = slice(block * CHUNK, (block + 1) * CHUNK)
             slot = len(copies)
             raw = parts[0][:, span]
-            for part in parts[1:]:
+            if len(parts) > 1:
+                share = len(starts) // (len(parts) - 1)
+                part = parts[1 + block // share]
                 if part.dtype == jnp.int32:
-                    raw = raw + unpack(part, begin // CHUNK, raw.shape[0])
+                    raw = raw + unpack(part, block % share, raw.shape[0])
                 else:
                     raw = raw + part[:, span]
             if cols.shape[0] == out.shape[0]:
@@ -244,10 +257,10 @@
 def finish(row_coord, row_level, groups, out, shape, period, width, members):
     operands = [row_coord, row_level]
     plan = []
-    for cols, parts, kind in groups:
+    for cols, parts, kind, starts in groups:
         operands += [cols, *parts]
-        plan.append((len(parts), kind))
-    copies = len(plan) * (width // CHUNK)
+        plan.append((len(parts), kind, starts))
+    copies = sum(len(starts) for _, _, starts in plan)
     specs = [VMEM] * len(operands)
     aliases = {}
     if out is not None:
@@ -292,20 +305,21 @@
 
     def reduced(parts):
         if split:
-            return [parts[1], lax.ppermute(parts[0], "mem", [(0, 1), (1, 0)])]
+            return [parts[-1]] + [lax.ppermute(a, "mem", [(0, 1), (1, 0)]) for a in parts[:-1]]
         return [lax.psum_scatter(parts[0], "mem", scatter_dimension=0, tiled=True)]
 
     half = width // 2
     low = perturbations[:, :half]
-    high = prepare(after(perturbations, low), coord)
+    high, *highs = prepare(after(perturbations, low), coord)
     lt, row_coord, row_level, *own = own_tile(low, high, coord, levels, owned, rows)
     own_parts = reduced(own)
     own_cols = jnp.concatenate([high[members : members + PAD // 2], high[members + PAD // 2 :]], axis=1).astype(F32)
 
     first = permute(low, swap_x)
     extra = [permute(a, extra_pairs) for a in (low, high)]
-    straight = permute(after(high, first), back_two)
-    passed = permute(first, relay)
+    straight = [permute(after(a, first), back_two) for a in highs]
+    near = cut(first)
+    passed = [permute(a, relay) for a in near]
 
     def tile(panels, picks, *tokens, keep=False):
         return panel_tile(after(lt, *tokens), panels, picks, rows, keep)
@@ -316,21 +330,36 @@
 
     extra_cols, *extra_parts = tile(extra, [[0, 1]], own_parts[-1])
     extra_parts = reduced(extra_parts)
-    out = finished(None, extra_cols, (own_cols, own_parts, "own"), (extra_cols, extra_parts, "extra"))
-    two_cols, *two_parts, two = tile([first, passed, straight], [[0, 2], [1, 2]], out, keep=True)
-    two_parts = reduced(two_parts)
-    other = permute(two, siblings)
-    other_cols, *other_parts = tile([other], [[0]])
-    other_parts = reduced(other_parts)
+    whole = [i * CHUNK for i in range(width // CHUNK)]
+    places = [whole[::2], whole[1::2]]
+    sides = [[0, 2], [1, 2]]
+    cols0, *parts0, two0 = tile([near[0], passed[0], straight[0]], sides, extra_cols, keep=True)
+    parts0 = reduced(parts0)
+    out = finished(None, cols0, (own_cols, own_parts, "own", whole), (extra_cols, extra_parts, "extra", whole))
+    cols1, *parts1, two1 = tile([near[1], passed[1], straight[1]], sides, out, parts0[-1], keep=True)
+    parts1 = reduced(parts1)
+    other0, other1 = permute(two0, siblings), permute(two1, siblings)
+    other_cols0, *other_parts0 = tile([other0], [[0]], cols1)
+    other_parts0 = reduced(other_parts0)
+    other_cols1, *other_parts1 = tile([other1], [[0]], other_cols0)
+    other_parts1 = reduced(other_parts1)
     weights = call(
-        functools.partial(weigh_kernel, kind="other", period=period, width=width, members=everyone),
-        [jax.ShapeDtypeStruct((owned, width), F32)],
+        functools.partial(
+            weigh_kernel, kind="other", starts=places[1], period=period, width=width, members=everyone
+        ),
+        [jax.ShapeDtypeStruct((owned, half), F32)],
         row_coord,
-        other_cols,
+        other_cols1,
         name="weigh",
     )[0]
-    out = finished(out, weights, (two_cols, two_parts, "two"))
-    return finished(out, other_cols, (weights, other_parts, "other"))
+    out = finished(
+        out,
+        weights,
+        (cols0, parts0, "two", places[0]),
+        (cols1, parts1, "two", places[1]),
+        (other_cols0, other_parts0, "other", places[0]),
+    )
+    return finished(out, other_cols1, (weights, other_parts1, "other", places[1]))
 
 
 def solution(mesh):

time: 60 us -> 56.8 us (0.947)
  waiting for transfers between devices: 37.5 us -> 27.6 us
  starting transfers between devices: 10.6 us -> 15.2 us
  local copies, waits for them, and re-layouts: 1.99 us -> 3.35 us
  Pallas kernels: 9.59 us -> 10.3 us
    ppermute x4 -> x6, waiting for transfers between devices: 13.9 us -> 6 us  [reduced(): lax.ppermute(a, 'mem', [(0, 1), (1, 0)])]
    ppermute x6 -> x9, starting transfers between devices: 4.16 us -> 6.6 us  [permute(): return lax.ppermute(array, 'mesh', pairs)]
    ppermute x4 -> x6, starting transfers between devices: 6.4 us -> 8.57 us  [reduced(): lax.ppermute(a, 'mem', [(0, 1), (1, 0)])]
    ppermute x6 -> x9, waiting for transfers between devices: 23.6 us -> 21.6 us  [permute(): return lax.ppermute(array, 'mesh', pairs)]
    unnamed x6 -> x8, local copies, waits for them, and re-layouts: 0.69 us -> 2.05 us
    pallas_call x6 -> x9, Pallas kernels: 5.06 us -> 5.49 us  [call(): pl.pallas_call(kernel, out_shape=outs, in_specs=[VMEM] * len(operands), o...]
  transfers between devices with their start and end apart: 10 -> 15, of which waited for: 6 -> 7; matrix products, arithmetic and copies ran while one was open for 0% -> 0% of each run, Pallas kernels for 13% -> 17%
where the time goes in v8:
time: 56.8 us; the launch traced here: 56.5 us
  waiting for transfers between devices  27.6 us (49%)
  starting transfers between devices  15.2 us (27%)
  Pallas kernels  10.3 us (18%)
  local copies, waits for them, and re-layouts  3.35 us (6%)
    ppermute x9, waiting for transfers between devices, permute(): return lax.ppermute(array, 'mesh', pairs)  21.6 us
    ppermute x6, starting transfers between devices, reduced(): lax.ppermute(a, 'mem', [(0, 1), (1, 0)])  8.57 us
    ppermute x9, starting transfers between devices, permute(): return lax.ppermute(array, 'mesh', pairs)  6.6 us
    ppermute x6, waiting for transfers between devices, reduced(): lax.ppermute(a, 'mem', [(0, 1), (1, 0)])  6 us
    pallas_call x9, Pallas kernels, call(): pl.pallas_call(kernel, out_shape=outs, in_specs=[VMEM] * len(operands), o...  5.49 us
    pallas_call x3, Pallas kernels, finish(): pl.pallas_call(functools.partial(finish_kernel, plan=plan, period=period,...  4.8 us
    unnamed x8, local copies, waits for them, and re-layouts  2.05 us
    slice x1, local copies, waits for them, and re-layouts, per_device(): low = perturbations[:, :half]  1.3 us
  transfers between devices with their start and end apart: 15, of which 7 were waited for; matrix products, arithmetic and copies ran while one was open for 0% of the time, Pallas kernels for 17%

profile of v8, /device:TPU:26, one launch (start us, length us, event | category | flops | bytes accessed | tf_op | source)
XLA Modules:
  0.0 56.5 jit_solution(11575977056495652636)
XLA Ops:
  0.0 1.3 %slice.9.low = bf16[1536,256]{1,0:T(8,128)(2,1)S(1)} slice(bf16[1536,512]{1,0:T(8,128)(2,1)} %x), slice={[0:1536], [0:256]} | slice | bytes 1572864 | tf_op jit(solution)/shard_map/slice | solution.py:312
  1.9 0.7 %copy-done.1 = s32[512]{0:T(512)S(1)} copy-done((s32[512]{0:T(512)S(1)}, s32[512]{0:T(512)}, u32[]{:S(2)}) %copy-start.1) | copy-done | bytes 2072
  2.8 0.6 %collective-permute-start.2 = (bf16[1552,256]{1,0:T(8,128)(2,1)S(1)}, bf16[1552,256]{1,0:T(8,128)(2,1)S(1)}, u32[]{:S(2)}, u32[]{:S(2)}) collective-permute-start(bf16[1552,256]{1,0:T(8,128)(2,1)S(1)} %get-tuple-element.44.high), channel_id=1, source_target_pairs={{0,26},{2,0},{4,30},{6,4},{8,2},{10,8},{12,6},{14,12},{16,10},{18,... | collective-permute-start | bytes 2383880 | tf_op jit(solution)/shard_map/ppermute | solution.py:297
  3.4 0.7 %copy-done.2 = s32[512]{0:T(512)S(1)} copy-done((s32[512]{0:T(512)S(1)}, s32[512]{0:T(512)}, u32[]{:S(2)}) %copy-start.2) | copy-done | bytes 2072
  4.1 0.7 %copy-done.3 = s32[512]{0:T(512)S(1)} copy-done((s32[512]{0:T(512)S(1)}, s32[512]{0:T(512)}, u32[]{:S(2)}) %copy-start.3) | copy-done | bytes 2072
  4.8 1.2 %own_tile.1 = (bf16[512,1536]{1,0:T(8,128)(2,1)S(1)}, f32[256,128]{1,0:T(8,128)S(1)}, f32[256,128]{1,0:T(8,128)S(1)}, f32[256,512]{1,0:T(8,128)S(1)}, f32[256,512]{1,0:T(8,128)S(1)}) custom-call(bf16[1536,256]{1,0:T(8,128)(2,1)S(1)} %slice.9.low, bf16[1552,256]{1,0:T(8,128)(2,1)S(1)} %get-tuple-element.44.high, s32[1,512]{1,0:T(1,128)S(1)} %bitcast.3, ...), custom_call_target="tpu_custom_call" | custom-call | flops 1 | bytes 1 | tf_op jit(solution)/shard_map/own_tile/pallas_call | solution.py:24
  6.0 1.7 %collective-permute-start = (f32[256,512]{1,0:T(8,128)S(1)}, f32[256,512]{1,0:T(8,128)S(1)}, u32[]{:S(2)}, u32[]{:S(2)}) collective-permute-start(f32[256,512]{1,0:T(8,128)S(1)} %get-tuple-element.48), channel_id=1, source_target_pairs={{0,1},{1,0},{2,3},{3,2},{4,5},{5,4},{6,7},{7,6},{8,9},{9,8},{10,11... | collective-permute-start | bytes 1572872 | tf_op jit(solution)/shard_map/ppermute | solution.py:308
  7.7 13.0 %collective-permute-done.3.whole = bf16[1536,256]{1,0:T(8,128)(2,1)S(1)} collective-permute-done((bf16[1536,256]{1,0:T(8,128)(2,1)S(1)}, bf16[1536,256]{1,0:T(8,128)(2,1)S(1)}, u32[]{:S(2)}, u32[]{:S(2)}) %collective-permute-start.3) | collective-permute-done | bytes 786464 | tf_op jit(solution)/shard_map/ppermute | solution.py:297
  21.3 2.4 %collective-permute-start.4 = (bf16[1536,128]{1,0:T(8,128)(2,1)S(1)}, bf16[1536,128]{1,0:T(8,128)(2,1)S(1)}, u32[]{:S(2)}, u32[]{:S(2)}) collective-permute-start(bf16[1536,128]{1,0:T(8,128)(2,1)S(1)} %get-tuple-element.52.refs_0_), channel_id=1, source_target_pairs={{4,28},{6,30},{12,4},{14,6},{20,12},{22,14},{28,20},{30,22},{5,29}... | collective-permute-start | bytes 1179656 | tf_op jit(solution)/shard_map/ppermute | solution.py:297
  23.8 2.4 %collective-permute-start.8 = (bf16[1536,128]{1,0:T(8,128)(2,1)S(1)}, bf16[1536,128]{1,0:T(8,128)(2,1)S(1)}, u32[]{:S(2)}, u32[]{:S(2)}) collective-permute-start(bf16[1536,128]{1,0:T(8,128)(2,1)S(1)} %get-tuple-element.62.refs_0_), channel_id=1, source_target_pairs={{4,28},{6,30},{12,4},{14,6},{20,12},{22,14},{28,20},{30,22},{5,29}... | collective-permute-start | bytes 1179656 | tf_op jit(solution)/shard_map/ppermute | solution.py:297
  26.2 1.0 %panel_tile.5 = (f32[8,512]{1,0:T(8,128)S(1)}, s32[264,256]{1,0:T(8,128)S(1)}, f32[256,512]{1,0:T(8,128)S(1)}) custom-call(bf16[512,1536]{1,0:T(8,128)(2,1)S(1)} %get-tuple-element.69.lt, bf16[1536,256]{1,0:T(8,128)(2,1)S(1)} %collective-permute-done.1.refs_0_, bf16[1552,256]{1,0:T(8,128)(2,1)S(1)} %collective-permute-done.2.refs_1_), custom_call_target="tpu_custom_call" | custom-call | flops 1 | bytes 1 | tf_op jit(solution)/shard_map/panel_tile/pallas_call | solution.py:24
  27.2 1.6 %collective-permute-start.6 = (s32[264,256]{1,0:T(8,128)S(1)}, s32[264,256]{1,0:T(8,128)S(1)}, u32[]{:S(2)}, u32[]{:S(2)}) collective-permute-start(s32[264,256]{1,0:T(8,128)S(1)} %get-tuple-element.59), channel_id=1, source_target_pairs={{0,1},{1,0},{2,3},{3,2},{4,5},{5,4},{6,7},{7,6},{8,9},{9,8},{10,11... | collective-permute-start | bytes 811016 | tf_op jit(solution)/shard_map/ppermute | solution.py:308
  28.8 8.3 %collective-permute-done.4.refs_1_ = bf16[1536,128]{1,0:T(8,128)(2,1)S(1)} collective-permute-done((bf16[1536,128]{1,0:T(8,128)(2,1)S(1)}, bf16[1536,128]{1,0:T(8,128)(2,1)S(1)}, u32[]{:S(2)}, u32[]{:S(2)}) %collective-permute-start.4) | collective-permute-done | bytes 393248 | tf_op jit(solution)/shard_map/ppermute | solution.py:297
  37.1 0.7 %panel_tile.6 = (f32[8,256]{1,0:T(8,128)S(1)}, s32[264,128]{1,0:T(8,128)S(1)}, f32[256,256]{1,0:T(8,128)S(1)}, bf16[1552,256]{1,0:T(8,128)(2,1)S(1)}) custom-call(bf16[512,1536]{1,0:T(8,128)(2,1)S(1)} %get-tuple-element.69.lt, bf16[1536,128]{1,0:T(8,128)(2,1)S(1)} %get-tuple-element.52.refs_0_, bf16[1536,128]{1,0:T(8,128)(2,1)S(1)} %collective-permute-done.4.refs_1_, ...), custom_call_target="tpu_custom_call" | custom-call | flops 1 | bytes 1 | tf_op jit(solution)/shard_map/panel_tile/pallas_call | solution.py:24
  37.8 1.6 %collective-permute-start.7 = (s32[264,128]{1,0:T(8,128)S(1)}, s32[264,128]{1,0:T(8,128)S(1)}, u32[]{:S(2)}, u32[]{:S(2)}) collective-permute-start(s32[264,128]{1,0:T(8,128)S(1)} %get-tuple-element.60), channel_id=1, source_target_pairs={{0,1},{1,0},{2,3},{3,2},{4,5},{5,4},{6,7},{7,6},{8,9},{9,8},{10,11... | collective-permute-start | bytes 405512 | tf_op jit(solution)/shard_map/ppermute | solution.py:308
  39.4 2.2 %finish.3.refs_9_ = f32[256,2048]{1,0:T(8,128)} custom-call(f32[256,128]{1,0:T(8,128)S(1)} %get-tuple-element.45.row_coord, f32[256,128]{1,0:T(8,128)S(1)} %get-tuple-element.46.row_level, f32[8,512]{1,0:T(8,128)S(1)} %maximum_convert_fusion.refs_0_, f32[256,512]{1,0:T(8,128)S(1)} %get-tuple-element.57.refs_1_, f32[256,512]{1,0:T(8,128)S(1)} %collective-permute-done.refs_2_, ...), custom_call_target="tpu_custom_call" | custom-call | flops 1 | bytes 1 | tf_op jit(solution)/shard_map/finish/pallas_call | solution.py:270
  41.6 1.3 %collective-permute-done.7.refs_2_ = s32[264,128]{1,0:T(8,128)S(1)} collective-permute-done((s32[264,128]{1,0:T(8,128)S(1)}, s32[264,128]{1,0:T(8,128)S(1)}, u32[]{:S(2)}, u32[]{:S(2)}) %collective-permute-start.7) | collective-permute-done | bytes 135200 | tf_op jit(solution)/shard_map/ppermute | solution.py:308
  43.2 0.7 %panel_tile.7 = (f32[8,256]{1,0:T(8,128)S(1)}, s32[264,128]{1,0:T(8,128)S(1)}, f32[256,256]{1,0:T(8,128)S(1)}, bf16[1552,256]{1,0:T(8,128)(2,1)S(1)}) custom-call(bf16[512,1536]{1,0:T(8,128)(2,1)S(1)} %get-tuple-element.69.lt, bf16[1536,128]{1,0:T(8,128)(2,1)S(1)} %get-tuple-element.62.refs_0_, bf16[1536,128]{1,0:T(8,128)(2,1)S(1)} %collective-permute-done.8.refs_1_, ...), custom_call_target="tpu_custom_call" | custom-call | flops 1 | bytes 1 | tf_op jit(solution)/shard_map/panel_tile/pallas_call | solution.py:24
  44.0 1.6 %collective-permute-start.13 = (s32[264,128]{1,0:T(8,128)S(1)}, s32[264,128]{1,0:T(8,128)S(1)}, u32[]{:S(2)}, u32[]{:S(2)}) collective-permute-start(s32[264,128]{1,0:T(8,128)S(1)} %get-tuple-element.78), channel_id=1, source_target_pairs={{0,1},{1,0},{2,3},{3,2},{4,5},{5,4},{6,7},{7,6},{8,9},{9,8},{10,11... | collective-permute-start | bytes 405512 | tf_op jit(solution)/shard_map/ppermute | solution.py:308
  47.3 1.6 %collective-permute-start.12 = (s32[264,128]{1,0:T(8,128)S(1)}, s32[264,128]{1,0:T(8,128)S(1)}, u32[]{:S(2)}, u32[]{:S(2)}) collective-permute-start(s32[264,128]{1,0:T(8,128)S(1)} %get-tuple-element.74), channel_id=1, source_target_pairs={{0,1},{1,0},{2,3},{3,2},{4,5},{5,4},{6,7},{7,6},{8,9},{9,8},{10,11... | collective-permute-start | bytes 405512 | tf_op jit(solution)/shard_map/ppermute | solution.py:308
  49.2 1.2 %collective-permute-done.13.refs_5_ = s32[264,128]{1,0:T(8,128)S(1)} collective-permute-done((s32[264,128]{1,0:T(8,128)S(1)}, s32[264,128]{1,0:T(8,128)S(1)}, u32[]{:S(2)}, u32[]{:S(2)}) %collective-permute-start.13) | collective-permute-done | bytes 135200 | tf_op jit(solution)/shard_map/ppermute | solution.py:308
  50.4 2.9 %collective-permute-done.14.refs_8_ = s32[264,128]{1,0:T(8,128)S(1)} collective-permute-done((s32[264,128]{1,0:T(8,128)S(1)}, s32[264,128]{1,0:T(8,128)S(1)}, u32[]{:S(2)}, u32[]{:S(2)}) %collective-permute-start.14) | collective-permute-done | bytes 135200 | tf_op jit(solution)/shard_map/ppermute | solution.py:308
  53.3 1.9 %finish.4.refs_3_ = f32[256,2048]{1,0:T(8,128)} custom-call(f32[256,128]{1,0:T(8,128)S(1)} %get-tuple-element.45.row_coord, f32[256,128]{1,0:T(8,128)S(1)} %get-tuple-element.46.row_level, f32[8,256]{1,0:T(8,128)S(1)} %get-tuple-element.75.refs_0_, f32[256,256]{1,0:T(8,128)S(1)} %get-tuple-element.76.refs_1_, ...), custom_call_target="tpu_custom_call", output_to_operand_aliasing={{}: (11, {})} | custom-call | flops 1 | bytes 1 | tf_op jit(solution)/shard_map/finish/pallas_call | solution.py:270
  55.8 0.8 %finish.5 = f32[256,2048]{1,0:T(8,128)} custom-call(f32[256,128]{1,0:T(8,128)S(1)} %get-tuple-element.45.row_coord, f32[256,128]{1,0:T(8,128)S(1)} %get-tuple-element.46.row_level, f32[256,256]{1,0:T(8,128)S(1)} %weigh.1.refs_0_, f32[256,256]{1,0:T(8,128)S(1)} %get-tuple-element.73.refs_1_, ...), custom_call_target="tpu_custom_call", output_to_operand_aliasing={{}: (5, {})} | custom-call | flops 1 | bytes 1 | tf_op jit(solution)/shard_map/finish/pallas_call | solution.py:270
  (29 shorter events, 4.5 us)
Async XLA Ops:
  0.0 1.9 %copy-start = (bf16[1536,512]{1,0:T(8,128)(2,1)S(1)}, bf16[1536,512]{1,0:T(8,128)(2,1)}, u32[]{:S(2)}) copy-start(bf16[1536,512]{1,0:T(8,128)(2,1)} %x) | copy-start | bytes 4718596
  1.3 19.3 %collective-permute-start.3 = (bf16[1536,256]{1,0:T(8,128)(2,1)S(1)}, bf16[1536,256]{1,0:T(8,128)(2,1)S(1)}, u32[]{:S(2)}, u32[]{:S(2)}) collective-permute-start(bf16[1536,256]{1,0:T(8,128)(2,1)S(1)} %slice.9.low), channel_id=1, source_target_pairs={{0,4},{2,6},{4,0},{6,2},{8,12},{10,14},{12,8},{14,10},{16,20},{18,... | collective-permute-start | bytes 2359304 | tf_op jit(solution)/shard_map/ppermute | solution.py:297
  1.9 21.9 %collective-permute-start.1 = (bf16[1536,256]{1,0:T(8,128)(2,1)S(1)}, bf16[1536,256]{1,0:T(8,128)(2,1)S(1)}, u32[]{:S(2)}, u32[]{:S(2)}) collective-permute-start(bf16[1536,256]{1,0:T(8,128)(2,1)S(1)} %slice.9.low), channel_id=1, source_target_pairs={{0,26},{2,0},{4,30},{6,4},{8,2},{10,8},{12,6},{14,12},{16,10},{18,... | collective-permute-start | bytes 2359304 | tf_op jit(solution)/shard_map/ppermute | solution.py:297
  1.9 0.7 %copy-start.1 = (s32[512]{0:T(512)S(1)}, s32[512]{0:T(512)}, u32[]{:S(2)}) copy-start(s32[512]{0:T(512)} %param.4) | copy-start | bytes 6148
  2.8 23.4 %collective-permute-start.2 = (bf16[1552,256]{1,0:T(8,128)(2,1)S(1)}, bf16[1552,256]{1,0:T(8,128)(2,1)S(1)}, u32[]{:S(2)}, u32[]{:S(2)}) collective-permute-start(bf16[1552,256]{1,0:T(8,128)(2,1)S(1)} %get-tuple-element.44.high), channel_id=1, source_target_pairs={{0,26},{2,0},{4,30},{6,4},{8,2},{10,8},{12,6},{14,12},{16,10},{18,... | collective-permute-start | bytes 2383880 | tf_op jit(solution)/shard_map/ppermute | solution.py:297
  3.4 0.7 %copy-start.2 = (s32[512]{0:T(512)S(1)}, s32[512]{0:T(512)}, u32[]{:S(2)}) copy-start(s32[512]{0:T(512)} %param.4) | copy-start | bytes 6148
  4.1 0.7 %copy-start.3 = (s32[512]{0:T(512)S(1)}, s32[512]{0:T(512)}, u32[]{:S(2)}) copy-start(s32[512]{0:T(512)} %param.5) | copy-start | bytes 6148
  6.0 17.7 %collective-permute-start = (f32[256,512]{1,0:T(8,128)S(1)}, f32[256,512]{1,0:T(8,128)S(1)}, u32[]{:S(2)}, u32[]{:S(2)}) collective-permute-start(f32[256,512]{1,0:T(8,128)S(1)} %get-tuple-element.48), channel_id=1, source_target_pairs={{0,1},{1,0},{2,3},{3,2},{4,5},{5,4},{6,7},{7,6},{8,9},{9,8},{10,11... | collective-permute-start | bytes 1572872 | tf_op jit(solution)/shard_map/ppermute | solution.py:308
  20.7 16.4 %collective-permute-start.5 = (bf16[1552,128]{1,0:T(8,128)(2,1)S(1)}, bf16[1552,128]{1,0:T(8,128)(2,1)S(1)}, u32[]{:S(2)}, u32[]{:S(2)}) collective-permute-start(bf16[1552,128]{1,0:T(8,128)(2,1)S(1)} %get-tuple-element.54), channel_id=1, source_target_pairs={{0,28},{2,30},{4,0},{6,2},{8,4},{10,6},{12,8},{14,10},{16,12},{18,... | collective-permute-start | bytes 1191944 | tf_op jit(solution)/shard_map/ppermute | solution.py:297
  21.3 15.7 %collective-permute-start.4 = (bf16[1536,128]{1,0:T(8,128)(2,1)S(1)}, bf16[1536,128]{1,0:T(8,128)(2,1)S(1)}, u32[]{:S(2)}, u32[]{:S(2)}) collective-permute-start(bf16[1536,128]{1,0:T(8,128)(2,1)S(1)} %get-tuple-element.52.refs_0_), channel_id=1, source_target_pairs={{4,28},{6,30},{12,4},{14,6},{20,12},{22,14},{28,20},{30,22},{5,29}... | collective-permute-start | bytes 1179656 | tf_op jit(solution)/shard_map/ppermute | solution.py:297
  23.7 19.4 %collective-permute-start.9 = (bf16[1552,128]{1,0:T(8,128)(2,1)S(1)}, bf16[1552,128]{1,0:T(8,128)(2,1)S(1)}, u32[]{:S(2)}, u32[]{:S(2)}) collective-permute-start(bf16[1552,128]{1,0:T(8,128)(2,1)S(1)} %get-tuple-element.64), channel_id=1, source_target_pairs={{0,28},{2,30},{4,0},{6,2},{8,4},{10,6},{12,8},{14,10},{16,12},{18,... | collective-permute-start | bytes 1191944 | tf_op jit(solution)/shard_map/ppermute | solution.py:297
  23.8 19.4 %collective-permute-start.8 = (bf16[1536,128]{1,0:T(8,128)(2,1)S(1)}, bf16[1536,128]{1,0:T(8,128)(2,1)S(1)}, u32[]{:S(2)}, u32[]{:S(2)}) collective-permute-start(bf16[1536,128]{1,0:T(8,128)(2,1)S(1)} %get-tuple-element.62.refs_0_), channel_id=1, source_target_pairs={{4,28},{6,30},{12,4},{14,6},{20,12},{22,14},{28,20},{30,22},{5,29}... | collective-permute-start | bytes 1179656 | tf_op jit(solution)/shard_map/ppermute | solution.py:297
  27.2 12.2 %collective-permute-start.6 = (s32[264,256]{1,0:T(8,128)S(1)}, s32[264,256]{1,0:T(8,128)S(1)}, u32[]{:S(2)}, u32[]{:S(2)}) collective-permute-start(s32[264,256]{1,0:T(8,128)S(1)} %get-tuple-element.59), channel_id=1, source_target_pairs={{0,1},{1,0},{2,3},{3,2},{4,5},{5,4},{6,7},{7,6},{8,9},{9,8},{10,11... | collective-permute-start | bytes 811016 | tf_op jit(solution)/shard_map/ppermute | solution.py:308
  37.8 5.1 %collective-permute-start.7 = (s32[264,128]{1,0:T(8,128)S(1)}, s32[264,128]{1,0:T(8,128)S(1)}, u32[]{:S(2)}, u32[]{:S(2)}) collective-permute-start(s32[264,128]{1,0:T(8,128)S(1)} %get-tuple-element.60), channel_id=1, source_target_pairs={{0,1},{1,0},{2,3},{3,2},{4,5},{5,4},{6,7},{7,6},{8,9},{9,8},{10,11... | collective-permute-start | bytes 405512 | tf_op jit(solution)/shard_map/ppermute | solution.py:308
  39.4 6.2 %collective-permute-start.10 = (bf16[1552,256]{1,0:T(8,128)(2,1)S(1)}, bf16[1552,256]{1,0:T(8,128)(2,1)S(1)}, u32[]{:S(2)}, u32[]{:S(2)}) collective-permute-start(bf16[1552,256]{1,0:T(8,128)(2,1)S(1)} %get-tuple-element.67), channel_id=1, source_target_pairs={{0,2},{2,0},{4,6},{6,4},{8,10},{10,8},{12,14},{14,12},{16,18},{18,... | collective-permute-start | bytes 2383880 | tf_op jit(solution)/shard_map/ppermute | solution.py:297
  43.9 2.8 %collective-permute-start.11 = (bf16[1552,256]{1,0:T(8,128)(2,1)S(1)}, bf16[1552,256]{1,0:T(8,128)(2,1)S(1)}, u32[]{:S(2)}, u32[]{:S(2)}) collective-permute-start(bf16[1552,256]{1,0:T(8,128)(2,1)S(1)} %get-tuple-element.70), channel_id=1, source_target_pairs={{0,2},{2,0},{4,6},{6,4},{8,10},{10,8},{12,14},{14,12},{16,18},{18,... | collective-permute-start | bytes 2383880 | tf_op jit(solution)/shard_map/ppermute | solution.py:297
  44.0 6.5 %collective-permute-start.13 = (s32[264,128]{1,0:T(8,128)S(1)}, s32[264,128]{1,0:T(8,128)S(1)}, u32[]{:S(2)}, u32[]{:S(2)}) collective-permute-start(s32[264,128]{1,0:T(8,128)S(1)} %get-tuple-element.78), channel_id=1, source_target_pairs={{0,1},{1,0},{2,3},{3,2},{4,5},{5,4},{6,7},{7,6},{8,9},{9,8},{10,11... | collective-permute-start | bytes 405512 | tf_op jit(solution)/shard_map/ppermute | solution.py:308
  46.1 7.2 %collective-permute-start.14 = (s32[264,128]{1,0:T(8,128)S(1)}, s32[264,128]{1,0:T(8,128)S(1)}, u32[]{:S(2)}, u32[]{:S(2)}) collective-permute-start(s32[264,128]{1,0:T(8,128)S(1)} %get-tuple-element.80), channel_id=1, source_target_pairs={{0,1},{1,0},{2,3},{3,2},{4,5},{5,4},{6,7},{7,6},{8,9},{9,8},{10,11... | collective-permute-start | bytes 405512 | tf_op jit(solution)/shard_map/ppermute | solution.py:308
  47.3 8.5 %collective-permute-start.12 = (s32[264,128]{1,0:T(8,128)S(1)}, s32[264,128]{1,0:T(8,128)S(1)}, u32[]{:S(2)}, u32[]{:S(2)}) collective-permute-start(s32[264,128]{1,0:T(8,128)S(1)} %get-tuple-element.74), channel_id=1, source_target_pairs={{0,1},{1,0},{2,3},{3,2},{4,5},{5,4},{6,7},{7,6},{8,9},{9,8},{10,11... | collective-permute-start | bytes 405512 | tf_op jit(solution)/shard_map/ppermute | solution.py:308

commit v9 on v8

--- a/solution.py
+++ b/solution.py
@@ -8,6 +8,7 @@
 from jax.sharding import PartitionSpec as P
 
 PAD = 16
+TAIL = 32
 STEPS = 32766.0
 CHUNK = 128
 PARAMS = pltpu.CompilerParams(vmem_limit_bytes=32 * 1024 * 1024)
@@ -50,7 +51,10 @@
         [jnp.broadcast_to(jitter[:, :half], (PAD // 2, half)), jnp.broadcast_to(jitter[:, half:], (PAD // 2, half))],
         axis=0,
     ).astype(x.dtype)
-    cut_kernel(high, *parts)
+    for i, part in enumerate(parts):
+        span = slice(i * CHUNK, (i + 1) * CHUNK)
+        part[: members + PAD, :] = high[:, span]
+        part[members + PAD :, :] = x[members - TAIL :, span]
 
 
 def cut_kernel(whole, *parts):
@@ -64,9 +68,19 @@
     return call(cut_kernel, [half] * 2, panel, name="cut")
 
 
+def head_kernel(whole, part):
+    part[...] = whole[: part.shape[0], :]
+
+
+def head(panel):
+    short = jax.ShapeDtypeStruct((panel.shape[0] - TAIL, panel.shape[1]), panel.dtype)
+    return call(head_kernel, [short], panel, name="head")[0]
+
+
 def prepare(x, coord):
     members, width = x.shape
-    outs = [jax.ShapeDtypeStruct((members + PAD, w), x.dtype) for w in (width // 2, width // 4, width // 4)]
+    outs = [jax.ShapeDtypeStruct((members + PAD, width // 2), x.dtype)]
+    outs += [jax.ShapeDtypeStruct((members + PAD + TAIL, CHUNK), x.dtype)] * (width // 2 // CHUNK)
     return call(prepare_kernel, outs, x, coord, name="prepare")
 
 
@@ -158,16 +172,19 @@
     def run(which):
         chosen = [panels[i] for i in which]
         half = cols.shape[1] // 2
-        pad = [chosen[-1][members:, :].astype(F32)] * 2
+        pad = [chosen[-1][members : members + PAD, :].astype(F32)] * 2
         if len(chosen) == 1:
             pad = [pad[0][:, :half], pad[0][:, half:]]
         cols[:, :half] = pad[0][: PAD // 2]
         cols[:, half:] = pad[1][PAD // 2 :]
+        blocks = [panel[:members, :] for panel in chosen]
+        if chosen[0].shape[0] < members:
+            blocks[0] = jnp.concatenate([chosen[0][...], chosen[1][members + PAD :, :]], axis=0)
         if keep:
-            for at, panel in zip((0, half), chosen):
-                outs[-1][:members, at : at + half] = panel[:members, :]
-                outs[-1][members:, at : at + half] = chosen[-1][members:, :]
-        block = jnp.concatenate([panel[:members, :] for panel in chosen], axis=1)
+            for at, block in zip((0, half), blocks):
+                outs[-1][:members, at : at + half] = block
+                outs[-1][members:, at : at + half] = chosen[-1][members : members + PAD, :]
+        block = jnp.concatenate(blocks, axis=1)
         tile = jnp.dot(lt[...], block, preferred_element_type=F32)
         if len(rows) > 1:
             pack(tile[: rows[0]], outs[0])
@@ -315,7 +332,7 @@
     own_parts = reduced(own)
     own_cols = jnp.concatenate([high[members : members + PAD // 2], high[members + PAD // 2 :]], axis=1).astype(F32)
 
-    first = permute(low, swap_x)
+    first = permute(head(low), swap_x)
     extra = [permute(a, extra_pairs) for a in (low, high)]
     straight = [permute(after(a, first), back_two) for a in highs]
     near = cut(first)

time: 56.8 us -> 56.2 us (0.989)
  local copies, waits for them, and re-layouts: 3.35 us -> 1.32 us
  waiting for transfers between devices: 27.6 us -> 29 us
    unnamed x8 -> x6, local copies, waits for them, and re-layouts: 2.05 us -> 0.01 us
    ppermute x9, waiting for transfers between devices: 21.6 us -> 23 us  [permute(): return lax.ppermute(array, 'mesh', pairs)]
    pallas_call x9 -> x10, Pallas kernels: 5.49 us -> 5.3 us  [call(): pl.pallas_call(kernel, out_shape=outs, in_specs=[VMEM] * len(operands), o...]
where the time goes in v9:
time: 56.2 us; the launch traced here: 55.8 us
  waiting for transfers between devices  29 us (52%)
  starting transfers between devices  15.2 us (27%)
  Pallas kernels  10.1 us (18%)
  local copies, waits for them, and re-layouts  1.32 us (2%)
    ppermute x9, waiting for transfers between devices, permute(): return lax.ppermute(array, 'mesh', pairs)  23 us
    ppermute x6, starting transfers between devices, reduced(): lax.ppermute(a, 'mem', [(0, 1), (1, 0)])  8.59 us
    ppermute x9, starting transfers between devices, permute(): return lax.ppermute(array, 'mesh', pairs)  6.59 us
    ppermute x6, waiting for transfers between devices, reduced(): lax.ppermute(a, 'mem', [(0, 1), (1, 0)])  6 us
    pallas_call x10, Pallas kernels, call(): pl.pallas_call(kernel, out_shape=outs, in_specs=[VMEM] * len(operands), o...  5.3 us
    pallas_call x3, Pallas kernels, finish(): pl.pallas_call(functools.partial(finish_kernel, plan=plan, period=period,...  4.8 us
    slice x1, local copies, waits for them, and re-layouts, per_device(): low = perturbations[:, :half]  1.3 us
  transfers between devices with their start and end apart: 15, of which 7 were waited for; matrix products, arithmetic and copies ran while one was open for 0% of the time, Pallas kernels for 17%

profile of v9, /device:TPU:26, one launch (start us, length us, event | category | flops | bytes accessed | tf_op | source)
XLA Modules:
  0.0 55.8 jit_solution(10836205963827753917)
XLA Ops:
  0.0 1.3 %slice.9.low.whole = bf16[1536,256]{1,0:T(8,128)(2,1)S(1)} slice(bf16[1536,512]{1,0:T(8,128)(2,1)} %x), slice={[0:1536], [0:256]} | slice | bytes 1572864 | tf_op jit(solution)/shard_map/slice | solution.py:329
  1.4 0.6 %collective-permute-start.3 = (bf16[1504,256]{1,0:T(8,128)(2,1)S(1)}, bf16[1504,256]{1,0:T(8,128)(2,1)S(1)}, u32[]{:S(2)}, u32[]{:S(2)}) collective-permute-start(bf16[1504,256]{1,0:T(8,128)(2,1)S(1)} %head.1), channel_id=1, source_target_pairs={{0,4},{2,6},{4,0},{6,2},{8,12},{10,14},{12,8},{14,10},{16,20},{18,... | collective-permute-start | bytes 2310152 | tf_op jit(solution)/shard_map/ppermute | solution.py:314
  2.2 0.6 %collective-permute-start.2 = (bf16[1552,256]{1,0:T(8,128)(2,1)S(1)}, bf16[1552,256]{1,0:T(8,128)(2,1)S(1)}, u32[]{:S(2)}, u32[]{:S(2)}) collective-permute-start(bf16[1552,256]{1,0:T(8,128)(2,1)S(1)} %get-tuple-element.44.high), channel_id=1, source_target_pairs={{0,26},{2,0},{4,30},{6,4},{8,2},{10,8},{12,6},{14,12},{16,10},{18,... | collective-permute-start | bytes 2383880 | tf_op jit(solution)/shard_map/ppermute | solution.py:314
  2.8 1.2 %own_tile.1 = (bf16[512,1536]{1,0:T(8,128)(2,1)S(1)}, f32[256,128]{1,0:T(8,128)S(1)}, f32[256,128]{1,0:T(8,128)S(1)}, f32[256,512]{1,0:T(8,128)S(1)}, f32[256,512]{1,0:T(8,128)S(1)}) custom-call(bf16[1536,256]{1,0:T(8,128)(2,1)S(1)} %slice.9.low.whole, bf16[1552,256]{1,0:T(8,128)(2,1)S(1)} %get-tuple-element.44.high, s32[1,512]{1,0:T(1,128)S(1)} %bitcast.3, ...), custom_call_target="tpu_custom_call" | custom-call | flops 1 | bytes 1 | tf_op jit(solution)/shard_map/own_tile/pallas_call | solution.py:25
  4.0 1.7 %collective-permute-start = (f32[256,512]{1,0:T(8,128)S(1)}, f32[256,512]{1,0:T(8,128)S(1)}, u32[]{:S(2)}, u32[]{:S(2)}) collective-permute-start(f32[256,512]{1,0:T(8,128)S(1)} %get-tuple-element.48), channel_id=1, source_target_pairs={{0,1},{1,0},{2,3},{3,2},{4,5},{5,4},{6,7},{7,6},{8,9},{9,8},{10,11... | collective-permute-start | bytes 1572872 | tf_op jit(solution)/shard_map/ppermute | solution.py:325
  5.7 14.7 %collective-permute-done.3.whole = bf16[1504,256]{1,0:T(8,128)(2,1)S(1)} collective-permute-done((bf16[1504,256]{1,0:T(8,128)(2,1)S(1)}, bf16[1504,256]{1,0:T(8,128)(2,1)S(1)}, u32[]{:S(2)}, u32[]{:S(2)}) %collective-permute-start.3) | collective-permute-done | bytes 770080 | tf_op jit(solution)/shard_map/ppermute | solution.py:314
  21.0 2.4 %collective-permute-start.4 = (bf16[1504,128]{1,0:T(8,128)(2,1)S(1)}, bf16[1504,128]{1,0:T(8,128)(2,1)S(1)}, u32[]{:S(2)}, u32[]{:S(2)}) collective-permute-start(bf16[1504,128]{1,0:T(8,128)(2,1)S(1)} %get-tuple-element.52.refs_0_), channel_id=1, source_target_pairs={{4,28},{6,30},{12,4},{14,6},{20,12},{22,14},{28,20},{30,22},{5,29}... | collective-permute-start | bytes 1155080 | tf_op jit(solution)/shard_map/ppermute | solution.py:314
  23.5 2.4 %collective-permute-start.8 = (bf16[1504,128]{1,0:T(8,128)(2,1)S(1)}, bf16[1504,128]{1,0:T(8,128)(2,1)S(1)}, u32[]{:S(2)}, u32[]{:S(2)}) collective-permute-start(bf16[1504,128]{1,0:T(8,128)(2,1)S(1)} %get-tuple-element.62.refs_0_), channel_id=1, source_target_pairs={{4,28},{6,30},{12,4},{14,6},{20,12},{22,14},{28,20},{30,22},{5,29}... | collective-permute-start | bytes 1155080 | tf_op jit(solution)/shard_map/ppermute | solution.py:314
  25.9 1.0 %panel_tile.5 = (f32[8,512]{1,0:T(8,128)S(1)}, s32[264,256]{1,0:T(8,128)S(1)}, f32[256,512]{1,0:T(8,128)S(1)}) custom-call(bf16[512,1536]{1,0:T(8,128)(2,1)S(1)} %get-tuple-element.69.lt, bf16[1536,256]{1,0:T(8,128)(2,1)S(1)} %collective-permute-done.1.refs_0_, bf16[1552,256]{1,0:T(8,128)(2,1)S(1)} %collective-permute-done.2.refs_1_), custom_call_target="tpu_custom_call" | custom-call | flops 1 | bytes 1 | tf_op jit(solution)/shard_map/panel_tile/pallas_call | solution.py:25
  26.9 1.6 %collective-permute-start.6 = (s32[264,256]{1,0:T(8,128)S(1)}, s32[264,256]{1,0:T(8,128)S(1)}, u32[]{:S(2)}, u32[]{:S(2)}) collective-permute-start(s32[264,256]{1,0:T(8,128)S(1)} %get-tuple-element.59), channel_id=1, source_target_pairs={{0,1},{1,0},{2,3},{3,2},{4,5},{5,4},{6,7},{7,6},{8,9},{9,8},{10,11... | collective-permute-start | bytes 811016 | tf_op jit(solution)/shard_map/ppermute | solution.py:325
  28.5 8.1 %collective-permute-done.4.refs_1_ = bf16[1504,128]{1,0:T(8,128)(2,1)S(1)} collective-permute-done((bf16[1504,128]{1,0:T(8,128)(2,1)S(1)}, bf16[1504,128]{1,0:T(8,128)(2,1)S(1)}, u32[]{:S(2)}, u32[]{:S(2)}) %collective-permute-start.4) | collective-permute-done | bytes 385056 | tf_op jit(solution)/shard_map/ppermute | solution.py:314
  36.6 0.6 %panel_tile.6 = (f32[8,256]{1,0:T(8,128)S(1)}, s32[264,128]{1,0:T(8,128)S(1)}, f32[256,256]{1,0:T(8,128)S(1)}, bf16[1552,256]{1,0:T(8,128)(2,1)S(1)}) custom-call(bf16[512,1536]{1,0:T(8,128)(2,1)S(1)} %get-tuple-element.69.lt, bf16[1504,128]{1,0:T(8,128)(2,1)S(1)} %get-tuple-element.52.refs_0_, bf16[1504,128]{1,0:T(8,128)(2,1)S(1)} %collective-permute-done.4.refs_1_, ...), custom_call_target="tpu_custom_call" | custom-call | flops 1 | bytes 1 | tf_op jit(solution)/shard_map/panel_tile/pallas_call | solution.py:25
  37.2 1.6 %collective-permute-start.7 = (s32[264,128]{1,0:T(8,128)S(1)}, s32[264,128]{1,0:T(8,128)S(1)}, u32[]{:S(2)}, u32[]{:S(2)}) collective-permute-start(s32[264,128]{1,0:T(8,128)S(1)} %get-tuple-element.60), channel_id=1, source_target_pairs={{0,1},{1,0},{2,3},{3,2},{4,5},{5,4},{6,7},{7,6},{8,9},{9,8},{10,11... | collective-permute-start | bytes 405512 | tf_op jit(solution)/shard_map/ppermute | solution.py:325
  38.8 2.2 %finish.3.refs_9_ = f32[256,2048]{1,0:T(8,128)} custom-call(f32[256,128]{1,0:T(8,128)S(1)} %get-tuple-element.45.row_coord, f32[256,128]{1,0:T(8,128)S(1)} %get-tuple-element.46.row_level, f32[8,512]{1,0:T(8,128)S(1)} %maximum_convert_fusion.refs_0_, f32[256,512]{1,0:T(8,128)S(1)} %get-tuple-element.57.refs_1_, f32[256,512]{1,0:T(8,128)S(1)} %collective-permute-done.refs_2_, ...), custom_call_target="tpu_custom_call" | custom-call | flops 1 | bytes 1 | tf_op jit(solution)/shard_map/finish/pallas_call | solution.py:287
  41.0 1.3 %collective-permute-done.7.refs_2_ = s32[264,128]{1,0:T(8,128)S(1)} collective-permute-done((s32[264,128]{1,0:T(8,128)S(1)}, s32[264,128]{1,0:T(8,128)S(1)}, u32[]{:S(2)}, u32[]{:S(2)}) %collective-permute-start.7) | collective-permute-done | bytes 135200 | tf_op jit(solution)/shard_map/ppermute | solution.py:325
  42.5 0.6 %panel_tile.7 = (f32[8,256]{1,0:T(8,128)S(1)}, s32[264,128]{1,0:T(8,128)S(1)}, f32[256,256]{1,0:T(8,128)S(1)}, bf16[1552,256]{1,0:T(8,128)(2,1)S(1)}) custom-call(bf16[512,1536]{1,0:T(8,128)(2,1)S(1)} %get-tuple-element.69.lt, bf16[1504,128]{1,0:T(8,128)(2,1)S(1)} %get-tuple-element.62.refs_0_, bf16[1504,128]{1,0:T(8,128)(2,1)S(1)} %collective-permute-done.8.refs_1_, ...), custom_call_target="tpu_custom_call" | custom-call | flops 1 | bytes 1 | tf_op jit(solution)/shard_map/panel_tile/pallas_call | solution.py:25
  43.2 1.6 %collective-permute-start.13 = (s32[264,128]{1,0:T(8,128)S(1)}, s32[264,128]{1,0:T(8,128)S(1)}, u32[]{:S(2)}, u32[]{:S(2)}) collective-permute-start(s32[264,128]{1,0:T(8,128)S(1)} %get-tuple-element.78), channel_id=1, source_target_pairs={{0,1},{1,0},{2,3},{3,2},{4,5},{5,4},{6,7},{7,6},{8,9},{9,8},{10,11... | collective-permute-start | bytes 405512 | tf_op jit(solution)/shard_map/ppermute | solution.py:325
  44.8 0.6 %panel_tile.8 = (f32[8,256]{1,0:T(8,128)S(1)}, s32[264,128]{1,0:T(8,128)S(1)}, f32[256,256]{1,0:T(8,128)S(1)}) custom-call(bf16[512,1536]{1,0:T(8,128)(2,1)S(1)} %get-tuple-element.69.lt, bf16[1552,256]{1,0:T(8,128)(2,1)S(1)} %collective-permute-done.10.refs_0_), custom_call_target="tpu_custom_call" | custom-call | flops 1 | bytes 1 | tf_op jit(solution)/shard_map/panel_tile/pallas_call | solution.py:25
  46.5 1.6 %collective-permute-start.12 = (s32[264,128]{1,0:T(8,128)S(1)}, s32[264,128]{1,0:T(8,128)S(1)}, u32[]{:S(2)}, u32[]{:S(2)}) collective-permute-start(s32[264,128]{1,0:T(8,128)S(1)} %get-tuple-element.74), channel_id=1, source_target_pairs={{0,1},{1,0},{2,3},{3,2},{4,5},{5,4},{6,7},{7,6},{8,9},{9,8},{10,11... | collective-permute-start | bytes 405512 | tf_op jit(solution)/shard_map/ppermute | solution.py:325
  48.4 1.2 %collective-permute-done.13.refs_5_ = s32[264,128]{1,0:T(8,128)S(1)} collective-permute-done((s32[264,128]{1,0:T(8,128)S(1)}, s32[264,128]{1,0:T(8,128)S(1)}, u32[]{:S(2)}, u32[]{:S(2)}) %collective-permute-start.13) | collective-permute-done | bytes 135200 | tf_op jit(solution)/shard_map/ppermute | solution.py:325
  49.7 2.9 %collective-permute-done.14.refs_8_ = s32[264,128]{1,0:T(8,128)S(1)} collective-permute-done((s32[264,128]{1,0:T(8,128)S(1)}, s32[264,128]{1,0:T(8,128)S(1)}, u32[]{:S(2)}, u32[]{:S(2)}) %collective-permute-start.14) | collective-permute-done | bytes 135200 | tf_op jit(solution)/shard_map/ppermute | solution.py:325
  52.6 1.9 %finish.4.refs_3_ = f32[256,2048]{1,0:T(8,128)} custom-call(f32[256,128]{1,0:T(8,128)S(1)} %get-tuple-element.45.row_coord, f32[256,128]{1,0:T(8,128)S(1)} %get-tuple-element.46.row_level, f32[8,256]{1,0:T(8,128)S(1)} %get-tuple-element.75.refs_0_, f32[256,256]{1,0:T(8,128)S(1)} %get-tuple-element.76.refs_1_, ...), custom_call_target="tpu_custom_call", output_to_operand_aliasing={{}: (11, {})} | custom-call | flops 1 | bytes 1 | tf_op jit(solution)/shard_map/finish/pallas_call | solution.py:287
  54.4 0.6 %collective-permute-done.12.refs_2_ = s32[264,128]{1,0:T(8,128)S(1)} collective-permute-done((s32[264,128]{1,0:T(8,128)S(1)}, s32[264,128]{1,0:T(8,128)S(1)}, u32[]{:S(2)}, u32[]{:S(2)}) %collective-permute-start.12) | collective-permute-done | bytes 135200 | tf_op jit(solution)/shard_map/ppermute | solution.py:325
  55.0 0.8 %finish.5 = f32[256,2048]{1,0:T(8,128)} custom-call(f32[256,128]{1,0:T(8,128)S(1)} %get-tuple-element.45.row_coord, f32[256,128]{1,0:T(8,128)S(1)} %get-tuple-element.46.row_level, f32[256,256]{1,0:T(8,128)S(1)} %weigh.1.refs_0_, f32[256,256]{1,0:T(8,128)S(1)} %get-tuple-element.73.refs_1_, ...), custom_call_target="tpu_custom_call", output_to_operand_aliasing={{}: (5, {})} | custom-call | flops 1 | bytes 1 | tf_op jit(solution)/shard_map/finish/pallas_call | solution.py:287
  (28 shorter events, 2.7 us)
Async XLA Ops:
  0.0 2.0 %copy-start = (bf16[1536,512]{1,0:T(8,128)(2,1)S(1)}, bf16[1536,512]{1,0:T(8,128)(2,1)}, u32[]{:S(2)}) copy-start(bf16[1536,512]{1,0:T(8,128)(2,1)} %x) | copy-start | bytes 4718596
  0.0 2.0 %copy-start.1 = (s32[512]{0:T(512)S(1)}, s32[512]{0:T(512)}, u32[]{:S(2)}) copy-start(s32[512]{0:T(512)} %param.4) | copy-start | bytes 6148
  0.0 2.8 %copy-start.2 = (s32[512]{0:T(512)S(1)}, s32[512]{0:T(512)}, u32[]{:S(2)}) copy-start(s32[512]{0:T(512)} %param.5) | copy-start | bytes 6148
  1.4 19.0 %collective-permute-start.3 = (bf16[1504,256]{1,0:T(8,128)(2,1)S(1)}, bf16[1504,256]{1,0:T(8,128)(2,1)S(1)}, u32[]{:S(2)}, u32[]{:S(2)}) collective-permute-start(bf16[1504,256]{1,0:T(8,128)(2,1)S(1)} %head.1), channel_id=1, source_target_pairs={{0,4},{2,6},{4,0},{6,2},{8,12},{10,14},{12,8},{14,10},{16,20},{18,... | collective-permute-start | bytes 2310152 | tf_op jit(solution)/shard_map/ppermute | solution.py:314
  2.0 21.5 %collective-permute-start.1 = (bf16[1536,256]{1,0:T(8,128)(2,1)S(1)}, bf16[1536,256]{1,0:T(8,128)(2,1)S(1)}, u32[]{:S(2)}, u32[]{:S(2)}) collective-permute-start(bf16[1536,256]{1,0:T(8,128)(2,1)S(1)} %slice.9.low.whole), channel_id=1, source_target_pairs={{0,26},{2,0},{4,30},{6,4},{8,2},{10,8},{12,6},{14,12},{16,10},{18,... | collective-permute-start | bytes 2359304 | tf_op jit(solution)/shard_map/ppermute | solution.py:314
  2.2 23.7 %collective-permute-start.2 = (bf16[1552,256]{1,0:T(8,128)(2,1)S(1)}, bf16[1552,256]{1,0:T(8,128)(2,1)S(1)}, u32[]{:S(2)}, u32[]{:S(2)}) collective-permute-start(bf16[1552,256]{1,0:T(8,128)(2,1)S(1)} %get-tuple-element.44.high), channel_id=1, source_target_pairs={{0,26},{2,0},{4,30},{6,4},{8,2},{10,8},{12,6},{14,12},{16,10},{18,... | collective-permute-start | bytes 2383880 | tf_op jit(solution)/shard_map/ppermute | solution.py:314
  4.0 19.4 %collective-permute-start = (f32[256,512]{1,0:T(8,128)S(1)}, f32[256,512]{1,0:T(8,128)S(1)}, u32[]{:S(2)}, u32[]{:S(2)}) collective-permute-start(f32[256,512]{1,0:T(8,128)S(1)} %get-tuple-element.48), channel_id=1, source_target_pairs={{0,1},{1,0},{2,3},{3,2},{4,5},{5,4},{6,7},{7,6},{8,9},{9,8},{10,11... | collective-permute-start | bytes 1572872 | tf_op jit(solution)/shard_map/ppermute | solution.py:325
  20.4 16.2 %collective-permute-start.5 = (bf16[1584,128]{1,0:T(8,128)(2,1)S(1)}, bf16[1584,128]{1,0:T(8,128)(2,1)S(1)}, u32[]{:S(2)}, u32[]{:S(2)}) collective-permute-start(bf16[1584,128]{1,0:T(8,128)(2,1)S(1)} %get-tuple-element.54), channel_id=1, source_target_pairs={{0,28},{2,30},{4,0},{6,2},{8,4},{10,6},{12,8},{14,10},{16,12},{18,... | collective-permute-start | bytes 1216520 | tf_op jit(solution)/shard_map/ppermute | solution.py:314
  21.0 15.6 %collective-permute-start.4 = (bf16[1504,128]{1,0:T(8,128)(2,1)S(1)}, bf16[1504,128]{1,0:T(8,128)(2,1)S(1)}, u32[]{:S(2)}, u32[]{:S(2)}) collective-permute-start(bf16[1504,128]{1,0:T(8,128)(2,1)S(1)} %get-tuple-element.52.refs_0_), channel_id=1, source_target_pairs={{4,28},{6,30},{12,4},{14,6},{20,12},{22,14},{28,20},{30,22},{5,29}... | collective-permute-start | bytes 1155080 | tf_op jit(solution)/shard_map/ppermute | solution.py:314
  23.4 19.1 %collective-permute-start.9 = (bf16[1584,128]{1,0:T(8,128)(2,1)S(1)}, bf16[1584,128]{1,0:T(8,128)(2,1)S(1)}, u32[]{:S(2)}, u32[]{:S(2)}) collective-permute-start(bf16[1584,128]{1,0:T(8,128)(2,1)S(1)} %get-tuple-element.64), channel_id=1, source_target_pairs={{0,28},{2,30},{4,0},{6,2},{8,4},{10,6},{12,8},{14,10},{16,12},{18,... | collective-permute-start | bytes 1216520 | tf_op jit(solution)/shard_map/ppermute | solution.py:314
  23.5 19.0 %collective-permute-start.8 = (bf16[1504,128]{1,0:T(8,128)(2,1)S(1)}, bf16[1504,128]{1,0:T(8,128)(2,1)S(1)}, u32[]{:S(2)}, u32[]{:S(2)}) collective-permute-start(bf16[1504,128]{1,0:T(8,128)(2,1)S(1)} %get-tuple-element.62.refs_0_), channel_id=1, source_target_pairs={{4,28},{6,30},{12,4},{14,6},{20,12},{22,14},{28,20},{30,22},{5,29}... | collective-permute-start | bytes 1155080 | tf_op jit(solution)/shard_map/ppermute | solution.py:314
  26.9 11.9 %collective-permute-start.6 = (s32[264,256]{1,0:T(8,128)S(1)}, s32[264,256]{1,0:T(8,128)S(1)}, u32[]{:S(2)}, u32[]{:S(2)}) collective-permute-start(s32[264,256]{1,0:T(8,128)S(1)} %get-tuple-element.59), channel_id=1, source_target_pairs={{0,1},{1,0},{2,3},{3,2},{4,5},{5,4},{6,7},{7,6},{8,9},{9,8},{10,11... | collective-permute-start | bytes 811016 | tf_op jit(solution)/shard_map/ppermute | solution.py:325
  37.2 5.1 %collective-permute-start.7 = (s32[264,128]{1,0:T(8,128)S(1)}, s32[264,128]{1,0:T(8,128)S(1)}, u32[]{:S(2)}, u32[]{:S(2)}) collective-permute-start(s32[264,128]{1,0:T(8,128)S(1)} %get-tuple-element.60), channel_id=1, source_target_pairs={{0,1},{1,0},{2,3},{3,2},{4,5},{5,4},{6,7},{7,6},{8,9},{9,8},{10,11... | collective-permute-start | bytes 405512 | tf_op jit(solution)/shard_map/ppermute | solution.py:325
  38.8 6.0 %collective-permute-start.10 = (bf16[1552,256]{1,0:T(8,128)(2,1)S(1)}, bf16[1552,256]{1,0:T(8,128)(2,1)S(1)}, u32[]{:S(2)}, u32[]{:S(2)}) collective-permute-start(bf16[1552,256]{1,0:T(8,128)(2,1)S(1)} %get-tuple-element.67), channel_id=1, source_target_pairs={{0,2},{2,0},{4,6},{6,4},{8,10},{10,8},{12,14},{14,12},{16,18},{18,... | collective-permute-start | bytes 2383880 | tf_op jit(solution)/shard_map/ppermute | solution.py:314
  43.1 2.8 %collective-permute-start.11 = (bf16[1552,256]{1,0:T(8,128)(2,1)S(1)}, bf16[1552,256]{1,0:T(8,128)(2,1)S(1)}, u32[]{:S(2)}, u32[]{:S(2)}) collective-permute-start(bf16[1552,256]{1,0:T(8,128)(2,1)S(1)} %get-tuple-element.70), channel_id=1, source_target_pairs={{0,2},{2,0},{4,6},{6,4},{8,10},{10,8},{12,14},{14,12},{16,18},{18,... | collective-permute-start | bytes 2383880 | tf_op jit(solution)/shard_map/ppermute | solution.py:314
  43.2 6.5 %collective-permute-start.13 = (s32[264,128]{1,0:T(8,128)S(1)}, s32[264,128]{1,0:T(8,128)S(1)}, u32[]{:S(2)}, u32[]{:S(2)}) collective-permute-start(s32[264,128]{1,0:T(8,128)S(1)} %get-tuple-element.78), channel_id=1, source_target_pairs={{0,1},{1,0},{2,3},{3,2},{4,5},{5,4},{6,7},{7,6},{8,9},{9,8},{10,11... | collective-permute-start | bytes 405512 | tf_op jit(solution)/shard_map/ppermute | solution.py:325
  45.4 7.2 %collective-permute-start.14 = (s32[264,128]{1,0:T(8,128)S(1)}, s32[264,128]{1,0:T(8,128)S(1)}, u32[]{:S(2)}, u32[]{:S(2)}) collective-permute-start(s32[264,128]{1,0:T(8,128)S(1)} %get-tuple-element.80), channel_id=1, source_target_pairs={{0,1},{1,0},{2,3},{3,2},{4,5},{5,4},{6,7},{7,6},{8,9},{9,8},{10,11... | collective-permute-start | bytes 405512 | tf_op jit(solution)/shard_map/ppermute | solution.py:325
  46.5 8.5 %collective-permute-start.12 = (s32[264,128]{1,0:T(8,128)S(1)}, s32[264,128]{1,0:T(8,128)S(1)}, u32[]{:S(2)}, u32[]{:S(2)}) collective-permute-start(s32[264,128]{1,0:T(8,128)S(1)} %get-tuple-element.74), channel_id=1, source_target_pairs={{0,1},{1,0},{2,3},{3,2},{4,5},{5,4},{6,7},{7,6},{8,9},{9,8},{10,11... | collective-permute-start | bytes 405512 | tf_op jit(solution)/shard_map/ppermute | solution.py:325

commit v10 on v9

--- a/solution.py
+++ b/solution.py
@@ -138,12 +138,14 @@
 def narrowed(block):
     top = jnp.maximum(jnp.max(jnp.abs(block), axis=0, keepdims=True), 2.0**-126)
     power = jnp.ceil(8.0 * jnp.log2(top) + 0.01)
-    steps = jnp.round(block * jnp.exp2(-0.125 * power) * STEPS)
+    root = jnp.exp2(-0.0625 * power)
+    steps = jnp.round((block * root) * (root * STEPS))
     return steps.astype(jnp.int32), power.astype(jnp.int32)
 
 
 def widened(steps, power):
-    return (steps.astype(F32) * jnp.exp2(0.125 * power.astype(F32) - 16.0)) * (65536.0 / STEPS)
+    root = jnp.exp2(0.0625 * power.astype(F32))
+    return (steps.astype(F32) * (root * (1.0 / STEPS))) * root
 
 
 def pack(tile, packed):

time: 56.2 us -> 56.2 us (level)
  no operation moved by 1% of the time
where the time goes in v10:
time: 56.2 us; the launch traced here: 55.8 us
  waiting for transfers between devices  29 us (52%)
  starting transfers between devices  15.2 us (27%)
  Pallas kernels  10.1 us (18%)
  local copies, waits for them, and re-layouts  1.32 us (2%)
    ppermute x9, waiting for transfers between devices, permute(): return lax.ppermute(array, 'mesh', pairs)  23 us
    ppermute x6, starting transfers between devices, reduced(): lax.ppermute(a, 'mem', [(0, 1), (1, 0)])  8.59 us
    ppermute x9, starting transfers between devices, permute(): return lax.ppermute(array, 'mesh', pairs)  6.59 us
    ppermute x6, waiting for transfers between devices, reduced(): lax.ppermute(a, 'mem', [(0, 1), (1, 0)])  5.98 us
    pallas_call x10, Pallas kernels, call(): pl.pallas_call(kernel, out_shape=outs, in_specs=[VMEM] * len(operands), o...  5.3 us
    pallas_call x3, Pallas kernels, finish(): pl.pallas_call(functools.partial(finish_kernel, plan=plan, period=period,...  4.81 us
    slice x1, local copies, waits for them, and re-layouts, per_device(): low = perturbations[:, :half]  1.3 us
  transfers between devices with their start and end apart: 15, of which 7 were waited for; matrix products, arithmetic and copies ran while one was open for 0% of the time, Pallas kernels for 17%

profile of v10, /device:TPU:26, one launch (start us, length us, event | category | flops | bytes accessed | tf_op | source)
XLA Modules:
  0.0 55.8 jit_solution(17940695057318682771)
XLA Ops:
  0.0 1.3 %slice.9.low.whole = bf16[1536,256]{1,0:T(8,128)(2,1)S(1)} slice(bf16[1536,512]{1,0:T(8,128)(2,1)} %x), slice={[0:1536], [0:256]} | slice | bytes 1572864 | tf_op jit(solution)/shard_map/slice | solution.py:331
  1.4 0.6 %collective-permute-start.3 = (bf16[1504,256]{1,0:T(8,128)(2,1)S(1)}, bf16[1504,256]{1,0:T(8,128)(2,1)S(1)}, u32[]{:S(2)}, u32[]{:S(2)}) collective-permute-start(bf16[1504,256]{1,0:T(8,128)(2,1)S(1)} %head.1), channel_id=1, source_target_pairs={{0,4},{2,6},{4,0},{6,2},{8,12},{10,14},{12,8},{14,10},{16,20},{18,... | collective-permute-start | bytes 2310152 | tf_op jit(solution)/shard_map/ppermute | solution.py:316
  2.2 0.6 %collective-permute-start.2 = (bf16[1552,256]{1,0:T(8,128)(2,1)S(1)}, bf16[1552,256]{1,0:T(8,128)(2,1)S(1)}, u32[]{:S(2)}, u32[]{:S(2)}) collective-permute-start(bf16[1552,256]{1,0:T(8,128)(2,1)S(1)} %get-tuple-element.44.high), channel_id=1, source_target_pairs={{0,26},{2,0},{4,30},{6,4},{8,2},{10,8},{12,6},{14,12},{16,10},{18,... | collective-permute-start | bytes 2383880 | tf_op jit(solution)/shard_map/ppermute | solution.py:316
  2.8 1.2 %own_tile.1 = (bf16[512,1536]{1,0:T(8,128)(2,1)S(1)}, f32[256,128]{1,0:T(8,128)S(1)}, f32[256,128]{1,0:T(8,128)S(1)}, f32[256,512]{1,0:T(8,128)S(1)}, f32[256,512]{1,0:T(8,128)S(1)}) custom-call(bf16[1536,256]{1,0:T(8,128)(2,1)S(1)} %slice.9.low.whole, bf16[1552,256]{1,0:T(8,128)(2,1)S(1)} %get-tuple-element.44.high, s32[1,512]{1,0:T(1,128)S(1)} %bitcast.3, ...), custom_call_target="tpu_custom_call" | custom-call | flops 1 | bytes 1 | tf_op jit(solution)/shard_map/own_tile/pallas_call | solution.py:25
  4.0 1.7 %collective-permute-start = (f32[256,512]{1,0:T(8,128)S(1)}, f32[256,512]{1,0:T(8,128)S(1)}, u32[]{:S(2)}, u32[]{:S(2)}) collective-permute-start(f32[256,512]{1,0:T(8,128)S(1)} %get-tuple-element.48), channel_id=1, source_target_pairs={{0,1},{1,0},{2,3},{3,2},{4,5},{5,4},{6,7},{7,6},{8,9},{9,8},{10,11... | collective-permute-start | bytes 1572872 | tf_op jit(solution)/shard_map/ppermute | solution.py:327
  5.7 14.7 %collective-permute-done.3.whole = bf16[1504,256]{1,0:T(8,128)(2,1)S(1)} collective-permute-done((bf16[1504,256]{1,0:T(8,128)(2,1)S(1)}, bf16[1504,256]{1,0:T(8,128)(2,1)S(1)}, u32[]{:S(2)}, u32[]{:S(2)}) %collective-permute-start.3) | collective-permute-done | bytes 770080 | tf_op jit(solution)/shard_map/ppermute | solution.py:316
  21.0 2.4 %collective-permute-start.4 = (bf16[1504,128]{1,0:T(8,128)(2,1)S(1)}, bf16[1504,128]{1,0:T(8,128)(2,1)S(1)}, u32[]{:S(2)}, u32[]{:S(2)}) collective-permute-start(bf16[1504,128]{1,0:T(8,128)(2,1)S(1)} %get-tuple-element.52.refs_0_), channel_id=1, source_target_pairs={{4,28},{6,30},{12,4},{14,6},{20,12},{22,14},{28,20},{30,22},{5,29}... | collective-permute-start | bytes 1155080 | tf_op jit(solution)/shard_map/ppermute | solution.py:316
  23.5 2.4 %collective-permute-start.8 = (bf16[1504,128]{1,0:T(8,128)(2,1)S(1)}, bf16[1504,128]{1,0:T(8,128)(2,1)S(1)}, u32[]{:S(2)}, u32[]{:S(2)}) collective-permute-start(bf16[1504,128]{1,0:T(8,128)(2,1)S(1)} %get-tuple-element.62.refs_0_), channel_id=1, source_target_pairs={{4,28},{6,30},{12,4},{14,6},{20,12},{22,14},{28,20},{30,22},{5,29}... | collective-permute-start | bytes 1155080 | tf_op jit(solution)/shard_map/ppermute | solution.py:316
  25.9 1.0 %panel_tile.5 = (f32[8,512]{1,0:T(8,128)S(1)}, s32[264,256]{1,0:T(8,128)S(1)}, f32[256,512]{1,0:T(8,128)S(1)}) custom-call(bf16[512,1536]{1,0:T(8,128)(2,1)S(1)} %get-tuple-element.69.lt, bf16[1536,256]{1,0:T(8,128)(2,1)S(1)} %collective-permute-done.1.refs_0_, bf16[1552,256]{1,0:T(8,128)(2,1)S(1)} %collective-permute-done.2.refs_1_), custom_call_target="tpu_custom_call" | custom-call | flops 1 | bytes 1 | tf_op jit(solution)/shard_map/panel_tile/pallas_call | solution.py:25
  26.9 1.6 %collective-permute-start.6 = (s32[264,256]{1,0:T(8,128)S(1)}, s32[264,256]{1,0:T(8,128)S(1)}, u32[]{:S(2)}, u32[]{:S(2)}) collective-permute-start(s32[264,256]{1,0:T(8,128)S(1)} %get-tuple-element.59), channel_id=1, source_target_pairs={{0,1},{1,0},{2,3},{3,2},{4,5},{5,4},{6,7},{7,6},{8,9},{9,8},{10,11... | collective-permute-start | bytes 811016 | tf_op jit(solution)/shard_map/ppermute | solution.py:327
  28.5 8.1 %collective-permute-done.4.refs_1_ = bf16[1504,128]{1,0:T(8,128)(2,1)S(1)} collective-permute-done((bf16[1504,128]{1,0:T(8,128)(2,1)S(1)}, bf16[1504,128]{1,0:T(8,128)(2,1)S(1)}, u32[]{:S(2)}, u32[]{:S(2)}) %collective-permute-start.4) | collective-permute-done | bytes 385056 | tf_op jit(solution)/shard_map/ppermute | solution.py:316
  36.6 0.6 %panel_tile.6 = (f32[8,256]{1,0:T(8,128)S(1)}, s32[264,128]{1,0:T(8,128)S(1)}, f32[256,256]{1,0:T(8,128)S(1)}, bf16[1552,256]{1,0:T(8,128)(2,1)S(1)}) custom-call(bf16[512,1536]{1,0:T(8,128)(2,1)S(1)} %get-tuple-element.69.lt, bf16[1504,128]{1,0:T(8,128)(2,1)S(1)} %get-tuple-element.52.refs_0_, bf16[1504,128]{1,0:T(8,128)(2,1)S(1)} %collective-permute-done.4.refs_1_, ...), custom_call_target="tpu_custom_call" | custom-call | flops 1 | bytes 1 | tf_op jit(solution)/shard_map/panel_tile/pallas_call | solution.py:25
  37.2 1.6 %collective-permute-start.7 = (s32[264,128]{1,0:T(8,128)S(1)}, s32[264,128]{1,0:T(8,128)S(1)}, u32[]{:S(2)}, u32[]{:S(2)}) collective-permute-start(s32[264,128]{1,0:T(8,128)S(1)} %get-tuple-element.60), channel_id=1, source_target_pairs={{0,1},{1,0},{2,3},{3,2},{4,5},{5,4},{6,7},{7,6},{8,9},{9,8},{10,11... | collective-permute-start | bytes 405512 | tf_op jit(solution)/shard_map/ppermute | solution.py:327
  38.8 2.2 %finish.3.refs_9_ = f32[256,2048]{1,0:T(8,128)} custom-call(f32[256,128]{1,0:T(8,128)S(1)} %get-tuple-element.45.row_coord, f32[256,128]{1,0:T(8,128)S(1)} %get-tuple-element.46.row_level, f32[8,512]{1,0:T(8,128)S(1)} %maximum_convert_fusion.refs_0_, f32[256,512]{1,0:T(8,128)S(1)} %get-tuple-element.57.refs_1_, f32[256,512]{1,0:T(8,128)S(1)} %collective-permute-done.refs_2_, ...), custom_call_target="tpu_custom_call" | custom-call | flops 1 | bytes 1 | tf_op jit(solution)/shard_map/finish/pallas_call | solution.py:289
  41.0 1.3 %collective-permute-done.7.refs_2_ = s32[264,128]{1,0:T(8,128)S(1)} collective-permute-done((s32[264,128]{1,0:T(8,128)S(1)}, s32[264,128]{1,0:T(8,128)S(1)}, u32[]{:S(2)}, u32[]{:S(2)}) %collective-permute-start.7) | collective-permute-done | bytes 135200 | tf_op jit(solution)/shard_map/ppermute | solution.py:327
  42.5 0.6 %panel_tile.7 = (f32[8,256]{1,0:T(8,128)S(1)}, s32[264,128]{1,0:T(8,128)S(1)}, f32[256,256]{1,0:T(8,128)S(1)}, bf16[1552,256]{1,0:T(8,128)(2,1)S(1)}) custom-call(bf16[512,1536]{1,0:T(8,128)(2,1)S(1)} %get-tuple-element.69.lt, bf16[1504,128]{1,0:T(8,128)(2,1)S(1)} %get-tuple-element.62.refs_0_, bf16[1504,128]{1,0:T(8,128)(2,1)S(1)} %collective-permute-done.8.refs_1_, ...), custom_call_target="tpu_custom_call" | custom-call | flops 1 | bytes 1 | tf_op jit(solution)/shard_map/panel_tile/pallas_call | solution.py:25
  43.2 1.6 %collective-permute-start.13 = (s32[264,128]{1,0:T(8,128)S(1)}, s32[264,128]{1,0:T(8,128)S(1)}, u32[]{:S(2)}, u32[]{:S(2)}) collective-permute-start(s32[264,128]{1,0:T(8,128)S(1)} %get-tuple-element.78), channel_id=1, source_target_pairs={{0,1},{1,0},{2,3},{3,2},{4,5},{5,4},{6,7},{7,6},{8,9},{9,8},{10,11... | collective-permute-start | bytes 405512 | tf_op jit(solution)/shard_map/ppermute | solution.py:327
  44.8 0.6 %panel_tile.8 = (f32[8,256]{1,0:T(8,128)S(1)}, s32[264,128]{1,0:T(8,128)S(1)}, f32[256,256]{1,0:T(8,128)S(1)}) custom-call(bf16[512,1536]{1,0:T(8,128)(2,1)S(1)} %get-tuple-element.69.lt, bf16[1552,256]{1,0:T(8,128)(2,1)S(1)} %collective-permute-done.10.refs_0_), custom_call_target="tpu_custom_call" | custom-call | flops 1 | bytes 1 | tf_op jit(solution)/shard_map/panel_tile/pallas_call | solution.py:25
  46.5 1.6 %collective-permute-start.12 = (s32[264,128]{1,0:T(8,128)S(1)}, s32[264,128]{1,0:T(8,128)S(1)}, u32[]{:S(2)}, u32[]{:S(2)}) collective-permute-start(s32[264,128]{1,0:T(8,128)S(1)} %get-tuple-element.74), channel_id=1, source_target_pairs={{0,1},{1,0},{2,3},{3,2},{4,5},{5,4},{6,7},{7,6},{8,9},{9,8},{10,11... | collective-permute-start | bytes 405512 | tf_op jit(solution)/shard_map/ppermute | solution.py:327
  48.4 1.2 %collective-permute-done.13.refs_5_ = s32[264,128]{1,0:T(8,128)S(1)} collective-permute-done((s32[264,128]{1,0:T(8,128)S(1)}, s32[264,128]{1,0:T(8,128)S(1)}, u32[]{:S(2)}, u32[]{:S(2)}) %collective-permute-start.13) | collective-permute-done | bytes 135200 | tf_op jit(solution)/shard_map/ppermute | solution.py:327
  49.7 2.9 %collective-permute-done.14.refs_8_ = s32[264,128]{1,0:T(8,128)S(1)} collective-permute-done((s32[264,128]{1,0:T(8,128)S(1)}, s32[264,128]{1,0:T(8,128)S(1)}, u32[]{:S(2)}, u32[]{:S(2)}) %collective-permute-start.14) | collective-permute-done | bytes 135200 | tf_op jit(solution)/shard_map/ppermute | solution.py:327
  52.6 1.9 %finish.4.refs_3_ = f32[256,2048]{1,0:T(8,128)} custom-call(f32[256,128]{1,0:T(8,128)S(1)} %get-tuple-element.45.row_coord, f32[256,128]{1,0:T(8,128)S(1)} %get-tuple-element.46.row_level, f32[8,256]{1,0:T(8,128)S(1)} %get-tuple-element.75.refs_0_, f32[256,256]{1,0:T(8,128)S(1)} %get-tuple-element.76.refs_1_, ...), custom_call_target="tpu_custom_call", output_to_operand_aliasing={{}: (11, {})} | custom-call | flops 1 | bytes 1 | tf_op jit(solution)/shard_map/finish/pallas_call | solution.py:289
  54.4 0.6 %collective-permute-done.12.refs_2_ = s32[264,128]{1,0:T(8,128)S(1)} collective-permute-done((s32[264,128]{1,0:T(8,128)S(1)}, s32[264,128]{1,0:T(8,128)S(1)}, u32[]{:S(2)}, u32[]{:S(2)}) %collective-permute-start.12) | collective-permute-done | bytes 135200 | tf_op jit(solution)/shard_map/ppermute | solution.py:327
  55.0 0.8 %finish.5 = f32[256,2048]{1,0:T(8,128)} custom-call(f32[256,128]{1,0:T(8,128)S(1)} %get-tuple-element.45.row_coord, f32[256,128]{1,0:T(8,128)S(1)} %get-tuple-element.46.row_level, f32[256,256]{1,0:T(8,128)S(1)} %weigh.1.refs_0_, f32[256,256]{1,0:T(8,128)S(1)} %get-tuple-element.73.refs_1_, ...), custom_call_target="tpu_custom_call", output_to_operand_aliasing={{}: (5, {})} | custom-call | flops 1 | bytes 1 | tf_op jit(solution)/shard_map/finish/pallas_call | solution.py:289
  (28 shorter events, 2.7 us)
Async XLA Ops:
  0.0 2.0 %copy-start = (bf16[1536,512]{1,0:T(8,128)(2,1)S(1)}, bf16[1536,512]{1,0:T(8,128)(2,1)}, u32[]{:S(2)}) copy-start(bf16[1536,512]{1,0:T(8,128)(2,1)} %x) | copy-start | bytes 4718596
  0.0 2.0 %copy-start.1 = (s32[512]{0:T(512)S(1)}, s32[512]{0:T(512)}, u32[]{:S(2)}) copy-start(s32[512]{0:T(512)} %param.4) | copy-start | bytes 6148
  0.0 2.8 %copy-start.2 = (s32[512]{0:T(512)S(1)}, s32[512]{0:T(512)}, u32[]{:S(2)}) copy-start(s32[512]{0:T(512)} %param.5) | copy-start | bytes 6148
  1.4 19.0 %collective-permute-start.3 = (bf16[1504,256]{1,0:T(8,128)(2,1)S(1)}, bf16[1504,256]{1,0:T(8,128)(2,1)S(1)}, u32[]{:S(2)}, u32[]{:S(2)}) collective-permute-start(bf16[1504,256]{1,0:T(8,128)(2,1)S(1)} %head.1), channel_id=1, source_target_pairs={{0,4},{2,6},{4,0},{6,2},{8,12},{10,14},{12,8},{14,10},{16,20},{18,... | collective-permute-start | bytes 2310152 | tf_op jit(solution)/shard_map/ppermute | solution.py:316
  2.0 21.5 %collective-permute-start.1 = (bf16[1536,256]{1,0:T(8,128)(2,1)S(1)}, bf16[1536,256]{1,0:T(8,128)(2,1)S(1)}, u32[]{:S(2)}, u32[]{:S(2)}) collective-permute-start(bf16[1536,256]{1,0:T(8,128)(2,1)S(1)} %slice.9.low.whole), channel_id=1, source_target_pairs={{0,26},{2,0},{4,30},{6,4},{8,2},{10,8},{12,6},{14,12},{16,10},{18,... | collective-permute-start | bytes 2359304 | tf_op jit(solution)/shard_map/ppermute | solution.py:316
  2.2 23.7 %collective-permute-start.2 = (bf16[1552,256]{1,0:T(8,128)(2,1)S(1)}, bf16[1552,256]{1,0:T(8,128)(2,1)S(1)}, u32[]{:S(2)}, u32[]{:S(2)}) collective-permute-start(bf16[1552,256]{1,0:T(8,128)(2,1)S(1)} %get-tuple-element.44.high), channel_id=1, source_target_pairs={{0,26},{2,0},{4,30},{6,4},{8,2},{10,8},{12,6},{14,12},{16,10},{18,... | collective-permute-start | bytes 2383880 | tf_op jit(solution)/shard_map/ppermute | solution.py:316
  4.0 19.4 %collective-permute-start = (f32[256,512]{1,0:T(8,128)S(1)}, f32[256,512]{1,0:T(8,128)S(1)}, u32[]{:S(2)}, u32[]{:S(2)}) collective-permute-start(f32[256,512]{1,0:T(8,128)S(1)} %get-tuple-element.48), channel_id=1, source_target_pairs={{0,1},{1,0},{2,3},{3,2},{4,5},{5,4},{6,7},{7,6},{8,9},{9,8},{10,11... | collective-permute-start | bytes 1572872 | tf_op jit(solution)/shard_map/ppermute | solution.py:327
  20.4 16.2 %collective-permute-start.5 = (bf16[1584,128]{1,0:T(8,128)(2,1)S(1)}, bf16[1584,128]{1,0:T(8,128)(2,1)S(1)}, u32[]{:S(2)}, u32[]{:S(2)}) collective-permute-start(bf16[1584,128]{1,0:T(8,128)(2,1)S(1)} %get-tuple-element.54), channel_id=1, source_target_pairs={{0,28},{2,30},{4,0},{6,2},{8,4},{10,6},{12,8},{14,10},{16,12},{18,... | collective-permute-start | bytes 1216520 | tf_op jit(solution)/shard_map/ppermute | solution.py:316
  21.0 15.6 %collective-permute-start.4 = (bf16[1504,128]{1,0:T(8,128)(2,1)S(1)}, bf16[1504,128]{1,0:T(8,128)(2,1)S(1)}, u32[]{:S(2)}, u32[]{:S(2)}) collective-permute-start(bf16[1504,128]{1,0:T(8,128)(2,1)S(1)} %get-tuple-element.52.refs_0_), channel_id=1, source_target_pairs={{4,28},{6,30},{12,4},{14,6},{20,12},{22,14},{28,20},{30,22},{5,29}... | collective-permute-start | bytes 1155080 | tf_op jit(solution)/shard_map/ppermute | solution.py:316
  23.4 19.1 %collective-permute-start.9 = (bf16[1584,128]{1,0:T(8,128)(2,1)S(1)}, bf16[1584,128]{1,0:T(8,128)(2,1)S(1)}, u32[]{:S(2)}, u32[]{:S(2)}) collective-permute-start(bf16[1584,128]{1,0:T(8,128)(2,1)S(1)} %get-tuple-element.64), channel_id=1, source_target_pairs={{0,28},{2,30},{4,0},{6,2},{8,4},{10,6},{12,8},{14,10},{16,12},{18,... | collective-permute-start | bytes 1216520 | tf_op jit(solution)/shard_map/ppermute | solution.py:316
  23.5 19.0 %collective-permute-start.8 = (bf16[1504,128]{1,0:T(8,128)(2,1)S(1)}, bf16[1504,128]{1,0:T(8,128)(2,1)S(1)}, u32[]{:S(2)}, u32[]{:S(2)}) collective-permute-start(bf16[1504,128]{1,0:T(8,128)(2,1)S(1)} %get-tuple-element.62.refs_0_), channel_id=1, source_target_pairs={{4,28},{6,30},{12,4},{14,6},{20,12},{22,14},{28,20},{30,22},{5,29}... | collective-permute-start | bytes 1155080 | tf_op jit(solution)/shard_map/ppermute | solution.py:316
  26.9 11.9 %collective-permute-start.6 = (s32[264,256]{1,0:T(8,128)S(1)}, s32[264,256]{1,0:T(8,128)S(1)}, u32[]{:S(2)}, u32[]{:S(2)}) collective-permute-start(s32[264,256]{1,0:T(8,128)S(1)} %get-tuple-element.59), channel_id=1, source_target_pairs={{0,1},{1,0},{2,3},{3,2},{4,5},{5,4},{6,7},{7,6},{8,9},{9,8},{10,11... | collective-permute-start | bytes 811016 | tf_op jit(solution)/shard_map/ppermute | solution.py:327
  37.2 5.1 %collective-permute-start.7 = (s32[264,128]{1,0:T(8,128)S(1)}, s32[264,128]{1,0:T(8,128)S(1)}, u32[]{:S(2)}, u32[]{:S(2)}) collective-permute-start(s32[264,128]{1,0:T(8,128)S(1)} %get-tuple-element.60), channel_id=1, source_target_pairs={{0,1},{1,0},{2,3},{3,2},{4,5},{5,4},{6,7},{7,6},{8,9},{9,8},{10,11... | collective-permute-start | bytes 405512 | tf_op jit(solution)/shard_map/ppermute | solution.py:327
  38.8 6.0 %collective-permute-start.10 = (bf16[1552,256]{1,0:T(8,128)(2,1)S(1)}, bf16[1552,256]{1,0:T(8,128)(2,1)S(1)}, u32[]{:S(2)}, u32[]{:S(2)}) collective-permute-start(bf16[1552,256]{1,0:T(8,128)(2,1)S(1)} %get-tuple-element.67), channel_id=1, source_target_pairs={{0,2},{2,0},{4,6},{6,4},{8,10},{10,8},{12,14},{14,12},{16,18},{18,... | collective-permute-start | bytes 2383880 | tf_op jit(solution)/shard_map/ppermute | solution.py:316
  43.1 2.8 %collective-permute-start.11 = (bf16[1552,256]{1,0:T(8,128)(2,1)S(1)}, bf16[1552,256]{1,0:T(8,128)(2,1)S(1)}, u32[]{:S(2)}, u32[]{:S(2)}) collective-permute-start(bf16[1552,256]{1,0:T(8,128)(2,1)S(1)} %get-tuple-element.70), channel_id=1, source_target_pairs={{0,2},{2,0},{4,6},{6,4},{8,10},{10,8},{12,14},{14,12},{16,18},{18,... | collective-permute-start | bytes 2383880 | tf_op jit(solution)/shard_map/ppermute | solution.py:316
  43.2 6.5 %collective-permute-start.13 = (s32[264,128]{1,0:T(8,128)S(1)}, s32[264,128]{1,0:T(8,128)S(1)}, u32[]{:S(2)}, u32[]{:S(2)}) collective-permute-start(s32[264,128]{1,0:T(8,128)S(1)} %get-tuple-element.78), channel_id=1, source_target_pairs={{0,1},{1,0},{2,3},{3,2},{4,5},{5,4},{6,7},{7,6},{8,9},{9,8},{10,11... | collective-permute-start | bytes 405512 | tf_op jit(solution)/shard_map/ppermute | solution.py:327
  45.4 7.2 %collective-permute-start.14 = (s32[264,128]{1,0:T(8,128)S(1)}, s32[264,128]{1,0:T(8,128)S(1)}, u32[]{:S(2)}, u32[]{:S(2)}) collective-permute-start(s32[264,128]{1,0:T(8,128)S(1)} %get-tuple-element.80), channel_id=1, source_target_pairs={{0,1},{1,0},{2,3},{3,2},{4,5},{5,4},{6,7},{7,6},{8,9},{9,8},{10,11... | collective-permute-start | bytes 405512 | tf_op jit(solution)/shard_map/ppermute | solution.py:327
  46.5 8.5 %collective-permute-start.12 = (s32[264,128]{1,0:T(8,128)S(1)}, s32[264,128]{1,0:T(8,128)S(1)}, u32[]{:S(2)}, u32[]{:S(2)}) collective-permute-start(s32[264,128]{1,0:T(8,128)S(1)} %get-tuple-element.74), channel_id=1, source_target_pairs={{0,1},{1,0},{2,3},{3,2},{4,5},{5,4},{6,7},{7,6},{8,9},{9,8},{10,11... | collective-permute-start | bytes 405512 | tf_op jit(solution)/shard_map/ppermute | solution.py:327

commit v11 on v10

--- a/solution.py
+++ b/solution.py
@@ -40,13 +40,13 @@
     return jnp.where(r <= 1.0, near, jnp.where(r <= 2.0, far, 0.0))
 
 
-def prepare_kernel(x, coord, high, *parts):
-    members, width = x.shape
-    half = width // 2
+def prepare_kernel(x, tail, coord, high, *parts):
+    members, half = x.shape
+    width = 2 * half
     first = 4 * width * lax.axis_index("mesh")
     jitter = coord[...] - first - 4 * lax.broadcasted_iota(jnp.int32, (1, width), 1)
     jitter = jitter.astype(F32)
-    high[:members, :] = x[:, half:]
+    high[:members, :] = x[...]
     high[members:, :] = jnp.concatenate(
         [jnp.broadcast_to(jitter[:, :half], (PAD // 2, half)), jnp.broadcast_to(jitter[:, half:], (PAD // 2, half))],
         axis=0,
@@ -54,7 +54,7 @@
     for i, part in enumerate(parts):
         span = slice(i * CHUNK, (i + 1) * CHUNK)
         part[: members + PAD, :] = high[:, span]
-        part[members + PAD :, :] = x[members - TAIL :, span]
+        part[members + PAD :, :] = tail[:, span]
 
 
 def cut_kernel(whole, *parts):
@@ -77,11 +77,11 @@
     return call(head_kernel, [short], panel, name="head")[0]
 
 
-def prepare(x, coord):
-    members, width = x.shape
-    outs = [jax.ShapeDtypeStruct((members + PAD, width // 2), x.dtype)]
-    outs += [jax.ShapeDtypeStruct((members + PAD + TAIL, CHUNK), x.dtype)] * (width // 2 // CHUNK)
-    return call(prepare_kernel, outs, x, coord, name="prepare")
+def prepare(x, tail, coord):
+    members, half = x.shape
+    outs = [jax.ShapeDtypeStruct((members + PAD, half), x.dtype)]
+    outs += [jax.ShapeDtypeStruct((members + PAD + TAIL, CHUNK), x.dtype)] * (half // CHUNK)
+    return call(prepare_kernel, outs, x, tail, coord, name="prepare")
 
 
 def own_kernel(low, high, coord, level, lt, row_coord, row_level, *outs, owned, split):
@@ -329,7 +329,8 @@
 
     half = width // 2
     low = perturbations[:, :half]
-    high, *highs = prepare(after(perturbations, low), coord)
+    rest = after(perturbations, low)
+    high, *highs = prepare(rest[:, half:], rest[members - TAIL :, :half], coord)
     lt, row_coord, row_level, *own = own_tile(low, high, coord, levels, owned, rows)
     own_parts = reduced(own)
     own_cols = jnp.concatenate([high[members : members + PAD // 2], high[members + PAD // 2 :]], axis=1).astype(F32)

time: 56.2 us -> 56.2 us (level)
  no operation moved by 1% of the time
where the time goes in v11:
time: 56.2 us; the launch traced here: 55.8 us
  waiting for transfers between devices  28.9 us (51%)
  starting transfers between devices  15.2 us (27%)
  Pallas kernels  10.1 us (18%)
  local copies, waits for them, and re-layouts  1.37 us (2%)
    ppermute x9, waiting for transfers between devices, permute(): return lax.ppermute(array, 'mesh', pairs)  22.9 us
    ppermute x6, starting transfers between devices, reduced(): lax.ppermute(a, 'mem', [(0, 1), (1, 0)])  8.57 us
    ppermute x9, starting transfers between devices, permute(): return lax.ppermute(array, 'mesh', pairs)  6.59 us
    ppermute x6, waiting for transfers between devices, reduced(): lax.ppermute(a, 'mem', [(0, 1), (1, 0)])  5.99 us
    pallas_call x10, Pallas kernels, call(): pl.pallas_call(kernel, out_shape=outs, in_specs=[VMEM] * len(operands), o...  5.31 us
    pallas_call x3, Pallas kernels, finish(): pl.pallas_call(functools.partial(finish_kernel, plan=plan, period=period,...  4.81 us
    slice x1, local copies, waits for them, and re-layouts, per_device(): low = perturbations[:, :half]  1.3 us
  transfers between devices with their start and end apart: 15, of which 7 were waited for; matrix products, arithmetic and copies ran while one was open for 0% of the time, Pallas kernels for 17%

profile of v11, /device:TPU:26, one launch (start us, length us, event | category | flops | bytes accessed | tf_op | source)
XLA Modules:
  0.0 55.8 jit_solution(9477817895754808641)
XLA Ops:
  0.0 1.3 %slice.15.low.whole = bf16[1536,256]{1,0:T(8,128)(2,1)S(1)} slice(bf16[1536,512]{1,0:T(8,128)(2,1)} %param.3), slice={[0:1536], [0:256]} | slice | bytes 1572864 | tf_op jit(solution)/shard_map/slice | solution.py:331
  1.4 0.6 %collective-permute-start.3 = (bf16[1504,256]{1,0:T(8,128)(2,1)S(1)}, bf16[1504,256]{1,0:T(8,128)(2,1)S(1)}, u32[]{:S(2)}, u32[]{:S(2)}) collective-permute-start(bf16[1504,256]{1,0:T(8,128)(2,1)S(1)} %head.1), channel_id=1, source_target_pairs={{0,4},{2,6},{4,0},{6,2},{8,12},{10,14},{12,8},{14,10},{16,20},{18,... | collective-permute-start | bytes 2310152 | tf_op jit(solution)/shard_map/ppermute | solution.py:316
  2.3 0.6 %collective-permute-start.2 = (bf16[1552,256]{1,0:T(8,128)(2,1)S(1)}, bf16[1552,256]{1,0:T(8,128)(2,1)S(1)}, u32[]{:S(2)}, u32[]{:S(2)}) collective-permute-start(bf16[1552,256]{1,0:T(8,128)(2,1)S(1)} %get-tuple-element.44.high), channel_id=1, source_target_pairs={{0,26},{2,0},{4,30},{6,4},{8,2},{10,8},{12,6},{14,12},{16,10},{18,... | collective-permute-start | bytes 2383880 | tf_op jit(solution)/shard_map/ppermute | solution.py:316
  2.9 1.2 %own_tile.1 = (bf16[512,1536]{1,0:T(8,128)(2,1)S(1)}, f32[256,128]{1,0:T(8,128)S(1)}, f32[256,128]{1,0:T(8,128)S(1)}, f32[256,512]{1,0:T(8,128)S(1)}, f32[256,512]{1,0:T(8,128)S(1)}) custom-call(bf16[1536,256]{1,0:T(8,128)(2,1)S(1)} %slice.15.low.whole, bf16[1552,256]{1,0:T(8,128)(2,1)S(1)} %get-tuple-element.44.high, s32[1,512]{1,0:T(1,128)S(1)} %bitcast.3, ...), custom_call_target="tpu_custom_call" | custom-call | flops 1 | bytes 1 | tf_op jit(solution)/shard_map/own_tile/pallas_call | solution.py:25
  4.1 1.7 %collective-permute-start = (f32[256,512]{1,0:T(8,128)S(1)}, f32[256,512]{1,0:T(8,128)S(1)}, u32[]{:S(2)}, u32[]{:S(2)}) collective-permute-start(f32[256,512]{1,0:T(8,128)S(1)} %get-tuple-element.48), channel_id=1, source_target_pairs={{0,1},{1,0},{2,3},{3,2},{4,5},{5,4},{6,7},{7,6},{8,9},{9,8},{10,11... | collective-permute-start | bytes 1572872 | tf_op jit(solution)/shard_map/ppermute | solution.py:327
  5.8 14.6 %collective-permute-done.3.whole = bf16[1504,256]{1,0:T(8,128)(2,1)S(1)} collective-permute-done((bf16[1504,256]{1,0:T(8,128)(2,1)S(1)}, bf16[1504,256]{1,0:T(8,128)(2,1)S(1)}, u32[]{:S(2)}, u32[]{:S(2)}) %collective-permute-start.3) | collective-permute-done | bytes 770080 | tf_op jit(solution)/shard_map/ppermute | solution.py:316
  21.0 2.4 %collective-permute-start.4 = (bf16[1504,128]{1,0:T(8,128)(2,1)S(1)}, bf16[1504,128]{1,0:T(8,128)(2,1)S(1)}, u32[]{:S(2)}, u32[]{:S(2)}) collective-permute-start(bf16[1504,128]{1,0:T(8,128)(2,1)S(1)} %get-tuple-element.52.refs_0_), channel_id=1, source_target_pairs={{4,28},{6,30},{12,4},{14,6},{20,12},{22,14},{28,20},{30,22},{5,29}... | collective-permute-start | bytes 1155080 | tf_op jit(solution)/shard_map/ppermute | solution.py:316
  23.5 2.4 %collective-permute-start.8 = (bf16[1504,128]{1,0:T(8,128)(2,1)S(1)}, bf16[1504,128]{1,0:T(8,128)(2,1)S(1)}, u32[]{:S(2)}, u32[]{:S(2)}) collective-permute-start(bf16[1504,128]{1,0:T(8,128)(2,1)S(1)} %get-tuple-element.62.refs_0_), channel_id=1, source_target_pairs={{4,28},{6,30},{12,4},{14,6},{20,12},{22,14},{28,20},{30,22},{5,29}... | collective-permute-start | bytes 1155080 | tf_op jit(solution)/shard_map/ppermute | solution.py:316
  25.9 1.0 %panel_tile.5 = (f32[8,512]{1,0:T(8,128)S(1)}, s32[264,256]{1,0:T(8,128)S(1)}, f32[256,512]{1,0:T(8,128)S(1)}) custom-call(bf16[512,1536]{1,0:T(8,128)(2,1)S(1)} %get-tuple-element.69.lt, bf16[1536,256]{1,0:T(8,128)(2,1)S(1)} %collective-permute-done.1.refs_0_, bf16[1552,256]{1,0:T(8,128)(2,1)S(1)} %collective-permute-done.2.refs_1_), custom_call_target="tpu_custom_call" | custom-call | flops 1 | bytes 1 | tf_op jit(solution)/shard_map/panel_tile/pallas_call | solution.py:25
  26.9 1.6 %collective-permute-start.6 = (s32[264,256]{1,0:T(8,128)S(1)}, s32[264,256]{1,0:T(8,128)S(1)}, u32[]{:S(2)}, u32[]{:S(2)}) collective-permute-start(s32[264,256]{1,0:T(8,128)S(1)} %get-tuple-element.59), channel_id=1, source_target_pairs={{0,1},{1,0},{2,3},{3,2},{4,5},{5,4},{6,7},{7,6},{8,9},{9,8},{10,11... | collective-permute-start | bytes 811016 | tf_op jit(solution)/shard_map/ppermute | solution.py:327
  28.5 8.1 %collective-permute-done.4.refs_1_ = bf16[1504,128]{1,0:T(8,128)(2,1)S(1)} collective-permute-done((bf16[1504,128]{1,0:T(8,128)(2,1)S(1)}, bf16[1504,128]{1,0:T(8,128)(2,1)S(1)}, u32[]{:S(2)}, u32[]{:S(2)}) %collective-permute-start.4) | collective-permute-done | bytes 385056 | tf_op jit(solution)/shard_map/ppermute | solution.py:316
  36.6 0.6 %panel_tile.6 = (f32[8,256]{1,0:T(8,128)S(1)}, s32[264,128]{1,0:T(8,128)S(1)}, f32[256,256]{1,0:T(8,128)S(1)}, bf16[1552,256]{1,0:T(8,128)(2,1)S(1)}) custom-call(bf16[512,1536]{1,0:T(8,128)(2,1)S(1)} %get-tuple-element.69.lt, bf16[1504,128]{1,0:T(8,128)(2,1)S(1)} %get-tuple-element.52.refs_0_, bf16[1504,128]{1,0:T(8,128)(2,1)S(1)} %collective-permute-done.4.refs_1_, ...), custom_call_target="tpu_custom_call" | custom-call | flops 1 | bytes 1 | tf_op jit(solution)/shard_map/panel_tile/pallas_call | solution.py:25
  37.2 1.6 %collective-permute-start.7 = (s32[264,128]{1,0:T(8,128)S(1)}, s32[264,128]{1,0:T(8,128)S(1)}, u32[]{:S(2)}, u32[]{:S(2)}) collective-permute-start(s32[264,128]{1,0:T(8,128)S(1)} %get-tuple-element.60), channel_id=1, source_target_pairs={{0,1},{1,0},{2,3},{3,2},{4,5},{5,4},{6,7},{7,6},{8,9},{9,8},{10,11... | collective-permute-start | bytes 405512 | tf_op jit(solution)/shard_map/ppermute | solution.py:327
  38.8 2.2 %finish.3.refs_9_ = f32[256,2048]{1,0:T(8,128)} custom-call(f32[256,128]{1,0:T(8,128)S(1)} %get-tuple-element.45.row_coord, f32[256,128]{1,0:T(8,128)S(1)} %get-tuple-element.46.row_level, f32[8,512]{1,0:T(8,128)S(1)} %maximum_convert_fusion.refs_0_, f32[256,512]{1,0:T(8,128)S(1)} %get-tuple-element.57.refs_1_, f32[256,512]{1,0:T(8,128)S(1)} %collective-permute-done.refs_2_, ...), custom_call_target="tpu_custom_call" | custom-call | flops 1 | bytes 1 | tf_op jit(solution)/shard_map/finish/pallas_call | solution.py:289
  41.0 1.3 %collective-permute-done.7.refs_2_ = s32[264,128]{1,0:T(8,128)S(1)} collective-permute-done((s32[264,128]{1,0:T(8,128)S(1)}, s32[264,128]{1,0:T(8,128)S(1)}, u32[]{:S(2)}, u32[]{:S(2)}) %collective-permute-start.7) | collective-permute-done | bytes 135200 | tf_op jit(solution)/shard_map/ppermute | solution.py:327
  42.5 0.6 %panel_tile.7 = (f32[8,256]{1,0:T(8,128)S(1)}, s32[264,128]{1,0:T(8,128)S(1)}, f32[256,256]{1,0:T(8,128)S(1)}, bf16[1552,256]{1,0:T(8,128)(2,1)S(1)}) custom-call(bf16[512,1536]{1,0:T(8,128)(2,1)S(1)} %get-tuple-element.69.lt, bf16[1504,128]{1,0:T(8,128)(2,1)S(1)} %get-tuple-element.62.refs_0_, bf16[1504,128]{1,0:T(8,128)(2,1)S(1)} %collective-permute-done.8.refs_1_, ...), custom_call_target="tpu_custom_call" | custom-call | flops 1 | bytes 1 | tf_op jit(solution)/shard_map/panel_tile/pallas_call | solution.py:25
  43.2 1.6 %collective-permute-start.13 = (s32[264,128]{1,0:T(8,128)S(1)}, s32[264,128]{1,0:T(8,128)S(1)}, u32[]{:S(2)}, u32[]{:S(2)}) collective-permute-start(s32[264,128]{1,0:T(8,128)S(1)} %get-tuple-element.78), channel_id=1, source_target_pairs={{0,1},{1,0},{2,3},{3,2},{4,5},{5,4},{6,7},{7,6},{8,9},{9,8},{10,11... | collective-permute-start | bytes 405512 | tf_op jit(solution)/shard_map/ppermute | solution.py:327
  46.0 0.6 %panel_tile.9 = (f32[8,256]{1,0:T(8,128)S(1)}, s32[264,128]{1,0:T(8,128)S(1)}, f32[256,256]{1,0:T(8,128)S(1)}) custom-call(bf16[512,1536]{1,0:T(8,128)(2,1)S(1)} %get-tuple-element.69.lt, bf16[1552,256]{1,0:T(8,128)(2,1)S(1)} %collective-permute-done.11.refs_0_), custom_call_target="tpu_custom_call" | custom-call | flops 1 | bytes 1 | tf_op jit(solution)/shard_map/panel_tile/pallas_call | solution.py:25
  46.6 1.6 %collective-permute-start.12 = (s32[264,128]{1,0:T(8,128)S(1)}, s32[264,128]{1,0:T(8,128)S(1)}, u32[]{:S(2)}, u32[]{:S(2)}) collective-permute-start(s32[264,128]{1,0:T(8,128)S(1)} %get-tuple-element.74), channel_id=1, source_target_pairs={{0,1},{1,0},{2,3},{3,2},{4,5},{5,4},{6,7},{7,6},{8,9},{9,8},{10,11... | collective-permute-start | bytes 405512 | tf_op jit(solution)/shard_map/ppermute | solution.py:327
  48.4 1.2 %collective-permute-done.13.refs_5_ = s32[264,128]{1,0:T(8,128)S(1)} collective-permute-done((s32[264,128]{1,0:T(8,128)S(1)}, s32[264,128]{1,0:T(8,128)S(1)}, u32[]{:S(2)}, u32[]{:S(2)}) %collective-permute-start.13) | collective-permute-done | bytes 135200 | tf_op jit(solution)/shard_map/ppermute | solution.py:327
  49.7 2.9 %collective-permute-done.14.refs_8_ = s32[264,128]{1,0:T(8,128)S(1)} collective-permute-done((s32[264,128]{1,0:T(8,128)S(1)}, s32[264,128]{1,0:T(8,128)S(1)}, u32[]{:S(2)}, u32[]{:S(2)}) %collective-permute-start.14) | collective-permute-done | bytes 135200 | tf_op jit(solution)/shard_map/ppermute | solution.py:327
  52.6 1.8 %finish.4.refs_3_ = f32[256,2048]{1,0:T(8,128)} custom-call(f32[256,128]{1,0:T(8,128)S(1)} %get-tuple-element.45.row_coord, f32[256,128]{1,0:T(8,128)S(1)} %get-tuple-element.46.row_level, f32[8,256]{1,0:T(8,128)S(1)} %get-tuple-element.75.refs_0_, f32[256,256]{1,0:T(8,128)S(1)} %get-tuple-element.76.refs_1_, ...), custom_call_target="tpu_custom_call", output_to_operand_aliasing={{}: (11, {})} | custom-call | flops 1 | bytes 1 | tf_op jit(solution)/shard_map/finish/pallas_call | solution.py:289
  54.4 0.6 %collective-permute-done.12.refs_2_ = s32[264,128]{1,0:T(8,128)S(1)} collective-permute-done((s32[264,128]{1,0:T(8,128)S(1)}, s32[264,128]{1,0:T(8,128)S(1)}, u32[]{:S(2)}, u32[]{:S(2)}) %collective-permute-start.12) | collective-permute-done | bytes 135200 | tf_op jit(solution)/shard_map/ppermute | solution.py:327
  55.0 0.8 %finish.5 = f32[256,2048]{1,0:T(8,128)} custom-call(f32[256,128]{1,0:T(8,128)S(1)} %get-tuple-element.45.row_coord, f32[256,128]{1,0:T(8,128)S(1)} %get-tuple-element.46.row_level, f32[256,256]{1,0:T(8,128)S(1)} %weigh.1.refs_0_, f32[256,256]{1,0:T(8,128)S(1)} %get-tuple-element.73.refs_1_, ...), custom_call_target="tpu_custom_call", output_to_operand_aliasing={{}: (5, {})} | custom-call | flops 1 | bytes 1 | tf_op jit(solution)/shard_map/finish/pallas_call | solution.py:289
  (30 shorter events, 2.8 us)
Async XLA Ops:
  0.0 2.0 %copy-start.2 = (bf16[1536,512]{1,0:T(8,128)(2,1)S(1)}, bf16[1536,512]{1,0:T(8,128)(2,1)}, u32[]{:S(2)}) copy-start(bf16[1536,512]{1,0:T(8,128)(2,1)} %param.3) | copy-start | bytes 4718596
  0.0 2.1 %copy-start = (s32[512]{0:T(512)S(1)}, s32[512]{0:T(512)}, u32[]{:S(2)}) copy-start(s32[512]{0:T(512)} %param.4) | copy-start | bytes 6148
  1.3 1.6 %copy-start.1 = (s32[512]{0:T(512)S(1)}, s32[512]{0:T(512)}, u32[]{:S(2)}) copy-start(s32[512]{0:T(512)} %param.5) | copy-start | bytes 6148
  1.4 19.0 %collective-permute-start.3 = (bf16[1504,256]{1,0:T(8,128)(2,1)S(1)}, bf16[1504,256]{1,0:T(8,128)(2,1)S(1)}, u32[]{:S(2)}, u32[]{:S(2)}) collective-permute-start(bf16[1504,256]{1,0:T(8,128)(2,1)S(1)} %head.1), channel_id=1, source_target_pairs={{0,4},{2,6},{4,0},{6,2},{8,12},{10,14},{12,8},{14,10},{16,20},{18,... | collective-permute-start | bytes 2310152 | tf_op jit(solution)/shard_map/ppermute | solution.py:316
  2.0 21.5 %collective-permute-start.1 = (bf16[1536,256]{1,0:T(8,128)(2,1)S(1)}, bf16[1536,256]{1,0:T(8,128)(2,1)S(1)}, u32[]{:S(2)}, u32[]{:S(2)}) collective-permute-start(bf16[1536,256]{1,0:T(8,128)(2,1)S(1)} %slice.15.low.whole), channel_id=1, source_target_pairs={{0,26},{2,0},{4,30},{6,4},{8,2},{10,8},{12,6},{14,12},{16,10},{18,... | collective-permute-start | bytes 2359304 | tf_op jit(solution)/shard_map/ppermute | solution.py:316
  2.3 23.6 %collective-permute-start.2 = (bf16[1552,256]{1,0:T(8,128)(2,1)S(1)}, bf16[1552,256]{1,0:T(8,128)(2,1)S(1)}, u32[]{:S(2)}, u32[]{:S(2)}) collective-permute-start(bf16[1552,256]{1,0:T(8,128)(2,1)S(1)} %get-tuple-element.44.high), channel_id=1, source_target_pairs={{0,26},{2,0},{4,30},{6,4},{8,2},{10,8},{12,6},{14,12},{16,10},{18,... | collective-permute-start | bytes 2383880 | tf_op jit(solution)/shard_map/ppermute | solution.py:316
  4.1 19.3 %collective-permute-start = (f32[256,512]{1,0:T(8,128)S(1)}, f32[256,512]{1,0:T(8,128)S(1)}, u32[]{:S(2)}, u32[]{:S(2)}) collective-permute-start(f32[256,512]{1,0:T(8,128)S(1)} %get-tuple-element.48), channel_id=1, source_target_pairs={{0,1},{1,0},{2,3},{3,2},{4,5},{5,4},{6,7},{7,6},{8,9},{9,8},{10,11... | collective-permute-start | bytes 1572872 | tf_op jit(solution)/shard_map/ppermute | solution.py:327
  20.4 16.2 %collective-permute-start.5 = (bf16[1584,128]{1,0:T(8,128)(2,1)S(1)}, bf16[1584,128]{1,0:T(8,128)(2,1)S(1)}, u32[]{:S(2)}, u32[]{:S(2)}) collective-permute-start(bf16[1584,128]{1,0:T(8,128)(2,1)S(1)} %get-tuple-element.54), channel_id=1, source_target_pairs={{0,28},{2,30},{4,0},{6,2},{8,4},{10,6},{12,8},{14,10},{16,12},{18,... | collective-permute-start | bytes 1216520 | tf_op jit(solution)/shard_map/ppermute | solution.py:316
  21.0 15.6 %collective-permute-start.4 = (bf16[1504,128]{1,0:T(8,128)(2,1)S(1)}, bf16[1504,128]{1,0:T(8,128)(2,1)S(1)}, u32[]{:S(2)}, u32[]{:S(2)}) collective-permute-start(bf16[1504,128]{1,0:T(8,128)(2,1)S(1)} %get-tuple-element.52.refs_0_), channel_id=1, source_target_pairs={{4,28},{6,30},{12,4},{14,6},{20,12},{22,14},{28,20},{30,22},{5,29}... | collective-permute-start | bytes 1155080 | tf_op jit(solution)/shard_map/ppermute | solution.py:316
  23.4 19.1 %collective-permute-start.9 = (bf16[1584,128]{1,0:T(8,128)(2,1)S(1)}, bf16[1584,128]{1,0:T(8,128)(2,1)S(1)}, u32[]{:S(2)}, u32[]{:S(2)}) collective-permute-start(bf16[1584,128]{1,0:T(8,128)(2,1)S(1)} %get-tuple-element.64), channel_id=1, source_target_pairs={{0,28},{2,30},{4,0},{6,2},{8,4},{10,6},{12,8},{14,10},{16,12},{18,... | collective-permute-start | bytes 1216520 | tf_op jit(solution)/shard_map/ppermute | solution.py:316
  23.5 19.0 %collective-permute-start.8 = (bf16[1504,128]{1,0:T(8,128)(2,1)S(1)}, bf16[1504,128]{1,0:T(8,128)(2,1)S(1)}, u32[]{:S(2)}, u32[]{:S(2)}) collective-permute-start(bf16[1504,128]{1,0:T(8,128)(2,1)S(1)} %get-tuple-element.62.refs_0_), channel_id=1, source_target_pairs={{4,28},{6,30},{12,4},{14,6},{20,12},{22,14},{28,20},{30,22},{5,29}... | collective-permute-start | bytes 1155080 | tf_op jit(solution)/shard_map/ppermute | solution.py:316
  26.9 11.9 %collective-permute-start.6 = (s32[264,256]{1,0:T(8,128)S(1)}, s32[264,256]{1,0:T(8,128)S(1)}, u32[]{:S(2)}, u32[]{:S(2)}) collective-permute-start(s32[264,256]{1,0:T(8,128)S(1)} %get-tuple-element.59), channel_id=1, source_target_pairs={{0,1},{1,0},{2,3},{3,2},{4,5},{5,4},{6,7},{7,6},{8,9},{9,8},{10,11... | collective-permute-start | bytes 811016 | tf_op jit(solution)/shard_map/ppermute | solution.py:327
  37.2 5.1 %collective-permute-start.7 = (s32[264,128]{1,0:T(8,128)S(1)}, s32[264,128]{1,0:T(8,128)S(1)}, u32[]{:S(2)}, u32[]{:S(2)}) collective-permute-start(s32[264,128]{1,0:T(8,128)S(1)} %get-tuple-element.60), channel_id=1, source_target_pairs={{0,1},{1,0},{2,3},{3,2},{4,5},{5,4},{6,7},{7,6},{8,9},{9,8},{10,11... | collective-permute-start | bytes 405512 | tf_op jit(solution)/shard_map/ppermute | solution.py:327
  38.8 6.0 %collective-permute-start.10 = (bf16[1552,256]{1,0:T(8,128)(2,1)S(1)}, bf16[1552,256]{1,0:T(8,128)(2,1)S(1)}, u32[]{:S(2)}, u32[]{:S(2)}) collective-permute-start(bf16[1552,256]{1,0:T(8,128)(2,1)S(1)} %get-tuple-element.67), channel_id=1, source_target_pairs={{0,2},{2,0},{4,6},{6,4},{8,10},{10,8},{12,14},{14,12},{16,18},{18,... | collective-permute-start | bytes 2383880 | tf_op jit(solution)/shard_map/ppermute | solution.py:316
  43.1 2.8 %collective-permute-start.11 = (bf16[1552,256]{1,0:T(8,128)(2,1)S(1)}, bf16[1552,256]{1,0:T(8,128)(2,1)S(1)}, u32[]{:S(2)}, u32[]{:S(2)}) collective-permute-start(bf16[1552,256]{1,0:T(8,128)(2,1)S(1)} %get-tuple-element.70), channel_id=1, source_target_pairs={{0,2},{2,0},{4,6},{6,4},{8,10},{10,8},{12,14},{14,12},{16,18},{18,... | collective-permute-start | bytes 2383880 | tf_op jit(solution)/shard_map/ppermute | solution.py:316
  43.2 6.5 %collective-permute-start.13 = (s32[264,128]{1,0:T(8,128)S(1)}, s32[264,128]{1,0:T(8,128)S(1)}, u32[]{:S(2)}, u32[]{:S(2)}) collective-permute-start(s32[264,128]{1,0:T(8,128)S(1)} %get-tuple-element.78), channel_id=1, source_target_pairs={{0,1},{1,0},{2,3},{3,2},{4,5},{5,4},{6,7},{7,6},{8,9},{9,8},{10,11... | collective-permute-start | bytes 405512 | tf_op jit(solution)/shard_map/ppermute | solution.py:327
  45.4 7.2 %collective-permute-start.14 = (s32[264,128]{1,0:T(8,128)S(1)}, s32[264,128]{1,0:T(8,128)S(1)}, u32[]{:S(2)}, u32[]{:S(2)}) collective-permute-start(s32[264,128]{1,0:T(8,128)S(1)} %get-tuple-element.80), channel_id=1, source_target_pairs={{0,1},{1,0},{2,3},{3,2},{4,5},{5,4},{6,7},{7,6},{8,9},{9,8},{10,11... | collective-permute-start | bytes 405512 | tf_op jit(solution)/shard_map/ppermute | solution.py:327
  46.6 8.5 %collective-permute-start.12 = (s32[264,128]{1,0:T(8,128)S(1)}, s32[264,128]{1,0:T(8,128)S(1)}, u32[]{:S(2)}, u32[]{:S(2)}) collective-permute-start(s32[264,128]{1,0:T(8,128)S(1)} %get-tuple-element.74), channel_id=1, source_target_pairs={{0,1},{1,0},{2,3},{3,2},{4,5},{5,4},{6,7},{7,6},{8,9},{9,8},{10,11... | collective-permute-start | bytes 405512 | tf_op jit(solution)/shard_map/ppermute | solution.py:327

commit v12 on v10

--- a/solution.py
+++ b/solution.py
@@ -357,7 +357,7 @@
     out = finished(None, cols0, (own_cols, own_parts, "own", whole), (extra_cols, extra_parts, "extra", whole))
     cols1, *parts1, two1 = tile([near[1], passed[1], straight[1]], sides, out, parts0[-1], keep=True)
     parts1 = reduced(parts1)
-    other0, other1 = permute(two0, siblings), permute(two1, siblings)
+    other0, other1 = permute(after(two0, out), siblings), permute(two1, siblings)
     other_cols0, *other_parts0 = tile([other0], [[0]], cols1)
     other_parts0 = reduced(other_parts0)
     other_cols1, *other_parts1 = tile([other1], [[0]], other_cols0)

time: 56.2 us -> 56.2 us (level)
  no operation moved by 1% of the time
where the time goes in v12:
time: 56.2 us; the launch traced here: 55.8 us
  waiting for transfers between devices  28.9 us (51%)
  starting transfers between devices  15.3 us (27%)
  Pallas kernels  10.1 us (18%)
  local copies, waits for them, and re-layouts  1.32 us (2%)
    ppermute x9, waiting for transfers between devices, permute(): return lax.ppermute(array, 'mesh', pairs)  23 us
    ppermute x6, starting transfers between devices, reduced(): lax.ppermute(a, 'mem', [(0, 1), (1, 0)])  8.59 us
    ppermute x9, starting transfers between devices, permute(): return lax.ppermute(array, 'mesh', pairs)  6.66 us
    ppermute x6, waiting for transfers between devices, reduced(): lax.ppermute(a, 'mem', [(0, 1), (1, 0)])  5.92 us
    pallas_call x10, Pallas kernels, call(): pl.pallas_call(kernel, out_shape=outs, in_specs=[VMEM] * len(operands), o...  5.3 us
    pallas_call x3, Pallas kernels, finish(): pl.pallas_call(functools.partial(finish_kernel, plan=plan, period=period,...  4.81 us
    slice x1, local copies, waits for them, and re-layouts, per_device(): low = perturbations[:, :half]  1.3 us
  transfers between devices with their start and end apart: 15, of which 7 were waited for; matrix products, arithmetic and copies ran while one was open for 0% of the time, Pallas kernels for 17%

profile of v12, /device:TPU:26, one launch (start us, length us, event | category | flops | bytes accessed | tf_op | source)
XLA Modules:
  0.0 55.8 jit_solution(14931437517313119355)
XLA Ops:
  0.0 1.3 %slice.9.low.whole = bf16[1536,256]{1,0:T(8,128)(2,1)S(1)} slice(bf16[1536,512]{1,0:T(8,128)(2,1)} %x), slice={[0:1536], [0:256]} | slice | bytes 1572864 | tf_op jit(solution)/shard_map/slice | solution.py:331
  1.4 0.6 %collective-permute-start.3 = (bf16[1504,256]{1,0:T(8,128)(2,1)S(1)}, bf16[1504,256]{1,0:T(8,128)(2,1)S(1)}, u32[]{:S(2)}, u32[]{:S(2)}) collective-permute-start(bf16[1504,256]{1,0:T(8,128)(2,1)S(1)} %head.1), channel_id=1, source_target_pairs={{0,4},{2,6},{4,0},{6,2},{8,12},{10,14},{12,8},{14,10},{16,20},{18,... | collective-permute-start | bytes 2310152 | tf_op jit(solution)/shard_map/ppermute | solution.py:316
  2.2 0.6 %collective-permute-start.2 = (bf16[1552,256]{1,0:T(8,128)(2,1)S(1)}, bf16[1552,256]{1,0:T(8,128)(2,1)S(1)}, u32[]{:S(2)}, u32[]{:S(2)}) collective-permute-start(bf16[1552,256]{1,0:T(8,128)(2,1)S(1)} %get-tuple-element.45.high), channel_id=1, source_target_pairs={{0,26},{2,0},{4,30},{6,4},{8,2},{10,8},{12,6},{14,12},{16,10},{18,... | collective-permute-start | bytes 2383880 | tf_op jit(solution)/shard_map/ppermute | solution.py:316
  2.8 1.2 %own_tile.1 = (bf16[512,1536]{1,0:T(8,128)(2,1)S(1)}, f32[256,128]{1,0:T(8,128)S(1)}, f32[256,128]{1,0:T(8,128)S(1)}, f32[256,512]{1,0:T(8,128)S(1)}, f32[256,512]{1,0:T(8,128)S(1)}) custom-call(bf16[1536,256]{1,0:T(8,128)(2,1)S(1)} %slice.9.low.whole, bf16[1552,256]{1,0:T(8,128)(2,1)S(1)} %get-tuple-element.45.high, s32[1,512]{1,0:T(1,128)S(1)} %bitcast.3, ...), custom_call_target="tpu_custom_call" | custom-call | flops 1 | bytes 1 | tf_op jit(solution)/shard_map/own_tile/pallas_call | solution.py:25
  4.0 1.7 %collective-permute-start = (f32[256,512]{1,0:T(8,128)S(1)}, f32[256,512]{1,0:T(8,128)S(1)}, u32[]{:S(2)}, u32[]{:S(2)}) collective-permute-start(f32[256,512]{1,0:T(8,128)S(1)} %get-tuple-element.49), channel_id=1, source_target_pairs={{0,1},{1,0},{2,3},{3,2},{4,5},{5,4},{6,7},{7,6},{8,9},{9,8},{10,11... | collective-permute-start | bytes 1572872 | tf_op jit(solution)/shard_map/ppermute | solution.py:327
  5.7 14.7 %collective-permute-done.3.whole = bf16[1504,256]{1,0:T(8,128)(2,1)S(1)} collective-permute-done((bf16[1504,256]{1,0:T(8,128)(2,1)S(1)}, bf16[1504,256]{1,0:T(8,128)(2,1)S(1)}, u32[]{:S(2)}, u32[]{:S(2)}) %collective-permute-start.3) | collective-permute-done | bytes 770080 | tf_op jit(solution)/shard_map/ppermute | solution.py:316
  21.0 2.4 %collective-permute-start.4 = (bf16[1504,128]{1,0:T(8,128)(2,1)S(1)}, bf16[1504,128]{1,0:T(8,128)(2,1)S(1)}, u32[]{:S(2)}, u32[]{:S(2)}) collective-permute-start(bf16[1504,128]{1,0:T(8,128)(2,1)S(1)} %get-tuple-element.53.refs_0_), channel_id=1, source_target_pairs={{4,28},{6,30},{12,4},{14,6},{20,12},{22,14},{28,20},{30,22},{5,29}... | collective-permute-start | bytes 1155080 | tf_op jit(solution)/shard_map/ppermute | solution.py:316
  23.5 2.4 %collective-permute-start.8 = (bf16[1504,128]{1,0:T(8,128)(2,1)S(1)}, bf16[1504,128]{1,0:T(8,128)(2,1)S(1)}, u32[]{:S(2)}, u32[]{:S(2)}) collective-permute-start(bf16[1504,128]{1,0:T(8,128)(2,1)S(1)} %get-tuple-element.63.refs_0_), channel_id=1, source_target_pairs={{4,28},{6,30},{12,4},{14,6},{20,12},{22,14},{28,20},{30,22},{5,29}... | collective-permute-start | bytes 1155080 | tf_op jit(solution)/shard_map/ppermute | solution.py:316
  25.9 1.0 %panel_tile.5 = (f32[8,512]{1,0:T(8,128)S(1)}, s32[264,256]{1,0:T(8,128)S(1)}, f32[256,512]{1,0:T(8,128)S(1)}) custom-call(bf16[512,1536]{1,0:T(8,128)(2,1)S(1)} %get-tuple-element.71.lt, bf16[1536,256]{1,0:T(8,128)(2,1)S(1)} %collective-permute-done.1.refs_0_, bf16[1552,256]{1,0:T(8,128)(2,1)S(1)} %collective-permute-done.2.refs_1_), custom_call_target="tpu_custom_call" | custom-call | flops 1 | bytes 1 | tf_op jit(solution)/shard_map/panel_tile/pallas_call | solution.py:25
  26.9 1.6 %collective-permute-start.6 = (s32[264,256]{1,0:T(8,128)S(1)}, s32[264,256]{1,0:T(8,128)S(1)}, u32[]{:S(2)}, u32[]{:S(2)}) collective-permute-start(s32[264,256]{1,0:T(8,128)S(1)} %get-tuple-element.60), channel_id=1, source_target_pairs={{0,1},{1,0},{2,3},{3,2},{4,5},{5,4},{6,7},{7,6},{8,9},{9,8},{10,11... | collective-permute-start | bytes 811016 | tf_op jit(solution)/shard_map/ppermute | solution.py:327
  28.5 8.1 %collective-permute-done.4.refs_1_ = bf16[1504,128]{1,0:T(8,128)(2,1)S(1)} collective-permute-done((bf16[1504,128]{1,0:T(8,128)(2,1)S(1)}, bf16[1504,128]{1,0:T(8,128)(2,1)S(1)}, u32[]{:S(2)}, u32[]{:S(2)}) %collective-permute-start.4) | collective-permute-done | bytes 385056 | tf_op jit(solution)/shard_map/ppermute | solution.py:316
  36.6 0.6 %panel_tile.6 = (f32[8,256]{1,0:T(8,128)S(1)}, s32[264,128]{1,0:T(8,128)S(1)}, f32[256,256]{1,0:T(8,128)S(1)}, bf16[1552,256]{1,0:T(8,128)(2,1)S(1)}) custom-call(bf16[512,1536]{1,0:T(8,128)(2,1)S(1)} %get-tuple-element.71.lt, bf16[1504,128]{1,0:T(8,128)(2,1)S(1)} %get-tuple-element.53.refs_0_, bf16[1504,128]{1,0:T(8,128)(2,1)S(1)} %collective-permute-done.4.refs_1_, ...), custom_call_target="tpu_custom_call" | custom-call | flops 1 | bytes 1 | tf_op jit(solution)/shard_map/panel_tile/pallas_call | solution.py:25
  37.2 1.6 %collective-permute-start.7 = (s32[264,128]{1,0:T(8,128)S(1)}, s32[264,128]{1,0:T(8,128)S(1)}, u32[]{:S(2)}, u32[]{:S(2)}) collective-permute-start(s32[264,128]{1,0:T(8,128)S(1)} %get-tuple-element.61), channel_id=1, source_target_pairs={{0,1},{1,0},{2,3},{3,2},{4,5},{5,4},{6,7},{7,6},{8,9},{9,8},{10,11... | collective-permute-start | bytes 405512 | tf_op jit(solution)/shard_map/ppermute | solution.py:327
  38.8 2.2 %finish.3.refs_9_ = f32[256,2048]{1,0:T(8,128)} custom-call(f32[256,128]{1,0:T(8,128)S(1)} %get-tuple-element.46.row_coord, f32[256,128]{1,0:T(8,128)S(1)} %get-tuple-element.47.row_level, f32[8,512]{1,0:T(8,128)S(1)} %maximum_convert_fusion.refs_0_, f32[256,512]{1,0:T(8,128)S(1)} %get-tuple-element.58.refs_1_, f32[256,512]{1,0:T(8,128)S(1)} %collective-permute-done.refs_2_, ...), custom_call_target="tpu_custom_call" | custom-call | flops 1 | bytes 1 | tf_op jit(solution)/shard_map/finish/pallas_call | solution.py:289
  41.1 1.2 %collective-permute-done.7.refs_2_ = s32[264,128]{1,0:T(8,128)S(1)} collective-permute-done((s32[264,128]{1,0:T(8,128)S(1)}, s32[264,128]{1,0:T(8,128)S(1)}, u32[]{:S(2)}, u32[]{:S(2)}) %collective-permute-start.7) | collective-permute-done | bytes 135200 | tf_op jit(solution)/shard_map/ppermute | solution.py:327
  42.5 0.6 %panel_tile.7 = (f32[8,256]{1,0:T(8,128)S(1)}, s32[264,128]{1,0:T(8,128)S(1)}, f32[256,256]{1,0:T(8,128)S(1)}, bf16[1552,256]{1,0:T(8,128)(2,1)S(1)}) custom-call(bf16[512,1536]{1,0:T(8,128)(2,1)S(1)} %get-tuple-element.71.lt, bf16[1504,128]{1,0:T(8,128)(2,1)S(1)} %get-tuple-element.63.refs_0_, bf16[1504,128]{1,0:T(8,128)(2,1)S(1)} %collective-permute-done.8.refs_1_, ...), custom_call_target="tpu_custom_call" | custom-call | flops 1 | bytes 1 | tf_op jit(solution)/shard_map/panel_tile/pallas_call | solution.py:25
  43.2 1.6 %collective-permute-start.13 = (s32[264,128]{1,0:T(8,128)S(1)}, s32[264,128]{1,0:T(8,128)S(1)}, u32[]{:S(2)}, u32[]{:S(2)}) collective-permute-start(s32[264,128]{1,0:T(8,128)S(1)} %get-tuple-element.80), channel_id=1, source_target_pairs={{0,1},{1,0},{2,3},{3,2},{4,5},{5,4},{6,7},{7,6},{8,9},{9,8},{10,11... | collective-permute-start | bytes 405512 | tf_op jit(solution)/shard_map/ppermute | solution.py:327
  44.8 0.6 %panel_tile.8 = (f32[8,256]{1,0:T(8,128)S(1)}, s32[264,128]{1,0:T(8,128)S(1)}, f32[256,256]{1,0:T(8,128)S(1)}) custom-call(bf16[512,1536]{1,0:T(8,128)(2,1)S(1)} %get-tuple-element.71.lt, bf16[1552,256]{1,0:T(8,128)(2,1)S(1)} %collective-permute-done.10.refs_0_), custom_call_target="tpu_custom_call" | custom-call | flops 1 | bytes 1 | tf_op jit(solution)/shard_map/panel_tile/pallas_call | solution.py:25
  46.5 1.6 %collective-permute-start.12 = (s32[264,128]{1,0:T(8,128)S(1)}, s32[264,128]{1,0:T(8,128)S(1)}, u32[]{:S(2)}, u32[]{:S(2)}) collective-permute-start(s32[264,128]{1,0:T(8,128)S(1)} %get-tuple-element.76), channel_id=1, source_target_pairs={{0,1},{1,0},{2,3},{3,2},{4,5},{5,4},{6,7},{7,6},{8,9},{9,8},{10,11... | collective-permute-start | bytes 405512 | tf_op jit(solution)/shard_map/ppermute | solution.py:327
  48.4 1.2 %collective-permute-done.13.refs_5_ = s32[264,128]{1,0:T(8,128)S(1)} collective-permute-done((s32[264,128]{1,0:T(8,128)S(1)}, s32[264,128]{1,0:T(8,128)S(1)}, u32[]{:S(2)}, u32[]{:S(2)}) %collective-permute-start.13) | collective-permute-done | bytes 135200 | tf_op jit(solution)/shard_map/ppermute | solution.py:327
  49.7 2.9 %collective-permute-done.14.refs_8_ = s32[264,128]{1,0:T(8,128)S(1)} collective-permute-done((s32[264,128]{1,0:T(8,128)S(1)}, s32[264,128]{1,0:T(8,128)S(1)}, u32[]{:S(2)}, u32[]{:S(2)}) %collective-permute-start.14) | collective-permute-done | bytes 135200 | tf_op jit(solution)/shard_map/ppermute | solution.py:327
  52.6 1.9 %finish.4.refs_3_ = f32[256,2048]{1,0:T(8,128)} custom-call(f32[256,128]{1,0:T(8,128)S(1)} %get-tuple-element.46.row_coord, f32[256,128]{1,0:T(8,128)S(1)} %get-tuple-element.47.row_level, f32[8,256]{1,0:T(8,128)S(1)} %get-tuple-element.77.refs_0_, f32[256,256]{1,0:T(8,128)S(1)} %get-tuple-element.78.refs_1_, ...), custom_call_target="tpu_custom_call", output_to_operand_aliasing={{}: (11, {})} | custom-call | flops 1 | bytes 1 | tf_op jit(solution)/shard_map/finish/pallas_call | solution.py:289
  54.4 0.6 %collective-permute-done.12.refs_2_ = s32[264,128]{1,0:T(8,128)S(1)} collective-permute-done((s32[264,128]{1,0:T(8,128)S(1)}, s32[264,128]{1,0:T(8,128)S(1)}, u32[]{:S(2)}, u32[]{:S(2)}) %collective-permute-start.12) | collective-permute-done | bytes 135200 | tf_op jit(solution)/shard_map/ppermute | solution.py:327
  55.0 0.8 %finish.5 = f32[256,2048]{1,0:T(8,128)} custom-call(f32[256,128]{1,0:T(8,128)S(1)} %get-tuple-element.46.row_coord, f32[256,128]{1,0:T(8,128)S(1)} %get-tuple-element.47.row_level, f32[256,256]{1,0:T(8,128)S(1)} %weigh.1.refs_0_, f32[256,256]{1,0:T(8,128)S(1)} %get-tuple-element.75.refs_1_, ...), custom_call_target="tpu_custom_call", output_to_operand_aliasing={{}: (5, {})} | custom-call | flops 1 | bytes 1 | tf_op jit(solution)/shard_map/finish/pallas_call | solution.py:289
  (28 shorter events, 2.8 us)
Async XLA Ops:
  0.0 2.0 %copy-start = (bf16[1536,512]{1,0:T(8,128)(2,1)S(1)}, bf16[1536,512]{1,0:T(8,128)(2,1)}, u32[]{:S(2)}) copy-start(bf16[1536,512]{1,0:T(8,128)(2,1)} %x) | copy-start | bytes 4718596
  0.0 2.0 %copy-start.1 = (s32[512]{0:T(512)S(1)}, s32[512]{0:T(512)}, u32[]{:S(2)}) copy-start(s32[512]{0:T(512)} %param.4) | copy-start | bytes 6148
  0.0 2.8 %copy-start.2 = (s32[512]{0:T(512)S(1)}, s32[512]{0:T(512)}, u32[]{:S(2)}) copy-start(s32[512]{0:T(512)} %param.5) | copy-start | bytes 6148
  1.4 19.0 %collective-permute-start.3 = (bf16[1504,256]{1,0:T(8,128)(2,1)S(1)}, bf16[1504,256]{1,0:T(8,128)(2,1)S(1)}, u32[]{:S(2)}, u32[]{:S(2)}) collective-permute-start(bf16[1504,256]{1,0:T(8,128)(2,1)S(1)} %head.1), channel_id=1, source_target_pairs={{0,4},{2,6},{4,0},{6,2},{8,12},{10,14},{12,8},{14,10},{16,20},{18,... | collective-permute-start | bytes 2310152 | tf_op jit(solution)/shard_map/ppermute | solution.py:316
  2.0 21.5 %collective-permute-start.1 = (bf16[1536,256]{1,0:T(8,128)(2,1)S(1)}, bf16[1536,256]{1,0:T(8,128)(2,1)S(1)}, u32[]{:S(2)}, u32[]{:S(2)}) collective-permute-start(bf16[1536,256]{1,0:T(8,128)(2,1)S(1)} %slice.9.low.whole), channel_id=1, source_target_pairs={{0,26},{2,0},{4,30},{6,4},{8,2},{10,8},{12,6},{14,12},{16,10},{18,... | collective-permute-start | bytes 2359304 | tf_op jit(solution)/shard_map/ppermute | solution.py:316
  2.2 23.7 %collective-permute-start.2 = (bf16[1552,256]{1,0:T(8,128)(2,1)S(1)}, bf16[1552,256]{1,0:T(8,128)(2,1)S(1)}, u32[]{:S(2)}, u32[]{:S(2)}) collective-permute-start(bf16[1552,256]{1,0:T(8,128)(2,1)S(1)} %get-tuple-element.45.high), channel_id=1, source_target_pairs={{0,26},{2,0},{4,30},{6,4},{8,2},{10,8},{12,6},{14,12},{16,10},{18,... | collective-permute-start | bytes 2383880 | tf_op jit(solution)/shard_map/ppermute | solution.py:316
  4.0 19.4 %collective-permute-start = (f32[256,512]{1,0:T(8,128)S(1)}, f32[256,512]{1,0:T(8,128)S(1)}, u32[]{:S(2)}, u32[]{:S(2)}) collective-permute-start(f32[256,512]{1,0:T(8,128)S(1)} %get-tuple-element.49), channel_id=1, source_target_pairs={{0,1},{1,0},{2,3},{3,2},{4,5},{5,4},{6,7},{7,6},{8,9},{9,8},{10,11... | collective-permute-start | bytes 1572872 | tf_op jit(solution)/shard_map/ppermute | solution.py:327
  20.4 16.2 %collective-permute-start.5 = (bf16[1584,128]{1,0:T(8,128)(2,1)S(1)}, bf16[1584,128]{1,0:T(8,128)(2,1)S(1)}, u32[]{:S(2)}, u32[]{:S(2)}) collective-permute-start(bf16[1584,128]{1,0:T(8,128)(2,1)S(1)} %get-tuple-element.55), channel_id=1, source_target_pairs={{0,28},{2,30},{4,0},{6,2},{8,4},{10,6},{12,8},{14,10},{16,12},{18,... | collective-permute-start | bytes 1216520 | tf_op jit(solution)/shard_map/ppermute | solution.py:316
  21.0 15.6 %collective-permute-start.4 = (bf16[1504,128]{1,0:T(8,128)(2,1)S(1)}, bf16[1504,128]{1,0:T(8,128)(2,1)S(1)}, u32[]{:S(2)}, u32[]{:S(2)}) collective-permute-start(bf16[1504,128]{1,0:T(8,128)(2,1)S(1)} %get-tuple-element.53.refs_0_), channel_id=1, source_target_pairs={{4,28},{6,30},{12,4},{14,6},{20,12},{22,14},{28,20},{30,22},{5,29}... | collective-permute-start | bytes 1155080 | tf_op jit(solution)/shard_map/ppermute | solution.py:316
  23.4 19.1 %collective-permute-start.9 = (bf16[1584,128]{1,0:T(8,128)(2,1)S(1)}, bf16[1584,128]{1,0:T(8,128)(2,1)S(1)}, u32[]{:S(2)}, u32[]{:S(2)}) collective-permute-start(bf16[1584,128]{1,0:T(8,128)(2,1)S(1)} %get-tuple-element.65), channel_id=1, source_target_pairs={{0,28},{2,30},{4,0},{6,2},{8,4},{10,6},{12,8},{14,10},{16,12},{18,... | collective-permute-start | bytes 1216520 | tf_op jit(solution)/shard_map/ppermute | solution.py:316
  23.5 19.0 %collective-permute-start.8 = (bf16[1504,128]{1,0:T(8,128)(2,1)S(1)}, bf16[1504,128]{1,0:T(8,128)(2,1)S(1)}, u32[]{:S(2)}, u32[]{:S(2)}) collective-permute-start(bf16[1504,128]{1,0:T(8,128)(2,1)S(1)} %get-tuple-element.63.refs_0_), channel_id=1, source_target_pairs={{4,28},{6,30},{12,4},{14,6},{20,12},{22,14},{28,20},{30,22},{5,29}... | collective-permute-start | bytes 1155080 | tf_op jit(solution)/shard_map/ppermute | solution.py:316
  26.9 11.9 %collective-permute-start.6 = (s32[264,256]{1,0:T(8,128)S(1)}, s32[264,256]{1,0:T(8,128)S(1)}, u32[]{:S(2)}, u32[]{:S(2)}) collective-permute-start(s32[264,256]{1,0:T(8,128)S(1)} %get-tuple-element.60), channel_id=1, source_target_pairs={{0,1},{1,0},{2,3},{3,2},{4,5},{5,4},{6,7},{7,6},{8,9},{9,8},{10,11... | collective-permute-start | bytes 811016 | tf_op jit(solution)/shard_map/ppermute | solution.py:327
  37.2 5.1 %collective-permute-start.7 = (s32[264,128]{1,0:T(8,128)S(1)}, s32[264,128]{1,0:T(8,128)S(1)}, u32[]{:S(2)}, u32[]{:S(2)}) collective-permute-start(s32[264,128]{1,0:T(8,128)S(1)} %get-tuple-element.61), channel_id=1, source_target_pairs={{0,1},{1,0},{2,3},{3,2},{4,5},{5,4},{6,7},{7,6},{8,9},{9,8},{10,11... | collective-permute-start | bytes 405512 | tf_op jit(solution)/shard_map/ppermute | solution.py:327
  41.0 3.8 %collective-permute-start.10 = (bf16[1552,256]{1,0:T(8,128)(2,1)S(1)}, bf16[1552,256]{1,0:T(8,128)(2,1)S(1)}, u32[]{:S(2)}, u32[]{:S(2)}) collective-permute-start(bf16[1552,256]{1,0:T(8,128)(2,1)S(1)} %get-tuple-element.69), channel_id=1, source_target_pairs={{0,2},{2,0},{4,6},{6,4},{8,10},{10,8},{12,14},{14,12},{16,18},{18,... | collective-permute-start | bytes 2383880 | tf_op jit(solution)/shard_map/ppermute | solution.py:316
  43.1 2.8 %collective-permute-start.11 = (bf16[1552,256]{1,0:T(8,128)(2,1)S(1)}, bf16[1552,256]{1,0:T(8,128)(2,1)S(1)}, u32[]{:S(2)}, u32[]{:S(2)}) collective-permute-start(bf16[1552,256]{1,0:T(8,128)(2,1)S(1)} %get-tuple-element.72), channel_id=1, source_target_pairs={{0,2},{2,0},{4,6},{6,4},{8,10},{10,8},{12,14},{14,12},{16,18},{18,... | collective-permute-start | bytes 2383880 | tf_op jit(solution)/shard_map/ppermute | solution.py:316
  43.2 6.5 %collective-permute-start.13 = (s32[264,128]{1,0:T(8,128)S(1)}, s32[264,128]{1,0:T(8,128)S(1)}, u32[]{:S(2)}, u32[]{:S(2)}) collective-permute-start(s32[264,128]{1,0:T(8,128)S(1)} %get-tuple-element.80), channel_id=1, source_target_pairs={{0,1},{1,0},{2,3},{3,2},{4,5},{5,4},{6,7},{7,6},{8,9},{9,8},{10,11... | collective-permute-start | bytes 405512 | tf_op jit(solution)/shard_map/ppermute | solution.py:327
  45.4 7.2 %collective-permute-start.14 = (s32[264,128]{1,0:T(8,128)S(1)}, s32[264,128]{1,0:T(8,128)S(1)}, u32[]{:S(2)}, u32[]{:S(2)}) collective-permute-start(s32[264,128]{1,0:T(8,128)S(1)} %get-tuple-element.82), channel_id=1, source_target_pairs={{0,1},{1,0},{2,3},{3,2},{4,5},{5,4},{6,7},{7,6},{8,9},{9,8},{10,11... | collective-permute-start | bytes 405512 | tf_op jit(solution)/shard_map/ppermute | solution.py:327
  46.5 8.5 %collective-permute-start.12 = (s32[264,128]{1,0:T(8,128)S(1)}, s32[264,128]{1,0:T(8,128)S(1)}, u32[]{:S(2)}, u32[]{:S(2)}) collective-permute-start(s32[264,128]{1,0:T(8,128)S(1)} %get-tuple-element.76), channel_id=1, source_target_pairs={{0,1},{1,0},{2,3},{3,2},{4,5},{5,4},{6,7},{7,6},{8,9},{9,8},{10,11... | collective-permute-start | bytes 405512 | tf_op jit(solution)/shard_map/ppermute | solution.py:327
